TPU v7x, 256 devices: a whole 4x4x8 slice. The times are simulated.
256 devices in a mesh: level: 4 (over y), gx: 8 (over z_hi, core), gy: 8 (over x, z_lo).
Axes of the slice: x: 4, y: 4, z: 8 (z_hi: 4, z_lo: 2; z = z_hi * 2 + z_lo), core: 2. Of those that a mesh axis runs over, the one named last changes fastest.
Arguments:
- state_init: float32 [2, 128, 128, 128], P(None, 'gx', 'gy'), may hold values from 0 to 1
- feed_rate: float32 [128, 128, 128], P('gx', 'gy'), may hold values from 0.04 to 0.4
- kill_rate: float32 [128, 128, 128], P('gx', 'gy'), may hold values from 0.04 to 0.4
Outputs:
- level_states: float32 [4, 2, 128, 128, 128], P('level', None, 'gx', 'gy')
All inputs are finite; a program needn't handle non-finite values.
Results may differ from a plain program's by a relative error of at most 0.00002.
Values sent between devices are 32-bit elements; how exact they have to be, the bound alone decides.
No kernel may reach another device: no remote copies, remote signals or barrier semaphores. Data moves between devices by JAX's collectives and lax.ppermute only.
A program may use at most 128 MiB of HBM per device.

v0:
```python
import functools

import jax
import jax.numpy as jnp
import numpy as np
from jax import lax
from jax.experimental import pallas as pl
from jax.experimental.pallas import tpu as pltpu
from jax.sharding import PartitionSpec as P


BRICK = 8
EXT = 3 * BRICK
LANES = 128
AXES = ("level", "gx", "gy")
COEF = (0.5, 0.25)
INV = tuple(1.0 / (1.0 + 6.0 * c) for c in COEF)
MIX = tuple(c / (1.0 + 6.0 * c) for c in COEF)
STEPS = 4
VMEM = pl.BlockSpec(memory_space=pltpu.VMEM)
SMEM = pl.BlockSpec(memory_space=pltpu.SMEM)


def quad_table(step_count):
    table_rows = []
    for n in range(step_count):
        first_node = min(max(n - 1, 0), step_count - 3)
        weights_row = []
        for j in range(4):
            coeffs = [1.0]
            for i in range(4):
                if i != j:
                    shifted = [0.0] + coeffs
                    scaled_terms = [-float(first_node + i) * c for c in coeffs] + [0.0]
                    coeffs = [
                        (shifted[k] + scaled_terms[k]) / float(j - i) for k in range(len(shifted))
                    ]
            integral = 0.0
            for k in range(len(coeffs)):
                integral = integral + coeffs[k] * ((n + 1.0) ** (k + 1) - float(n) ** (k + 1)) / (
                    k + 1.0
                )
            weights_row.append(float(np.float32(integral)))
        table_rows.append(weights_row)
    return table_rows


TABLE = quad_table(STEPS)


def linear(level, gx, gy):
    return (level * 8 + gx) * 8 + gy


def walk(x, level):
    return level if x % 2 == 0 else 3 - level


def device_at(bx, by):
    z, core = bx // 2, bx % 2
    x, place = by // 4, by % 4
    return linear(walk(x, place), (z // 2) * 2 + core, x * 2 + z % 2)


def pairs_along(dim, odd):
    pairs = []
    for bx in range(16):
        for by in range(16):
            at = [bx, by]
            at[dim] = (at[dim] ^ 1) if not odd else (((at[dim] + 1) ^ 1) - 1) % 16
            pairs.append((device_at(bx, by), device_at(*at)))
    return pairs


def spread_pairs():
    pairs = []
    for level in range(4):
        for gx in range(8):
            for gy in range(8):
                x, zl, zh, core = gy // 2, gy % 2, gx // 2, gx % 2
                place = walk(x, level)
                same = place // 2 == zl
                by = 4 * x + (place if same else 3 - place)
                bx = 2 * (2 * zh + core) + (0 if same else 1)
                pairs.append((linear(level, gx, gy), device_at(bx, by)))
    return pairs


def gather_pairs(turn):
    pairs = []
    for bx in range(16):
        for by in range(16):
            piece = 2 * (bx % 2) + by % 2
            pairs.append((device_at(bx, by), linear((piece + turn) % 4, bx // 2, by // 2)))
    return pairs


def swap(array, dim):
    return (
        lax.ppermute(array, AXES, pairs_along(dim, False)),
        lax.ppermute(array, AXES, pairs_along(dim, True)),
    )


def call(kernel, name, out_shapes, args, scratch=()):
    return pl.pallas_call(
        kernel,
        name=name,
        out_shape=[jax.ShapeDtypeStruct(s, jnp.float32) for s in out_shapes],
        in_specs=[SMEM if a.dtype == jnp.int32 else VMEM for a in args],
        out_specs=[VMEM] * len(out_shapes),
        scratch_shapes=[pltpu.VMEM(s, jnp.float32) for s in scratch],
        compiler_params=pltpu.CompilerParams(vmem_limit_bytes=40 << 20),
    )(*args)


def around(prev, cur, nxt):
    second = pltpu.roll(cur, 1, 0) + pltpu.roll(cur, EXT - 1, 0)
    third = pltpu.roll(cur, 1, 1) + pltpu.roll(cur, LANES - 1, 1)
    return (prev + nxt) + (second + third)


def planes(halo):
    return range(BRICK - halo, 2 * BRICK + halo)


def assemble(dst, own, near, far, first):
    for i in range(BRICK):
        for s in range(2):
            dst[s, BRICK + i] = own[first + s, i]
            dst[s, 2 * BRICK + i] = near[first + s, BRICK - 1 - i]
            dst[s, i] = far[first + s, BRICK - 1 - i]


def reacted(u, v, feed, both):
    uptake = u * v * v
    return 0.5 * (feed * (1.0 - u) - uptake), 0.5 * (uptake - both * v)


def advance(dst, field, rates, right, halo, source=None):
    for x in planes(halo - 1):
        u, v = field[0, x], field[1, x]
        du, dv = reacted(u, v, rates[0, x], rates[1, x])
        u, v = u + du, v + dv
        if source is not None:
            u, v = u + source[0, x], v + source[1, x]
        right[0, x] = INV[0] * u
        right[1, x] = INV[1] * v
    src = field
    for k in range(1, 5):
        span = planes(halo - k)
        prev = [src[s, span[0] - 1] for s in range(2)]
        cur = [src[s, span[0]] for s in range(2)]
        for x in span:
            for s in range(2):
                nxt = src[s, x + 1]
                dst[s, x] = right[s, x] + MIX[s] * around(prev[s], cur[s], nxt)
                prev[s], cur[s] = cur[s], nxt
        src = dst


def sources(outs, nodes, first, rates, mixed):
    for n, (out, step, halo) in enumerate(outs):
        linear_w = [TABLE[step][j] - (1.0 if first + j == step + 1 else 0.0) for j in range(4)]
        react_w = [TABLE[step][j] - (1.0 if first + j == step else 0.0) for j in range(4)]
        total = sum(react_w)
        for x in planes(halo + 1):
            us = [node[0, x] for node in nodes]
            vs = [node[1, x] for node in nodes]
            mix_u = sum(w * u for w, u in zip(linear_w, us))
            mix_v = sum(w * v for w, v in zip(linear_w, vs))
            mixed[0, x], mixed[1, x] = mix_u, mix_v
            if x in planes(halo):
                after, now = step + 1 - first, step - first
                sum_u = mix_u + (us[after] - us[now])
                sum_v = mix_v + (vs[after] - vs[now])
                uptake = sum(w * (u * v * v) for w, u, v in zip(react_w, us, vs))
                out[0, x] = 0.5 * (rates[0, x] * (total - sum_u) - uptake)
                out[1, x] = 0.5 * (uptake - rates[1, x] * sum_v)
        span = planes(halo)
        for s in range(2):
            prev, cur = mixed[s, span[0] - 1], mixed[s, span[0]]
            for x in span:
                nxt = mixed[s, x + 1]
                out[s, x] = out[s, x] + COEF[s] * (around(prev, cur, nxt) - 6.0 * cur)
                prev, cur = cur, nxt


def give(dst, first, field):
    for s in range(2):
        for i in range(BRICK):
            dst[first + s, i] = field[s, BRICK + i, BRICK : 2 * BRICK]


def pick_kernel(where, state, feed, kill, out):
    p, q = where[0], where[1]
    rows = pl.ds(pl.multiple_of(q * BRICK, BRICK), BRICK)
    for i in range(BRICK):
        x = jnp.where(p == 0, i, 2 * BRICK - 1 - i)
        out[0, i] = state[0, x, rows]
        out[1, i] = state[1, x, rows]
        out[2, i] = feed[x, rows]
        out[3, i] = kill[x, rows]


def widen_kernel(where, own, near, far, out):
    even = where[2] == 0
    for f in range(own.shape[0]):
        for i in range(BRICK):
            a, b = near[f, i], far[f, i]
            out[f, i, :BRICK] = jnp.where(even, b, a)
            out[f, i, BRICK : 2 * BRICK] = own[f, i]
            out[f, i, 2 * BRICK :] = jnp.where(even, a, b)


def round_0(own, near, far, out, start, rates, y1, y2, right):
    assemble(start, own, near, far, 0)
    assemble(rates, own, near, far, 2)
    for x in range(EXT):
        rates[1, x] = rates[0, x] + rates[1, x]
    advance(y1, start, rates, right, 8)
    advance(y2, y1, rates, right, 4)
    give(out, 0, y2)


def round_1(own, near, far, start, rates, y1, out, y2, y3, y4, z1, s, t, right, mixed):
    assemble(y2, own, near, far, 0)
    advance(y3, y2, rates, right, 8)
    sources([(s, 0, 3), (t, 1, 0)], (start, y1, y2, y3), 0, rates, mixed)
    advance(z1, start, rates, right, 4, s)
    advance(y4, y3, rates, right, 4)
    give(out, 0, z1)
    give(out, 2, t)
    give(out, 4, y4)


def round_2(own, near, far, rates, y1, y2, y3, out, z1, y4, s1, s2, s3, z2, z3, right, mixed):
    assemble(z1, own, near, far, 0)
    assemble(s1, own, near, far, 2)
    assemble(y4, own, near, far, 4)
    advance(z2, z1, rates, right, 8, s1)
    sources([(s2, 2, 3), (s3, 3, 0)], (y1, y2, y3, y4), 1, rates, mixed)
    advance(z3, z2, rates, right, 4, s2)
    give(out, 0, z3)
    give(out, 2, z2)
    give(out, 4, s3)


def round_3(own, near, far, start, rates, y1, out, final, z1, s3, y2, y3, y4, s, z2, right, mixed):
    assemble(y3, own, near, far, 0)
    assemble(y2, own, near, far, 2)
    assemble(s, own, near, far, 4)
    advance(y4, y3, rates, right, 8, s)
    give(final, 0, y4)
    sources([(s, 0, 7), (s3, 1, 3)], (start, y1, y2, y3), 0, rates, mixed)
    advance(z1, start, rates, right, 8, s)
    advance(z2, z1, rates, right, 4, s3)
    sources([(s, 2, 0), (s3, 3, 3)], (y1, y2, y3, y4), 1, rates, mixed)
    give(out, 0, z2)
    give(out, 2, s)


def round_4(own, near, far, start, rates, y1, s3, out, y2, y3, s2, y4, z1, t, right, mixed):
    assemble(y2, own, near, far, 0)
    assemble(s2, own, near, far, 2)
    advance(y3, y2, rates, right, 8, s2)
    sources([(s2, 0, 3), (t, 1, 0)], (start, y1, y2, y3), 0, rates, mixed)
    advance(z1, start, rates, right, 4, s2)
    advance(y4, y3, rates, right, 4, s3)
    give(out, 0, z1)
    give(out, 2, t)
    give(out, 4, y4)


def round_5(own, near, far, rates, y1, y2, y3, out, s3, z1, y4, s1, s2, z2, z3, right, mixed):
    assemble(z1, own, near, far, 0)
    assemble(s1, own, near, far, 2)
    assemble(y4, own, near, far, 4)
    advance(z2, z1, rates, right, 8, s1)
    sources([(s2, 2, 3), (s3, 3, 3)], (y1, y2, y3, y4), 1, rates, mixed)
    advance(z3, z2, rates, right, 4, s2)
    give(out, 0, z3)


def round_6(where, own, near, far, rates, s3, f0, f1, f2, out0, out1, out2, out3, y3, y4, right, last):
    assemble(y3, own, near, far, 0)
    advance(y4, y3, rates, right, 4, s3)
    for i in range(BRICK):
        for s in range(2):
            last[0, s, i] = f0[s, i]
            last[1, s, i] = f1[s, i]
            last[2, s, i] = f2[s, i]
            last[3, s, i] = y4[s, BRICK + i, BRICK : 2 * BRICK]
    turned = where[4]
    for turn, out in enumerate((out0, out1, out2, out3)):
        level = lax.rem(where[3] + turn, 4)
        for i in range(BRICK):
            x = jnp.where(turned == 0, i, BRICK - 1 - i)
            for s in range(2):
                out[s, i] = last[level, s, x]


def place_kernel(where, in0, in1, in2, in3, out):
    for turn, piece in enumerate((in0, in1, in2, in3)):
        at = lax.rem(where[5] + (4 - turn), 4)
        p, q = at // 2, lax.rem(at, 2)
        rows = pl.ds(pl.multiple_of(q * BRICK, BRICK), BRICK)
        for i in range(BRICK):
            for s in range(2):
                out[0, s, p * BRICK + i, rows] = piece[s, i]


def per_device(state, feed, kill):
    level, gx, gy = (lax.axis_index(a) for a in AXES)
    x, low, high, core = gy // 2, gy % 2, gx // 2, gx % 2
    place = jnp.where(x % 2 == 0, level, 3 - level)
    same = place // 2 == low
    where = jnp.stack(
        [
            jnp.where(same, 0, 1),
            jnp.where(same, place, 3 - place) % 2,
            place % 2,
            2 * core + place % 2,
            core,
            level,
        ]
    ).astype(jnp.int32)

    field = (2, EXT, EXT, LANES)

    def send(n):
        return (n, BRICK, BRICK, LANES)

    def exchange(own, name):
        wide = call(
            widen_kernel,
            "widen_" + name,
            [(own.shape[0], BRICK, EXT, LANES)],
            (where, own, *swap(own, 1)),
        )[0]
        return (wide, *swap(wide, 0))

    own = call(pick_kernel, "pick", [send(4)], (where, state, feed, kill))[0]
    own = lax.ppermute(own, AXES, spread_pairs())
    own, start, rates, y1 = call(
        round_0, "round_0", [send(2)] + [field] * 3, exchange(own, "0"), [field] * 2
    )
    own, y2, y3 = call(
        round_1,
        "round_1",
        [send(6), field, field],
        (*exchange(own, "1"), start, rates, y1),
        [field] * 6,
    )
    final_0 = own[4:6]
    own, z1 = call(
        round_2,
        "round_2",
        [send(6), field],
        (*exchange(own, "2"), rates, y1, y2, y3),
        [field] * 8,
    )
    own, final_1, y1, s3 = call(
        round_3,
        "round_3",
        [send(4), send(2), field, field],
        (*exchange(own, "3"), start, rates, z1),
        [field] * 7,
    )
    own, y2, y3 = call(
        round_4,
        "round_4",
        [send(6), field, field],
        (*exchange(own, "4"), start, rates, y1, s3),
        [field] * 6,
    )
    final_2 = own[4:6]
    own, s3 = call(
        round_5,
        "round_5",
        [send(2), field],
        (*exchange(own, "5"), rates, y1, y2, y3),
        [field] * 8,
    )
    outs = call(
        round_6,
        "round_6",
        [send(2)] * 4,
        (where, *exchange(own, "6"), rates, s3, final_0, final_1, final_2),
        [field] * 3 + [(4, 2, BRICK, BRICK, LANES)],
    )
    outs = [lax.ppermute(o, AXES, gather_pairs(turn)) for turn, o in enumerate(outs)]
    return call(place_kernel, "place", [(1, 2, 2 * BRICK, 2 * BRICK, LANES)], (where, *outs))[0]


def solution(mesh):
    return jax.shard_map(
        per_device,
        mesh=mesh,
        in_specs=(P(None, "gx", "gy", None), P("gx", "gy", None), P("gx", "gy", None)),
        out_specs=P("level", None, "gx", "gy", None),
        check_vma=False,
    )
```

profile of v0, /device:TPU:32, one launch (start us, length us, event | category | flops | bytes accessed | tf_op | source)
XLA Modules:
  0.0 157.2 jit_solution(12269260378119914578)
XLA Ops:
  3.3 3.9 %collective-permute-start = (f32[4,8,8,128]{3,2,1,0:T(8,128)S(1)}, f32[4,8,8,128]{3,2,1,0:T(8,128)S(1)}, u32[]{:S(2)}, u32[]{:S(2)}) collective-permute-start(f32[4,8,8,128]{3,2,1,0:T(8,128)S(1)} %pick.1), channel_id=1, source_target_pairs={{0,0},{1,200},{2,202},{3,2},{4,4},{5,204},{6,206},{7,6},{8,1},{9,2... | collective-permute-start | bytes 393224 | tf_op jit(solution)/shard_map/ppermute | solution.py:344
  7.2 2.5 %collective-permute-done.own = f32[4,8,8,128]{3,2,1,0:T(8,128)S(1)} collective-permute-done((f32[4,8,8,128]{3,2,1,0:T(8,128)S(1)}, f32[4,8,8,128]{3,2,1,0:T(8,128)S(1)}, u32[]{:S(2)}, u32[]{:S(2)}) %collective-permute-start) | collective-permute-done | bytes 131104 | tf_op jit(solution)/shard_map/ppermute | solution.py:344
  11.2 5.9 %collective-permute-done.2.far = f32[4,8,8,128]{3,2,1,0:T(8,128)S(1)} collective-permute-done((f32[4,8,8,128]{3,2,1,0:T(8,128)S(1)}, f32[4,8,8,128]{3,2,1,0:T(8,128)S(1)}, u32[]{:S(2)}, u32[]{:S(2)}) %collective-permute-start.2) | collective-permute-done | bytes 131104 | tf_op jit(solution)/shard_map/ppermute | solution.py:101
  21.1 3.9 %collective-permute-done.4.far = f32[4,8,24,128]{3,2,1,0:T(8,128)S(1)} collective-permute-done((f32[4,8,24,128]{3,2,1,0:T(8,128)S(1)}, f32[4,8,24,128]{3,2,1,0:T(8,128)S(1)}, u32[]{:S(2)}, u32[]{:S(2)}) %collective-permute-start.4) | collective-permute-done | bytes 393248 | tf_op jit(solution)/shard_map/ppermute | solution.py:101
  29.1 3.2 %collective-permute-done.6.far = f32[2,8,8,128]{3,2,1,0:T(8,128)S(1)} collective-permute-done((f32[2,8,8,128]{3,2,1,0:T(8,128)S(1)}, f32[2,8,8,128]{3,2,1,0:T(8,128)S(1)}, u32[]{:S(2)}, u32[]{:S(2)}) %collective-permute-start.6) | collective-permute-done | bytes 65568 | tf_op jit(solution)/shard_map/ppermute | solution.py:101
  33.8 2.8 %collective-permute-start.7 = (f32[2,8,24,128]{3,2,1,0:T(8,128)S(1)}, f32[2,8,24,128]{3,2,1,0:T(8,128)S(1)}, u32[]{:S(2)}, u32[]{:S(2)}) collective-permute-start(f32[2,8,24,128]{3,2,1,0:T(8,128)S(1)} %widen_1.1.own), channel_id=1, source_target_pairs={{0,8},{64,72},{128,136},{192,200},{194,202},{130,138},{66,74},{2,1... | collective-permute-start | bytes 589832 | tf_op jit(solution)/shard_map/ppermute | solution.py:100
  38.9 2.5 %round_1.1 = (f32[6,8,8,128]{3,2,1,0:T(8,128)S(1)}, f32[2,24,24,128]{3,2,1,0:T(8,128)S(1)}, f32[2,24,24,128]{3,2,1,0:T(8,128)S(1)}) custom-call(f32[2,8,24,128]{3,2,1,0:T(8,128)S(1)} %widen_1.1.own, f32[2,8,24,128]{3,2,1,0:T(8,128)S(1)} %collective-permute-done.7.near, f32[2,8,24,128]{3,2,1,0:T(8,128)S(1)} %collective-permute-done.8.far, ...), custom_call_target="tpu_custom_call" | custom-call | tf_op jit(solution)/shard_map/round_1/pallas_call | solution.py:106
  42.8 7.5 %collective-permute-done.10.far = f32[6,8,8,128]{3,2,1,0:T(8,128)S(1)} collective-permute-done((f32[6,8,8,128]{3,2,1,0:T(8,128)S(1)}, f32[6,8,8,128]{3,2,1,0:T(8,128)S(1)}, u32[]{:S(2)}, u32[]{:S(2)}) %collective-permute-start.10) | collective-permute-done | bytes 196640 | tf_op jit(solution)/shard_map/ppermute | solution.py:101
  53.1 7.3 %collective-permute-done.12.far = f32[6,8,24,128]{3,2,1,0:T(8,128)S(1)} collective-permute-done((f32[6,8,24,128]{3,2,1,0:T(8,128)S(1)}, f32[6,8,24,128]{3,2,1,0:T(8,128)S(1)}, u32[]{:S(2)}, u32[]{:S(2)}) %collective-permute-start.12) | collective-permute-done | bytes 589856 | tf_op jit(solution)/shard_map/ppermute | solution.py:101
  64.2 6.5 %collective-permute-done.14.far = f32[6,8,8,128]{3,2,1,0:T(8,128)S(1)} collective-permute-done((f32[6,8,8,128]{3,2,1,0:T(8,128)S(1)}, f32[6,8,8,128]{3,2,1,0:T(8,128)S(1)}, u32[]{:S(2)}, u32[]{:S(2)}) %collective-permute-start.14) | collective-permute-done | bytes 196640 | tf_op jit(solution)/shard_map/ppermute | solution.py:101
  71.6 2.9 %collective-permute-start.15 = (f32[6,8,24,128]{3,2,1,0:T(8,128)S(1)}, f32[6,8,24,128]{3,2,1,0:T(8,128)S(1)}, u32[]{:S(2)}, u32[]{:S(2)}) collective-permute-start(f32[6,8,24,128]{3,2,1,0:T(8,128)S(1)} %widen_3.1.own), channel_id=1, source_target_pairs={{0,8},{64,72},{128,136},{192,200},{194,202},{130,138},{66,74},{2,1... | collective-permute-start | bytes 1769480 | tf_op jit(solution)/shard_map/ppermute | solution.py:100
  74.4 6.4 %collective-permute-done.16.far = f32[6,8,24,128]{3,2,1,0:T(8,128)S(1)} collective-permute-done((f32[6,8,24,128]{3,2,1,0:T(8,128)S(1)}, f32[6,8,24,128]{3,2,1,0:T(8,128)S(1)}, u32[]{:S(2)}, u32[]{:S(2)}) %collective-permute-start.16) | collective-permute-done | bytes 589856 | tf_op jit(solution)/shard_map/ppermute | solution.py:101
  80.9 3.9 %round_3.1 = (f32[4,8,8,128]{3,2,1,0:T(8,128)S(1)}, f32[2,8,8,128]{3,2,1,0:T(8,128)S(1)}, f32[2,24,24,128]{3,2,1,0:T(8,128)S(1)}, f32[2,24,24,128]{3,2,1,0:T(8,128)S(1)}) custom-call(f32[6,8,24,128]{3,2,1,0:T(8,128)S(1)} %widen_3.1.own, f32[6,8,24,128]{3,2,1,0:T(8,128)S(1)} %collective-permute-done.15.near, ...), custom_call_target="tpu_custom_call" | custom-call | tf_op jit(solution)/shard_map/round_3/pallas_call | solution.py:106
  86.4 5.8 %collective-permute-done.18.far = f32[4,8,8,128]{3,2,1,0:T(8,128)S(1)} collective-permute-done((f32[4,8,8,128]{3,2,1,0:T(8,128)S(1)}, f32[4,8,8,128]{3,2,1,0:T(8,128)S(1)}, u32[]{:S(2)}, u32[]{:S(2)}) %collective-permute-start.18) | collective-permute-done | bytes 131104 | tf_op jit(solution)/shard_map/ppermute | solution.py:101
  93.2 2.4 %collective-permute-start.19 = (f32[4,8,24,128]{3,2,1,0:T(8,128)S(1)}, f32[4,8,24,128]{3,2,1,0:T(8,128)S(1)}, u32[]{:S(2)}, u32[]{:S(2)}) collective-permute-start(f32[4,8,24,128]{3,2,1,0:T(8,128)S(1)} %widen_4.1.own), channel_id=1, source_target_pairs={{0,8},{64,72},{128,136},{192,200},{194,202},{130,138},{66,74},{2,1... | collective-permute-start | bytes 1179656 | tf_op jit(solution)/shard_map/ppermute | solution.py:100
  95.6 4.8 %collective-permute-done.20.far = f32[4,8,24,128]{3,2,1,0:T(8,128)S(1)} collective-permute-done((f32[4,8,24,128]{3,2,1,0:T(8,128)S(1)}, f32[4,8,24,128]{3,2,1,0:T(8,128)S(1)}, u32[]{:S(2)}, u32[]{:S(2)}) %collective-permute-start.20) | collective-permute-done | bytes 393248 | tf_op jit(solution)/shard_map/ppermute | solution.py:101
  100.4 2.5 %round_4.1 = (f32[6,8,8,128]{3,2,1,0:T(8,128)S(1)}, f32[2,24,24,128]{3,2,1,0:T(8,128)S(1)}, f32[2,24,24,128]{3,2,1,0:T(8,128)S(1)}) custom-call(f32[4,8,24,128]{3,2,1,0:T(8,128)S(1)} %widen_4.1.own, f32[4,8,24,128]{3,2,1,0:T(8,128)S(1)} %collective-permute-done.19.near, f32[4,8,24,128]{3,2,1,0:T(8,128)S(1)} %collective-permute-done.20.far, ...), custom_call_target="tpu_custom_call" | custom-call | tf_op jit(solution)/shard_map/round_4/pallas_call | solution.py:106
  104.8 6.9 %collective-permute-done.22.far = f32[6,8,8,128]{3,2,1,0:T(8,128)S(1)} collective-permute-done((f32[6,8,8,128]{3,2,1,0:T(8,128)S(1)}, f32[6,8,8,128]{3,2,1,0:T(8,128)S(1)}, u32[]{:S(2)}, u32[]{:S(2)}) %collective-permute-start.22) | collective-permute-done | bytes 196640 | tf_op jit(solution)/shard_map/ppermute | solution.py:101
  114.2 7.5 %collective-permute-done.24.far = f32[6,8,24,128]{3,2,1,0:T(8,128)S(1)} collective-permute-done((f32[6,8,24,128]{3,2,1,0:T(8,128)S(1)}, f32[6,8,24,128]{3,2,1,0:T(8,128)S(1)}, u32[]{:S(2)}, u32[]{:S(2)}) %collective-permute-start.24) | collective-permute-done | bytes 589856 | tf_op jit(solution)/shard_map/ppermute | solution.py:101
  125.7 3.7 %collective-permute-done.26.far = f32[2,8,8,128]{3,2,1,0:T(8,128)S(1)} collective-permute-done((f32[2,8,8,128]{3,2,1,0:T(8,128)S(1)}, f32[2,8,8,128]{3,2,1,0:T(8,128)S(1)}, u32[]{:S(2)}, u32[]{:S(2)}) %collective-permute-start.26) | collective-permute-done | bytes 65568 | tf_op jit(solution)/shard_map/ppermute | solution.py:101
  132.5 3.2 %collective-permute-done.28.far = f32[2,8,24,128]{3,2,1,0:T(8,128)S(1)} collective-permute-done((f32[2,8,24,128]{3,2,1,0:T(8,128)S(1)}, f32[2,8,24,128]{3,2,1,0:T(8,128)S(1)}, u32[]{:S(2)}, u32[]{:S(2)}) %collective-permute-start.28) | collective-permute-done | bytes 196640 | tf_op jit(solution)/shard_map/ppermute | solution.py:101
  136.9 6.8 %collective-permute-start.29 = (f32[2,8,8,128]{3,2,1,0:T(8,128)S(1)}, f32[2,8,8,128]{3,2,1,0:T(8,128)S(1)}, u32[]{:S(2)}, u32[]{:S(2)}) collective-permute-start(f32[2,8,8,128]{3,2,1,0:T(8,128)S(1)} %get-tuple-element.45), channel_id=1, source_target_pairs={{0,0},{64,64},{128,1},{192,65},{194,2},{130,66},{66,3},{2,67},{4,4... | collective-permute-start | bytes 196616 | tf_op jit(solution)/shard_map/ppermute | solution.py:392
  143.7 3.7 %collective-permute-start.30 = (f32[2,8,8,128]{3,2,1,0:T(8,128)S(1)}, f32[2,8,8,128]{3,2,1,0:T(8,128)S(1)}, u32[]{:S(2)}, u32[]{:S(2)}) collective-permute-start(f32[2,8,8,128]{3,2,1,0:T(8,128)S(1)} %get-tuple-element.46), channel_id=1, source_target_pairs={{0,64},{64,128},{128,65},{192,129},{194,66},{130,130},{66,67},{2,1... | collective-permute-start | bytes 196616 | tf_op jit(solution)/shard_map/ppermute | solution.py:392
  147.5 3.9 %collective-permute-start.32 = (f32[2,8,8,128]{3,2,1,0:T(8,128)S(1)}, f32[2,8,8,128]{3,2,1,0:T(8,128)S(1)}, u32[]{:S(2)}, u32[]{:S(2)}) collective-permute-start(f32[2,8,8,128]{3,2,1,0:T(8,128)S(1)} %get-tuple-element.48), channel_id=1, source_target_pairs={{0,192},{64,0},{128,193},{192,1},{194,194},{130,2},{66,195},{2,3},... | collective-permute-start | bytes 196616 | tf_op jit(solution)/shard_map/ppermute | solution.py:392
  (67 shorter events, 46.7 us)
Async XLA Ops:
  3.3 6.4 %collective-permute-start = (f32[4,8,8,128]{3,2,1,0:T(8,128)S(1)}, f32[4,8,8,128]{3,2,1,0:T(8,128)S(1)}, u32[]{:S(2)}, u32[]{:S(2)}) collective-permute-start(f32[4,8,8,128]{3,2,1,0:T(8,128)S(1)} %pick.1), channel_id=1, source_target_pairs={{0,0},{1,200},{2,202},{3,2},{4,4},{5,204},{6,206},{7,6},{8,1},{9,2... | collective-permute-start | bytes 393224 | tf_op jit(solution)/shard_map/ppermute | solution.py:344
  9.7 7.3 %collective-permute-start.2 = (f32[4,8,8,128]{3,2,1,0:T(8,128)S(1)}, f32[4,8,8,128]{3,2,1,0:T(8,128)S(1)}, u32[]{:S(2)}, u32[]{:S(2)}) collective-permute-start(f32[4,8,8,128]{3,2,1,0:T(8,128)S(1)} %collective-permute-done.own), channel_id=1, source_target_pairs={{0,6},{64,128},{128,64},{192,194},{194,192},{130,66},{66,130},{2,4... | collective-permute-start | bytes 393224 | tf_op jit(solution)/shard_map/ppermute | solution.py:101
  10.6 6.4 %collective-permute-start.1 = (f32[4,8,8,128]{3,2,1,0:T(8,128)S(1)}, f32[4,8,8,128]{3,2,1,0:T(8,128)S(1)}, u32[]{:S(2)}, u32[]{:S(2)}) collective-permute-start(f32[4,8,8,128]{3,2,1,0:T(8,128)S(1)} %collective-permute-done.own), channel_id=1, source_target_pairs={{0,64},{64,0},{128,192},{192,128},{194,130},{130,194},{66,2},{2,66... | collective-permute-start | bytes 393224 | tf_op jit(solution)/shard_map/ppermute | solution.py:100
  17.6 7.4 %collective-permute-start.4 = (f32[4,8,24,128]{3,2,1,0:T(8,128)S(1)}, f32[4,8,24,128]{3,2,1,0:T(8,128)S(1)}, u32[]{:S(2)}, u32[]{:S(2)}) collective-permute-start(f32[4,8,24,128]{3,2,1,0:T(8,128)S(1)} %widen_0.1.own), channel_id=1, source_target_pairs={{0,57},{64,121},{128,185},{192,249},{194,251},{130,187},{66,123},{... | collective-permute-start | bytes 1179656 | tf_op jit(solution)/shard_map/ppermute | solution.py:101
  41.3 9.0 %collective-permute-start.10 = (f32[6,8,8,128]{3,2,1,0:T(8,128)S(1)}, f32[6,8,8,128]{3,2,1,0:T(8,128)S(1)}, u32[]{:S(2)}, u32[]{:S(2)}) collective-permute-start(f32[6,8,8,128]{3,2,1,0:T(8,128)S(1)} %get-tuple-element.31.own), channel_id=1, source_target_pairs={{0,6},{64,128},{128,64},{192,194},{194,192},{130,66},{66,130},{2,4... | collective-permute-start | bytes 589832 | tf_op jit(solution)/shard_map/ppermute | solution.py:101
  42.8 7.6 %collective-permute-start.9 = (f32[6,8,8,128]{3,2,1,0:T(8,128)S(1)}, f32[6,8,8,128]{3,2,1,0:T(8,128)S(1)}, u32[]{:S(2)}, u32[]{:S(2)}) collective-permute-start(f32[6,8,8,128]{3,2,1,0:T(8,128)S(1)} %get-tuple-element.31.own), channel_id=1, source_target_pairs={{0,64},{64,0},{128,192},{192,128},{194,130},{130,194},{66,2},{2,66... | collective-permute-start | bytes 589832 | tf_op jit(solution)/shard_map/ppermute | solution.py:100
  51.0 9.4 %collective-permute-start.12 = (f32[6,8,24,128]{3,2,1,0:T(8,128)S(1)}, f32[6,8,24,128]{3,2,1,0:T(8,128)S(1)}, u32[]{:S(2)}, u32[]{:S(2)}) collective-permute-start(f32[6,8,24,128]{3,2,1,0:T(8,128)S(1)} %widen_2.1.own), channel_id=1, source_target_pairs={{0,57},{64,121},{128,185},{192,249},{194,251},{130,187},{66,123},{... | collective-permute-start | bytes 1769480 | tf_op jit(solution)/shard_map/ppermute | solution.py:101
  51.1 9.3 %collective-permute-start.11 = (f32[6,8,24,128]{3,2,1,0:T(8,128)S(1)}, f32[6,8,24,128]{3,2,1,0:T(8,128)S(1)}, u32[]{:S(2)}, u32[]{:S(2)}) collective-permute-start(f32[6,8,24,128]{3,2,1,0:T(8,128)S(1)} %widen_2.1.own), channel_id=1, source_target_pairs={{0,8},{64,72},{128,136},{192,200},{194,202},{130,138},{66,74},{2,1... | collective-permute-start | bytes 1769480 | tf_op jit(solution)/shard_map/ppermute | solution.py:100
  62.3 8.4 %collective-permute-start.14 = (f32[6,8,8,128]{3,2,1,0:T(8,128)S(1)}, f32[6,8,8,128]{3,2,1,0:T(8,128)S(1)}, u32[]{:S(2)}, u32[]{:S(2)}) collective-permute-start(f32[6,8,8,128]{3,2,1,0:T(8,128)S(1)} %get-tuple-element.34.own), channel_id=1, source_target_pairs={{0,6},{64,128},{128,64},{192,194},{194,192},{130,66},{66,130},{2,4... | collective-permute-start | bytes 589832 | tf_op jit(solution)/shard_map/ppermute | solution.py:101
  64.2 6.6 %collective-permute-start.13 = (f32[6,8,8,128]{3,2,1,0:T(8,128)S(1)}, f32[6,8,8,128]{3,2,1,0:T(8,128)S(1)}, u32[]{:S(2)}, u32[]{:S(2)}) collective-permute-start(f32[6,8,8,128]{3,2,1,0:T(8,128)S(1)} %get-tuple-element.34.own), channel_id=1, source_target_pairs={{0,64},{64,0},{128,192},{192,128},{194,130},{130,194},{66,2},{2,66... | collective-permute-start | bytes 589832 | tf_op jit(solution)/shard_map/ppermute | solution.py:100
  71.5 9.4 %collective-permute-start.16 = (f32[6,8,24,128]{3,2,1,0:T(8,128)S(1)}, f32[6,8,24,128]{3,2,1,0:T(8,128)S(1)}, u32[]{:S(2)}, u32[]{:S(2)}) collective-permute-start(f32[6,8,24,128]{3,2,1,0:T(8,128)S(1)} %widen_3.1.own), channel_id=1, source_target_pairs={{0,57},{64,121},{128,185},{192,249},{194,251},{130,187},{66,123},{... | collective-permute-start | bytes 1769480 | tf_op jit(solution)/shard_map/ppermute | solution.py:101
  71.6 9.3 %collective-permute-start.15 = (f32[6,8,24,128]{3,2,1,0:T(8,128)S(1)}, f32[6,8,24,128]{3,2,1,0:T(8,128)S(1)}, u32[]{:S(2)}, u32[]{:S(2)}) collective-permute-start(f32[6,8,24,128]{3,2,1,0:T(8,128)S(1)} %widen_3.1.own), channel_id=1, source_target_pairs={{0,8},{64,72},{128,136},{192,200},{194,202},{130,138},{66,74},{2,1... | collective-permute-start | bytes 1769480 | tf_op jit(solution)/shard_map/ppermute | solution.py:100
  84.8 7.5 %collective-permute-start.18 = (f32[4,8,8,128]{3,2,1,0:T(8,128)S(1)}, f32[4,8,8,128]{3,2,1,0:T(8,128)S(1)}, u32[]{:S(2)}, u32[]{:S(2)}) collective-permute-start(f32[4,8,8,128]{3,2,1,0:T(8,128)S(1)} %get-tuple-element.36.own), channel_id=1, source_target_pairs={{0,6},{64,128},{128,64},{192,194},{194,192},{130,66},{66,130},{2,4... | collective-permute-start | bytes 393224 | tf_op jit(solution)/shard_map/ppermute | solution.py:101
  86.4 6.0 %collective-permute-start.17 = (f32[4,8,8,128]{3,2,1,0:T(8,128)S(1)}, f32[4,8,8,128]{3,2,1,0:T(8,128)S(1)}, u32[]{:S(2)}, u32[]{:S(2)}) collective-permute-start(f32[4,8,8,128]{3,2,1,0:T(8,128)S(1)} %get-tuple-element.36.own), channel_id=1, source_target_pairs={{0,64},{64,0},{128,192},{192,128},{194,130},{130,194},{66,2},{2,66... | collective-permute-start | bytes 393224 | tf_op jit(solution)/shard_map/ppermute | solution.py:100
  93.1 7.3 %collective-permute-start.20 = (f32[4,8,24,128]{3,2,1,0:T(8,128)S(1)}, f32[4,8,24,128]{3,2,1,0:T(8,128)S(1)}, u32[]{:S(2)}, u32[]{:S(2)}) collective-permute-start(f32[4,8,24,128]{3,2,1,0:T(8,128)S(1)} %widen_4.1.own), channel_id=1, source_target_pairs={{0,57},{64,121},{128,185},{192,249},{194,251},{130,187},{66,123},{... | collective-permute-start | bytes 1179656 | tf_op jit(solution)/shard_map/ppermute | solution.py:101
  93.2 7.2 %collective-permute-start.19 = (f32[4,8,24,128]{3,2,1,0:T(8,128)S(1)}, f32[4,8,24,128]{3,2,1,0:T(8,128)S(1)}, u32[]{:S(2)}, u32[]{:S(2)}) collective-permute-start(f32[4,8,24,128]{3,2,1,0:T(8,128)S(1)} %widen_4.1.own), channel_id=1, source_target_pairs={{0,8},{64,72},{128,136},{192,200},{194,202},{130,138},{66,74},{2,1... | collective-permute-start | bytes 1179656 | tf_op jit(solution)/shard_map/ppermute | solution.py:100
  102.9 8.8 %collective-permute-start.22 = (f32[6,8,8,128]{3,2,1,0:T(8,128)S(1)}, f32[6,8,8,128]{3,2,1,0:T(8,128)S(1)}, u32[]{:S(2)}, u32[]{:S(2)}) collective-permute-start(f32[6,8,8,128]{3,2,1,0:T(8,128)S(1)} %get-tuple-element.39.own), channel_id=1, source_target_pairs={{0,6},{64,128},{128,64},{192,194},{194,192},{130,66},{66,130},{2,4... | collective-permute-start | bytes 589832 | tf_op jit(solution)/shard_map/ppermute | solution.py:101
  104.8 6.9 %collective-permute-start.21 = (f32[6,8,8,128]{3,2,1,0:T(8,128)S(1)}, f32[6,8,8,128]{3,2,1,0:T(8,128)S(1)}, u32[]{:S(2)}, u32[]{:S(2)}) collective-permute-start(f32[6,8,8,128]{3,2,1,0:T(8,128)S(1)} %get-tuple-element.39.own), channel_id=1, source_target_pairs={{0,64},{64,0},{128,192},{192,128},{194,130},{130,194},{66,2},{2,66... | collective-permute-start | bytes 589832 | tf_op jit(solution)/shard_map/ppermute | solution.py:100
  112.3 9.4 %collective-permute-start.24 = (f32[6,8,24,128]{3,2,1,0:T(8,128)S(1)}, f32[6,8,24,128]{3,2,1,0:T(8,128)S(1)}, u32[]{:S(2)}, u32[]{:S(2)}) collective-permute-start(f32[6,8,24,128]{3,2,1,0:T(8,128)S(1)} %widen_5.1.own), channel_id=1, source_target_pairs={{0,57},{64,121},{128,185},{192,249},{194,251},{130,187},{66,123},{... | collective-permute-start | bytes 1769480 | tf_op jit(solution)/shard_map/ppermute | solution.py:101
  112.4 9.3 %collective-permute-start.23 = (f32[6,8,24,128]{3,2,1,0:T(8,128)S(1)}, f32[6,8,24,128]{3,2,1,0:T(8,128)S(1)}, u32[]{:S(2)}, u32[]{:S(2)}) collective-permute-start(f32[6,8,24,128]{3,2,1,0:T(8,128)S(1)} %widen_5.1.own), channel_id=1, source_target_pairs={{0,8},{64,72},{128,136},{192,200},{194,202},{130,138},{66,74},{2,1... | collective-permute-start | bytes 1769480 | tf_op jit(solution)/shard_map/ppermute | solution.py:100
  136.9 14.6 %collective-permute-start.29 = (f32[2,8,8,128]{3,2,1,0:T(8,128)S(1)}, f32[2,8,8,128]{3,2,1,0:T(8,128)S(1)}, u32[]{:S(2)}, u32[]{:S(2)}) collective-permute-start(f32[2,8,8,128]{3,2,1,0:T(8,128)S(1)} %get-tuple-element.45), channel_id=1, source_target_pairs={{0,0},{64,64},{128,1},{192,65},{194,2},{130,66},{66,3},{2,67},{4,4... | collective-permute-start | bytes 196616 | tf_op jit(solution)/shard_map/ppermute | solution.py:392
  143.7 7.8 %collective-permute-start.30 = (f32[2,8,8,128]{3,2,1,0:T(8,128)S(1)}, f32[2,8,8,128]{3,2,1,0:T(8,128)S(1)}, u32[]{:S(2)}, u32[]{:S(2)}) collective-permute-start(f32[2,8,8,128]{3,2,1,0:T(8,128)S(1)} %get-tuple-element.46), channel_id=1, source_target_pairs={{0,64},{64,128},{128,65},{192,129},{194,66},{130,130},{66,67},{2,1... | collective-permute-start | bytes 196616 | tf_op jit(solution)/shard_map/ppermute | solution.py:392
  147.4 6.2 %collective-permute-start.31 = (f32[2,8,8,128]{3,2,1,0:T(8,128)S(1)}, f32[2,8,8,128]{3,2,1,0:T(8,128)S(1)}, u32[]{:S(2)}, u32[]{:S(2)}) collective-permute-start(f32[2,8,8,128]{3,2,1,0:T(8,128)S(1)} %get-tuple-element.47), channel_id=1, source_target_pairs={{0,128},{64,192},{128,129},{192,193},{194,130},{130,194},{66,131},... | collective-permute-start | bytes 196616 | tf_op jit(solution)/shard_map/ppermute | solution.py:392
  147.5 8.4 %collective-permute-start.32 = (f32[2,8,8,128]{3,2,1,0:T(8,128)S(1)}, f32[2,8,8,128]{3,2,1,0:T(8,128)S(1)}, u32[]{:S(2)}, u32[]{:S(2)}) collective-permute-start(f32[2,8,8,128]{3,2,1,0:T(8,128)S(1)} %get-tuple-element.48), channel_id=1, source_target_pairs={{0,192},{64,0},{128,193},{192,1},{194,194},{130,2},{66,195},{2,3},... | collective-permute-start | bytes 196616 | tf_op jit(solution)/shard_map/ppermute | solution.py:392
  (12 other events, 48.5 us)
where the time goes:
time: 160 us; the launch traced here: 157 us
  waiting for transfers between devices  83.6 us (52%)
  starting transfers between devices  49.1 us (31%)
  Pallas kernels  21.5 us (13%)
  local copies, waits for them, and re-layouts  2.77 us (2%)
    ppermute x14, waiting for transfers between devices, swap(): lax.ppermute(array, AXES, pairs_along(dim, True))  74.7 us
    pallas_call x16, Pallas kernels, call(): pl.pallas_call(kernel, name=name, out_shape=[jax.ShapeDtypeStruct(s, jnp....  21.5 us
    ppermute x14, starting transfers between devices, swap(): lax.ppermute(array, AXES, pairs_along(dim, False))  16.2 us
    ppermute x4, starting transfers between devices, per_device(): lax.ppermute(o, AXES, gather_pairs(turn))  14.6 us
    ppermute x14, starting transfers between devices, swap(): lax.ppermute(array, AXES, pairs_along(dim, True))  14.5 us
    ppermute x4, waiting for transfers between devices, per_device(): lax.ppermute(o, AXES, gather_pairs(turn))  4.43 us
    ppermute x1, starting transfers between devices, per_device(): own = lax.ppermute(own, AXES, spread_pairs())  3.91 us
  transfers between devices with their start and end apart: 33, of which 22 were waited for; matrix products, arithmetic and copies ran while one was open for 0% of the time, Pallas kernels for 0%

commit v1 on v0

v1 whole, which is shorter than its diff:
```python
import functools

import jax
import jax.numpy as jnp
import numpy as np
from jax import lax
from jax.experimental import pallas as pl
from jax.experimental.pallas import tpu as pltpu
from jax.sharding import PartitionSpec as P


BRICK = 8
EXT = 3 * BRICK
LANES = 128
AXES = ("level", "gx", "gy")
COEF = (0.5, 0.25)
INV = tuple(1.0 / (1.0 + 6.0 * c) for c in COEF)
MIX = tuple(c / (1.0 + 6.0 * c) for c in COEF)
STEPS = 4
VMEM = pl.BlockSpec(memory_space=pltpu.VMEM)
ANY = pl.BlockSpec(memory_space=pl.ANY)


def quad_table(step_count):
    table_rows = []
    for n in range(step_count):
        first_node = min(max(n - 1, 0), step_count - 3)
        weights_row = []
        for j in range(4):
            coeffs = [1.0]
            for i in range(4):
                if i != j:
                    shifted = [0.0] + coeffs
                    scaled_terms = [-float(first_node + i) * c for c in coeffs] + [0.0]
                    coeffs = [
                        (shifted[k] + scaled_terms[k]) / float(j - i) for k in range(len(shifted))
                    ]
            integral = 0.0
            for k in range(len(coeffs)):
                integral = integral + coeffs[k] * ((n + 1.0) ** (k + 1) - float(n) ** (k + 1)) / (
                    k + 1.0
                )
            weights_row.append(float(np.float32(integral)))
        table_rows.append(weights_row)
    return table_rows


TABLE = quad_table(STEPS)


def linear(level, gx, gy):
    return (level * 8 + gx) * 8 + gy


def walk(x, level):
    return level if x % 2 == 0 else 3 - level


def device_at(bx, by):
    z, core = bx // 2, bx % 2
    x, place = by // 4, by % 4
    return linear(walk(x, place), (z // 2) * 2 + core, x * 2 + z % 2)


def pairs_along(dim, odd):
    pairs = []
    for bx in range(16):
        for by in range(16):
            at = [bx, by]
            at[dim] = (at[dim] ^ 1) if not odd else (((at[dim] + 1) ^ 1) - 1) % 16
            pairs.append((device_at(bx, by), device_at(*at)))
    return pairs


def spread_pairs(beside):
    pairs = []
    for level in range(4):
        for gx in range(8):
            for gy in range(8):
                x, zl = gy // 2, gy % 2
                place = walk(x, level)
                same = place // 2 == zl
                by = 4 * x + (place if same else 3 - place)
                if beside:
                    by = (((by + 1) ^ 1) - 1) % 16
                pairs.append((linear(level, gx, gy), device_at(2 * gx + (0 if same else 1), by)))
    return pairs


def gather_pairs(turn):
    pairs = []
    for bx in range(16):
        for by in range(16):
            level = 2 * (bx % 2) + (turn ^ (by % 2))
            pairs.append((device_at(bx, by), linear(level, bx // 2, by // 2)))
    return pairs


def sent(array, dim, odd):
    return lax.ppermute(array, AXES, pairs_along(dim, odd))


def call(kernel, name, out_shapes, args, scratch=(), space=VMEM, out_space=VMEM):
    return pl.pallas_call(
        kernel,
        name=name,
        out_shape=[jax.ShapeDtypeStruct(s, jnp.float32) for s in out_shapes],
        in_specs=[space] * len(args),
        out_specs=[out_space] * len(out_shapes),
        scratch_shapes=[s if not isinstance(s, tuple) else pltpu.VMEM(s, jnp.float32) for s in scratch],
        compiler_params=pltpu.CompilerParams(vmem_limit_bytes=40 << 20),
    )(*args)


def planes(halo):
    return range(BRICK - halo, 2 * BRICK + halo)


OWN = slice(BRICK, 2 * BRICK)


def rows(x, halo):
    away = max(BRICK - x, x - (2 * BRICK - 1), 0)
    return slice(0, EXT) if away < halo else OWN


def around(prev, cur, nxt, at):
    second = pltpu.roll(cur, 1, 0) + pltpu.roll(cur, EXT - 1, 0)
    third = pltpu.roll(cur[at], 1, 1) + pltpu.roll(cur[at], LANES - 1, 1)
    return (prev[at] + nxt[at]) + (second[at] + third)


def reacted(u, v, feed, both):
    uptake = u * v * v
    return 0.5 * (feed * (1.0 - u) - uptake), 0.5 * (uptake - both * v)


def advance(dst, field, rates, right, halo, source=None):
    for x in planes(halo - 1):
        at = rows(x, halo - 1)
        u, v = field[0, x, at], field[1, x, at]
        du, dv = reacted(u, v, rates[0, x, at], rates[1, x, at])
        u, v = u + du, v + dv
        if source is not None:
            u, v = u + source[0, x, at], v + source[1, x, at]
        right[0, x, at] = INV[0] * u
        right[1, x, at] = INV[1] * v
    src = field
    for k in range(1, 5):
        span = planes(halo - k)
        prev = [src[s, span[0] - 1] for s in range(2)]
        cur = [src[s, span[0]] for s in range(2)]
        for x in span:
            at = rows(x, halo - k)
            for s in range(2):
                nxt = src[s, x + 1]
                dst[s, x, at] = right[s, x, at] + MIX[s] * around(prev[s], cur[s], nxt, at)
                prev[s], cur[s] = cur[s], nxt
        src = dst


def sources(outs, nodes, first, rates, mixed):
    for out, step, halo in outs:
        linear_w = [TABLE[step][j] - (1.0 if first + j == step + 1 else 0.0) for j in range(4)]
        react_w = [TABLE[step][j] - (1.0 if first + j == step else 0.0) for j in range(4)]
        total = sum(react_w)
        for x in planes(halo + 1):
            at = rows(x, halo + 1)
            us = [node[0, x, at] for node in nodes]
            vs = [node[1, x, at] for node in nodes]
            mix_u = sum(w * u for w, u in zip(linear_w, us))
            mix_v = sum(w * v for w, v in zip(linear_w, vs))
            mixed[0, x, at], mixed[1, x, at] = mix_u, mix_v
            if x in planes(halo):
                after, now = step + 1 - first, step - first
                sum_u = mix_u + (us[after] - us[now])
                sum_v = mix_v + (vs[after] - vs[now])
                uptake = sum(w * (u * v * v) for w, u, v in zip(react_w, us, vs))
                out[0, x, at] = 0.5 * (rates[0, x, at] * (total - sum_u) - uptake)
                out[1, x, at] = 0.5 * (uptake - rates[1, x, at] * sum_v)
        span = planes(halo)
        for s in range(2):
            prev, cur = mixed[s, span[0] - 1], mixed[s, span[0]]
            for x in span:
                at = rows(x, halo)
                nxt = mixed[s, x + 1]
                out[s, x, at] = out[s, x, at] + COEF[s] * (around(prev, cur, nxt, at) - 6.0 * cur[at])
                prev, cur = cur, nxt


FULL = (1, 8, 7, None, None)
NEAR = (1, 4, 3, 4, 0)
RING_Y = (5, 8, 7, 0, 4)
RING_S = (4, 7, 7, 1, 3)


def tiles_y(kinds):
    return sum(2 if kind is FULL else 1 for kind in kinds)


def tiles_x(kind):
    return kind[1] - kind[0] + 1 + kind[2]


def row_index():
    return lax.broadcasted_iota(jnp.int32, (BRICK, LANES), 0)


def four(first):
    index = row_index()
    return (index >= first) & (index < first + 4)


def even_y():
    return (lax.axis_index("level") + lax.axis_index("gy") // 2) % 2 == 0


def pack_y(outs, kinds, fields):
    even = even_y()
    at = 0
    for kind, field in zip(kinds, fields):
        if kind is not FULL:
            masks = [
                four(jnp.where(even, kind[3], kind[4])),
                four(jnp.where(even, kind[4], kind[3])),
            ]
        for i in range(BRICK):
            u, v = field[0, BRICK + i, OWN], field[1, BRICK + i, OWN]
            if kind is FULL:
                for out in outs:
                    out[at, i], out[at + 1, i] = u, v
            else:
                v = pltpu.roll(v, 4, 0)
                for out, mask in zip(outs, masks):
                    out[at, i] = jnp.where(mask, u, v)
        at += tiles_y([kind])


def widen(kinds, near, far, *refs):
    fields, (wide, to_near, to_far) = refs[: len(kinds)], refs[len(kinds) :]
    even = even_y()
    at = 0
    for f, (kind, field) in enumerate(zip(kinds, fields)):
        for i in range(BRICK):
            for s in range(2):
                tile = at + (s if kind is FULL else 0)
                a, b = near[tile, i], far[tile, i]
                low, high = jnp.where(even, b, a), jnp.where(even, a, b)
                if kind is not FULL and s == 1:
                    low, high = pltpu.roll(low, 4, 0), pltpu.roll(high, 4, 0)
                if kind in (RING_Y, RING_S):
                    low = jnp.where(four(kind[3]), low, field[s, BRICK + i, :BRICK])
                    high = jnp.where(four(kind[4]), high, field[s, BRICK + i, 2 * BRICK :])
                wide[2 * f + s, i, :BRICK] = low
                wide[2 * f + s, i, OWN] = field[s, BRICK + i, OWN]
                wide[2 * f + s, i, 2 * BRICK :] = high
        at += tiles_y([kind])
    pack_x(kinds, wide, to_near, to_far)


def pack_x(kinds, wide, to_near, to_far):
    index = row_index()
    at = 0
    for f, kind in enumerate(kinds):
        first, last, corners = kind[:3]
        for s in range(2):
            field = wide.at[2 * f + s]
            for out, plane in ((to_near, lambda e: BRICK - e), (to_far, lambda e: e - 1)):
                for e in range(first, last + 1):
                    out[at + e - first] = field[plane(e), OWN]
                for e in range(1, corners + 1):
                    low, other = (e, BRICK - e) if corners == 7 else (4, e)
                    out[at + last - first + e] = jnp.where(
                        index >= low, field[plane(e), :BRICK], field[plane(other), 2 * BRICK :]
                    )
            at += tiles_x(kind)


def assemble(kinds, dsts, wide, near, far, bases=()):
    bases = list(bases)
    at = 0
    for f, (kind, dst) in enumerate(zip(kinds, dsts)):
        first, last, corners = kind[:3]
        base = bases.pop(0) if kind in (RING_Y, RING_S) else None
        for s in range(2):
            for i in range(BRICK):
                dst[s, BRICK + i] = wide[2 * f + s, i]
            for ref, plane in ((near, lambda e: 2 * BRICK - 1 + e), (far, lambda e: BRICK - e)):
                for e in range(1, first):
                    dst[s, plane(e), OWN] = base[s, plane(e), OWN]
                for e in range(first, last + 1):
                    dst[s, plane(e), OWN] = ref[at + e - first]
                for e in range(1, corners + 1):
                    other = BRICK - e if corners == 7 else e
                    both = ref[at + last - first + e]
                    dst[s, plane(e), :BRICK] = both
                    dst[s, plane(other), 2 * BRICK :] = both
            at += tiles_x(kind)


def pick(state, feed, kill, pair, brick, state_v, feed_v, kill_v, sems):
    x, low, level = lax.axis_index("gy") // 2, lax.axis_index("gy") % 2, lax.axis_index("level")
    place = jnp.where(x % 2 == 0, level, 3 - level)
    same = place // 2 == low
    q = jnp.where(same, place, 3 - place) % 2
    half = pl.ds(jnp.where(same, 0, BRICK), BRICK)
    copies = [
        pltpu.make_async_copy(state.at[:, half], state_v, sems.at[0]),
        pltpu.make_async_copy(feed.at[half], feed_v, sems.at[1]),
        pltpu.make_async_copy(kill.at[half], kill_v, sems.at[2]),
    ]
    for copy in copies:
        copy.start()
    for copy in copies:
        copy.wait()
    for i in range(BRICK):
        at = jnp.where(same, i, BRICK - 1 - i)
        for f, cells in enumerate((state_v[0, at], state_v[1, at], feed_v[at], kill_v[at])):
            pair[f, i] = cells
            brick[f, i] = jnp.where(q == 0, cells[:BRICK], cells[BRICK:])


def widen_0(pair, far, wide, to_near, to_far):
    even = even_y()
    for f in range(4):
        for i in range(BRICK):
            one, two, three = pair[f, i, :BRICK], pair[f, i, BRICK:], far[f, i]
            wide[f, i, :BRICK] = jnp.where(even, three, one)
            wide[f, i, OWN] = jnp.where(even, one, two)
            wide[f, i, 2 * BRICK :] = jnp.where(even, two, three)
    pack_x((FULL, FULL), wide, to_near, to_far)


KINDS = {
    0: (FULL, FULL),
    1: (FULL,),
    2: (FULL, RING_S, NEAR),
    3: (FULL, RING_Y, RING_S),
    4: (FULL, RING_S),
    5: (FULL, RING_S, NEAR),
    6: (NEAR,),
}


def round_0(wide, near, far, out, start, rates, y1, y2, right):
    assemble(KINDS[0], (start, rates), wide, near, far)
    for x in range(EXT):
        rates[1, x] = rates[0, x] + rates[1, x]
    advance(y1, start, rates, right, 8)
    advance(y2, y1, rates, right, 4)
    pack_y((out,), KINDS[1], (y2,))


def round_1(wide, near, far, start, rates, y1, out_a, out_b, y2, y3, z1, t, y4, s, right, mixed):
    assemble(KINDS[1], (y2,), wide, near, far)
    advance(y3, y2, rates, right, 8)
    sources([(s, 0, 3), (t, 1, 3)], (start, y1, y2, y3), 0, rates, mixed)
    advance(z1, start, rates, right, 4, s)
    advance(y4, y3, rates, right, 4)
    pack_y((out_a, out_b), KINDS[2], (z1, t, y4))


def round_2(wide, near, far, base, rates, y1, y2, y3, out_a, out_b, z1, z3, z2, s3, s1, y4, s2, right, mixed):
    assemble(KINDS[2], (z1, s1, y4), wide, near, far, (base,))
    advance(z2, z1, rates, right, 8, s1)
    sources([(s2, 2, 3), (s3, 3, 3)], (y1, y2, y3, y4), 1, rates, mixed)
    advance(z3, z2, rates, right, 4, s2)
    pack_y((out_a, out_b), KINDS[3], (z3, z2, s3))


def round_3(
    wide, near, far, base_y, base_s, start, rates, y1, out_a, out_b, y4, z1, z2, s2, s3, y2, y3, s, right, mixed
):
    assemble(KINDS[3], (y3, y2, s), wide, near, far, (base_y, base_s))
    advance(y4, y3, rates, right, 8, s)
    sources([(s, 0, 7), (s3, 1, 3)], (start, y1, y2, y3), 0, rates, mixed)
    advance(z1, start, rates, right, 8, s)
    advance(z2, z1, rates, right, 4, s3)
    sources([(s2, 2, 3), (s3, 3, 3)], (y1, y2, y3, y4), 1, rates, mixed)
    pack_y((out_a, out_b), KINDS[4], (z2, s2))


def round_4(
    wide, near, far, base, start, rates, y1, s3, out_a, out_b, y2, y3, z1, t, y4, s2, right, mixed
):
    assemble(KINDS[4], (y2, s2), wide, near, far, (base,))
    advance(y3, y2, rates, right, 8, s2)
    sources([(s2, 0, 3), (t, 1, 3)], (start, y1, y2, y3), 0, rates, mixed)
    advance(z1, start, rates, right, 4, s2)
    advance(y4, y3, rates, right, 4, s3)
    pack_y((out_a, out_b), KINDS[5], (z1, t, y4))


def round_5(wide, near, far, base, rates, y1, y2, y3, out_a, out_b, z3, s3, z1, s1, y4, z2, s2, right, mixed):
    assemble(KINDS[5], (z1, s1, y4), wide, near, far, (base,))
    advance(z2, z1, rates, right, 8, s1)
    sources([(s2, 2, 3), (s3, 3, 3)], (y1, y2, y3, y4), 1, rates, mixed)
    advance(z3, z2, rates, right, 4, s2)
    pack_y((out_a, out_b), KINDS[6], (z3,))


def round_6(wide, near, far, rates, s3, f0, f1, f2, keep, give, y3, y4, right, last):
    assemble(KINDS[6], (y3,), wide, near, far)
    advance(y4, y3, rates, right, 4, s3)
    core = lax.axis_index("gx") % 2
    for i in range(BRICK):
        x = jnp.where(core == 0, i, BRICK - 1 - i)
        for s in range(2):
            for level, field in enumerate((f0, f1, f2, y4)):
                last[level, s, x] = field[s, BRICK + i, OWN]
    for j in range(2):
        keep[j] = last[2 * core + j]
        give[j] = last[2 * (1 - core) + j]


def join(keep, got, out_0, out_1):
    core, odd = lax.axis_index("gx") % 2, jnp.where(even_y(), 0, 1)
    for turn, out in enumerate((out_0, out_1)):
        j = jnp.where(odd == turn, 0, 1)
        for i in range(BRICK):
            for s in range(2):
                out[s, core * BRICK + i] = keep[j, s, i]
                out[s, (1 - core) * BRICK + i] = got[j, s, i]


def put(in_0, in_1, out, sems):
    odd = lax.axis_index("level") % 2
    copies = []
    for turn, piece in enumerate((in_0, in_1)):
        q = jnp.where(odd == turn, 0, 1)
        at = pl.ds(pl.multiple_of(q * BRICK, BRICK), BRICK)
        copies.append(pltpu.make_async_copy(piece, out.at[0, :, :, at], sems.at[turn]))
    for copy in copies:
        copy.start()
    for copy in copies:
        copy.wait()


def per_device(state, feed, kill):
    field = (2, EXT, EXT, LANES)
    block = (2, 2 * BRICK, 2 * BRICK, LANES)

    def brick(n):
        return (n, BRICK, BRICK, LANES)

    def sends(n):
        return [brick(tiles_y(KINDS[n]))] * 2

    def wide_shapes(n):
        count = len(KINDS[n])
        flat = (2 * sum(tiles_x(kind) for kind in KINDS[n]), BRICK, LANES)
        return [(2 * count, BRICK, EXT, LANES), flat, flat]

    def along_x(wide, to_near, to_far):
        return wide, sent(to_near, 0, False), sent(to_far, 0, True)

    def exchange(n, to_near, to_far, *fields):
        got = sent(to_near, 1, False), sent(to_far, 1, True)
        kernel = functools.partial(widen, KINDS[n])
        return along_x(*call(kernel, f"widen_{n}", wide_shapes(n), (*got, *fields)))

    half = (BRICK, 2 * BRICK, LANES)
    pair, one = call(
        pick,
        "pick",
        [(4,) + half, brick(4)],
        (state, feed, kill),
        [(2,) + half, half, half, pltpu.SemaphoreType.DMA((3,))],
        space=ANY,
    )
    pair = lax.ppermute(pair, AXES, spread_pairs(False))
    one = lax.ppermute(one, AXES, spread_pairs(True))
    wide = along_x(*call(widen_0, "widen_0", wide_shapes(0), (pair, one)))
    out, start, rates, y1, y2 = call(
        round_0, "round_0", [brick(2)] + [field] * 4, wide, [field]
    )
    wide = exchange(1, out, out, y2)
    *out, y2, y3, z1, t, final_0 = call(
        round_1, "round_1", sends(2) + [field] * 5, (*wide, start, rates, y1), [field] * 3
    )
    wide = exchange(2, *out, z1, t, final_0)
    *out, z1, z3, z2, s3 = call(
        round_2, "round_2", sends(3) + [field] * 4, (*wide, t, rates, y1, y2, y3), [field] * 5
    )
    wide = exchange(3, *out, z3, z2, s3)
    *out, final_1, y1, y2, s2, s4 = call(
        round_3, "round_3", sends(4) + [field] * 5, (*wide, z2, s3, start, rates, z1), [field] * 5
    )
    wide = exchange(4, *out, y2, s2)
    *out, y2, y3, z1, t, final_2 = call(
        round_4, "round_4", sends(5) + [field] * 5, (*wide, s2, start, rates, y1, s4), [field] * 3
    )
    wide = exchange(5, *out, z1, t, final_2)
    *out, z3, s3 = call(
        round_5, "round_5", sends(6) + [field] * 2, (*wide, t, rates, y1, y2, y3), [field] * 7
    )
    wide = exchange(6, *out, z3)
    keep, give = call(
        round_6,
        "round_6",
        [(2,) + brick(2)] * 2,
        (*wide, rates, s3, final_0, final_1, final_2),
        [field] * 3 + [(4,) + brick(2)],
    )
    half = (2, 2 * BRICK, BRICK, LANES)
    outs = call(join, "join", [half] * 2, (keep, sent(give, 0, False)))
    outs = [lax.ppermute(o, AXES, gather_pairs(turn)) for turn, o in enumerate(outs)]
    return call(
        put, "put", [(1,) + block], outs, [pltpu.SemaphoreType.DMA((2,))], out_space=ANY
    )[0]


def solution(mesh):
    return jax.shard_map(
        per_device,
        mesh=mesh,
        in_specs=(P(None, "gx", "gy", None), P("gx", "gy", None), P("gx", "gy", None)),
        out_specs=P("level", None, "gx", "gy", None),
        check_vma=False,
    )
```

time: 160 us -> 134 us (0.84)
  waiting for transfers between devices: 83.6 us -> 66 us
  Pallas kernels: 21.5 us -> 16.9 us
  starting transfers between devices: 49.1 us -> 45.9 us
    ppermute x29, waiting for transfers between devices: 79.1 us -> 58.8 us  [the longest x27 56.2 us: sent(): return lax.ppermute(array, AXES, pairs_along(dim, odd))]
    ppermute x4 -> x2, starting transfers between devices: 14.6 us -> 4.84 us  [per_device(): lax.ppermute(o, AXES, gather_pairs(turn))]
    ppermute x29, starting transfers between devices: 34.6 us -> 41.1 us  [the longest x27 32.1 us: sent(): return lax.ppermute(array, AXES, pairs_along(dim, odd))]
    pallas_call x16 -> x17, Pallas kernels: 21.5 us -> 16.9 us  [call(): pl.pallas_call(kernel, name=name, out_shape=[jax.ShapeDtypeStruct(s, jnp....]
    ppermute x4 -> x2, waiting for transfers between devices: 4.43 us -> 7.24 us  [per_device(): lax.ppermute(o, AXES, gather_pairs(turn))]
  transfers between devices with their start and end apart: 33 -> 31, of which waited for: 22 -> 24; matrix products, arithmetic and copies ran while one was open for 0% -> 0% of each run, Pallas kernels for 0% -> 0%
where the time goes in v1:
time: 134 us; the launch traced here: 132 us
  waiting for transfers between devices  66 us (49%)
  starting transfers between devices  45.9 us (34%)
  Pallas kernels  16.9 us (13%)
  local copies, waits for them, and re-layouts  2.76 us (2%)
    ppermute x27, waiting for transfers between devices, sent(): return lax.ppermute(array, AXES, pairs_along(dim, odd))  56.2 us
    ppermute x27, starting transfers between devices, sent(): return lax.ppermute(array, AXES, pairs_along(dim, odd))  32.1 us
    pallas_call x17, Pallas kernels, call(): pl.pallas_call(kernel, name=name, out_shape=[jax.ShapeDtypeStruct(s, jnp....  16.9 us
    ppermute x2, waiting for transfers between devices, per_device(): lax.ppermute(o, AXES, gather_pairs(turn))  7.24 us
    ppermute x1, starting transfers between devices, per_device(): one = lax.ppermute(one, AXES, spread_pairs(True))  5.03 us
    ppermute x2, starting transfers between devices, per_device(): lax.ppermute(o, AXES, gather_pairs(turn))  4.84 us
    ppermute x1, starting transfers between devices, per_device(): pair = lax.ppermute(pair, AXES, spread_pairs(False))  3.91 us
    unnamed x6, local copies, waits for them, and re-layouts  2.76 us
  transfers between devices with their start and end apart: 31, of which 24 were waited for; matrix products, arithmetic and copies ran while one was open for 0% of the time, Pallas kernels for 0%

profile of v1, /device:TPU:32, one launch (start us, length us, event | category | flops | bytes accessed | tf_op | source)
XLA Modules:
  0.0 131.9 jit_solution(10594823075015784818)
XLA Ops:
  3.1 3.9 %collective-permute-start = (f32[4,8,16,128]{3,2,1,0:T(8,128)S(1)}, f32[4,8,16,128]{3,2,1,0:T(8,128)S(1)}, u32[]{:S(2)}, u32[]{:S(2)}) collective-permute-start(f32[4,8,16,128]{3,2,1,0:T(8,128)S(1)} %get-tuple-element.68), channel_id=1, source_target_pairs={{0,0},{1,200},{2,202},{3,2},{4,4},{5,204},{6,206},{7,6},{8,1},{9,2... | collective-permute-start | bytes 786440 | tf_op jit(solution)/shard_map/ppermute | solution.py:471
  7.0 5.0 %collective-permute-start.1 = (f32[4,8,8,128]{3,2,1,0:T(8,128)S(1)}, f32[4,8,8,128]{3,2,1,0:T(8,128)S(1)}, u32[]{:S(2)}, u32[]{:S(2)}) collective-permute-start(f32[4,8,8,128]{3,2,1,0:T(8,128)S(1)} %get-tuple-element.69), channel_id=1, source_target_pairs={{0,6},{1,202},{2,200},{3,4},{4,2},{5,206},{6,204},{7,0},{8,7},{9,2... | collective-permute-start | bytes 393224 | tf_op jit(solution)/shard_map/ppermute | solution.py:472
  17.9 4.5 %collective-permute-done.3.far = f32[60,8,128]{2,1,0:T(8,128)S(1)} collective-permute-done((f32[60,8,128]{2,1,0:T(8,128)S(1)}, f32[60,8,128]{2,1,0:T(8,128)S(1)}, u32[]{:S(2)}, u32[]{:S(2)}) %collective-permute-start.3) | collective-permute-done | bytes 245792 | tf_op jit(solution)/shard_map/ppermute | solution.py:100
  23.8 2.8 %collective-permute-start.5 = (f32[2,8,8,128]{3,2,1,0:T(8,128)S(1)}, f32[2,8,8,128]{3,2,1,0:T(8,128)S(1)}, u32[]{:S(2)}, u32[]{:S(2)}) collective-permute-start(f32[2,8,8,128]{3,2,1,0:T(8,128)S(1)} %get-tuple-element.73), channel_id=1, source_target_pairs={{0,6},{64,128},{128,64},{192,194},{194,192},{130,66},{66,130},{2,4... | collective-permute-start | bytes 196616 | tf_op jit(solution)/shard_map/ppermute | solution.py:100
  26.7 2.7 %collective-permute-done.5.far = f32[2,8,8,128]{3,2,1,0:T(8,128)S(1)} collective-permute-done((f32[2,8,8,128]{3,2,1,0:T(8,128)S(1)}, f32[2,8,8,128]{3,2,1,0:T(8,128)S(1)}, u32[]{:S(2)}, u32[]{:S(2)}) %collective-permute-start.5) | collective-permute-done | bytes 65568 | tf_op jit(solution)/shard_map/ppermute | solution.py:100
  31.9 2.6 %collective-permute-start.7 = (f32[30,8,128]{2,1,0:T(8,128)S(1)}, f32[30,8,128]{2,1,0:T(8,128)S(1)}, u32[]{:S(2)}, u32[]{:S(2)}) collective-permute-start(f32[30,8,128]{2,1,0:T(8,128)S(1)} %get-tuple-element.77), channel_id=1, source_target_pairs={{0,57},{64,121},{128,185},{192,249},{194,251},{130,187},{66,123},{... | collective-permute-start | bytes 368648 | tf_op jit(solution)/shard_map/ppermute | solution.py:100
  37.0 2.7 %round_1.1 = (f32[4,8,8,128]{3,2,1,0:T(8,128)S(1)}, f32[4,8,8,128]{3,2,1,0:T(8,128)S(1)}, f32[2,24,24,128]{3,2,1,0:T(8,128)S(1)}, f32[2,24,24,128]{3,2,1,0:T(8,1...) custom-call(f32[2,8,24,128]{3,2,1,0:T(8,128)S(1)} %get-tuple-element.75.wide, ...), custom_call_target="tpu_custom_call" | custom-call | tf_op jit(solution)/shard_map/round_1/pallas_call | solution.py:104
  41.1 4.8 %collective-permute-done.8.near = f32[4,8,8,128]{3,2,1,0:T(8,128)S(1)} collective-permute-done((f32[4,8,8,128]{3,2,1,0:T(8,128)S(1)}, f32[4,8,8,128]{3,2,1,0:T(8,128)S(1)}, u32[]{:S(2)}, u32[]{:S(2)}) %collective-permute-start.8) | collective-permute-done | bytes 131104 | tf_op jit(solution)/shard_map/ppermute | solution.py:100
  49.3 4.2 %collective-permute-done.11.far = f32[66,8,128]{2,1,0:T(8,128)S(1)} collective-permute-done((f32[66,8,128]{2,1,0:T(8,128)S(1)}, f32[66,8,128]{2,1,0:T(8,128)S(1)}, u32[]{:S(2)}, u32[]{:S(2)}) %collective-permute-start.11) | collective-permute-done | bytes 270368 | tf_op jit(solution)/shard_map/ppermute | solution.py:100
  57.6 4.0 %collective-permute-done.12.near = f32[4,8,8,128]{3,2,1,0:T(8,128)S(1)} collective-permute-done((f32[4,8,8,128]{3,2,1,0:T(8,128)S(1)}, f32[4,8,8,128]{3,2,1,0:T(8,128)S(1)}, u32[]{:S(2)}, u32[]{:S(2)}) %collective-permute-start.12) | collective-permute-done | bytes 131104 | tf_op jit(solution)/shard_map/ppermute | solution.py:100
  63.1 2.8 %collective-permute-start.15 = (f32[74,8,128]{2,1,0:T(8,128)S(1)}, f32[74,8,128]{2,1,0:T(8,128)S(1)}, u32[]{:S(2)}, u32[]{:S(2)}) collective-permute-start(f32[74,8,128]{2,1,0:T(8,128)S(1)} %get-tuple-element.98), channel_id=1, source_target_pairs={{0,57},{64,121},{128,185},{192,249},{194,251},{130,187},{66,123},{... | collective-permute-start | bytes 909320 | tf_op jit(solution)/shard_map/ppermute | solution.py:100
  66.0 4.5 %collective-permute-done.15.far = f32[74,8,128]{2,1,0:T(8,128)S(1)} collective-permute-done((f32[74,8,128]{2,1,0:T(8,128)S(1)}, f32[74,8,128]{2,1,0:T(8,128)S(1)}, u32[]{:S(2)}, u32[]{:S(2)}) %collective-permute-start.15) | collective-permute-done | bytes 303136 | tf_op jit(solution)/shard_map/ppermute | solution.py:100
  70.5 3.8 %round_3.1 = (f32[3,8,8,128]{3,2,1,0:T(8,128)S(1)}, f32[3,8,8,128]{3,2,1,0:T(8,128)S(1)}, f32[2,24,24,128]{3,2,1,0:T(8,128)S(1)}, f32[2,24,24,128]{3,2,1,0:T(8,1...) custom-call(f32[6,8,24,128]{3,2,1,0:T(8,128)S(1)} %get-tuple-element.96.wide, ...), custom_call_target="tpu_custom_call" | custom-call | tf_op jit(solution)/shard_map/round_3/pallas_call | solution.py:104
  75.6 3.3 %collective-permute-done.16.near = f32[3,8,8,128]{3,2,1,0:T(8,128)S(1)} collective-permute-done((f32[3,8,8,128]{3,2,1,0:T(8,128)S(1)}, f32[3,8,8,128]{3,2,1,0:T(8,128)S(1)}, u32[]{:S(2)}, u32[]{:S(2)}) %collective-permute-start.16) | collective-permute-done | bytes 98336 | tf_op jit(solution)/shard_map/ppermute | solution.py:100
  80.4 3.2 %collective-permute-start.19 = (f32[52,8,128]{2,1,0:T(8,128)S(1)}, f32[52,8,128]{2,1,0:T(8,128)S(1)}, u32[]{:S(2)}, u32[]{:S(2)}) collective-permute-start(f32[52,8,128]{2,1,0:T(8,128)S(1)} %get-tuple-element.106), channel_id=1, source_target_pairs={{0,57},{64,121},{128,185},{192,249},{194,251},{130,187},{66,123},{... | collective-permute-start | bytes 638984 | tf_op jit(solution)/shard_map/ppermute | solution.py:100
  83.7 3.5 %collective-permute-done.19.far = f32[52,8,128]{2,1,0:T(8,128)S(1)} collective-permute-done((f32[52,8,128]{2,1,0:T(8,128)S(1)}, f32[52,8,128]{2,1,0:T(8,128)S(1)}, u32[]{:S(2)}, u32[]{:S(2)}) %collective-permute-start.19) | collective-permute-done | bytes 213024 | tf_op jit(solution)/shard_map/ppermute | solution.py:100
  87.2 2.7 %round_4.1 = (f32[4,8,8,128]{3,2,1,0:T(8,128)S(1)}, f32[4,8,8,128]{3,2,1,0:T(8,128)S(1)}, f32[2,24,24,128]{3,2,1,0:T(8,128)S(1)}, f32[2,24,24,128]{3,2,1,0:T(8,1...) custom-call(f32[4,8,24,128]{3,2,1,0:T(8,128)S(1)} %get-tuple-element.104.wid, ...), custom_call_target="tpu_custom_call" | custom-call | tf_op jit(solution)/shard_map/round_4/pallas_call | solution.py:104
  91.9 3.0 %collective-permute-done.20.near = f32[4,8,8,128]{3,2,1,0:T(8,128)S(1)} collective-permute-done((f32[4,8,8,128]{3,2,1,0:T(8,128)S(1)}, f32[4,8,8,128]{3,2,1,0:T(8,128)S(1)}, u32[]{:S(2)}, u32[]{:S(2)}) %collective-permute-start.20) | collective-permute-done | bytes 131104 | tf_op jit(solution)/shard_map/ppermute | solution.py:100
  97.0 3.3 %collective-permute-start.23 = (f32[66,8,128]{2,1,0:T(8,128)S(1)}, f32[66,8,128]{2,1,0:T(8,128)S(1)}, u32[]{:S(2)}, u32[]{:S(2)}) collective-permute-start(f32[66,8,128]{2,1,0:T(8,128)S(1)} %get-tuple-element.116), channel_id=1, source_target_pairs={{0,57},{64,121},{128,185},{192,249},{194,251},{130,187},{66,123},{... | collective-permute-start | bytes 811016 | tf_op jit(solution)/shard_map/ppermute | solution.py:100
  100.3 4.1 %collective-permute-done.23.far = f32[66,8,128]{2,1,0:T(8,128)S(1)} collective-permute-done((f32[66,8,128]{2,1,0:T(8,128)S(1)}, f32[66,8,128]{2,1,0:T(8,128)S(1)}, u32[]{:S(2)}, u32[]{:S(2)}) %collective-permute-start.23) | collective-permute-done | bytes 270368 | tf_op jit(solution)/shard_map/ppermute | solution.py:100
  108.0 2.6 %collective-permute-done.24.near = f32[1,8,8,128]{3,2,1,0:T(8,128)S(1)} collective-permute-done((f32[1,8,8,128]{3,2,1,0:T(8,128)S(1)}, f32[1,8,8,128]{3,2,1,0:T(8,128)S(1)}, u32[]{:S(2)}, u32[]{:S(2)}) %collective-permute-start.24) | collective-permute-done | bytes 32800 | tf_op jit(solution)/shard_map/ppermute | solution.py:100
  112.0 3.0 %collective-permute-start.27 = (f32[14,8,128]{2,1,0:T(8,128)S(1)}, f32[14,8,128]{2,1,0:T(8,128)S(1)}, u32[]{:S(2)}, u32[]{:S(2)}) collective-permute-start(f32[14,8,128]{2,1,0:T(8,128)S(1)} %get-tuple-element.124), channel_id=1, source_target_pairs={{0,57},{64,121},{128,185},{192,249},{194,251},{130,187},{66,123},{... | collective-permute-start | bytes 172040 | tf_op jit(solution)/shard_map/ppermute | solution.py:100
  118.9 4.6 %collective-permute-start.29 = (f32[2,16,8,128]{3,2,1,0:T(8,128)S(1)}, f32[2,16,8,128]{3,2,1,0:T(8,128)S(1)}, u32[]{:S(2)}, u32[]{:S(2)}) collective-permute-start(f32[2,16,8,128]{3,2,1,0:T(8,128)S(1)} %get-tuple-element.129), channel_id=1, source_target_pairs={{0,0},{64,64},{128,1},{192,65},{194,2},{130,66},{66,3},{2,67},{4,4... | collective-permute-start | bytes 393224 | tf_op jit(solution)/shard_map/ppermute | solution.py:507
  123.8 5.4 %collective-permute-done.29.in_0 = f32[2,16,8,128]{3,2,1,0:T(8,128)S(1)} collective-permute-done((f32[2,16,8,128]{3,2,1,0:T(8,128)S(1)}, f32[2,16,8,128]{3,2,1,0:T(8,128)S(1)}, u32[]{:S(2)}, u32[]{:S(2)}) %collective-permute-start.29) | collective-permute-done | bytes 131104 | tf_op jit(solution)/shard_map/ppermute | solution.py:507
  (61 shorter events, 44.4 us)
Async XLA Ops:
  3.1 11.5 %collective-permute-start = (f32[4,8,16,128]{3,2,1,0:T(8,128)S(1)}, f32[4,8,16,128]{3,2,1,0:T(8,128)S(1)}, u32[]{:S(2)}, u32[]{:S(2)}) collective-permute-start(f32[4,8,16,128]{3,2,1,0:T(8,128)S(1)} %get-tuple-element.68), channel_id=1, source_target_pairs={{0,0},{1,200},{2,202},{3,2},{4,4},{5,204},{6,206},{7,6},{8,1},{9,2... | collective-permute-start | bytes 786440 | tf_op jit(solution)/shard_map/ppermute | solution.py:471
  7.0 7.5 %collective-permute-start.1 = (f32[4,8,8,128]{3,2,1,0:T(8,128)S(1)}, f32[4,8,8,128]{3,2,1,0:T(8,128)S(1)}, u32[]{:S(2)}, u32[]{:S(2)}) collective-permute-start(f32[4,8,8,128]{3,2,1,0:T(8,128)S(1)} %get-tuple-element.69), channel_id=1, source_target_pairs={{0,6},{1,202},{2,200},{3,4},{4,2},{5,206},{6,204},{7,0},{8,7},{9,2... | collective-permute-start | bytes 393224 | tf_op jit(solution)/shard_map/ppermute | solution.py:472
  16.8 5.6 %collective-permute-start.3 = (f32[60,8,128]{2,1,0:T(8,128)S(1)}, f32[60,8,128]{2,1,0:T(8,128)S(1)}, u32[]{:S(2)}, u32[]{:S(2)}) collective-permute-start(f32[60,8,128]{2,1,0:T(8,128)S(1)} %get-tuple-element.72), channel_id=1, source_target_pairs={{0,57},{64,121},{128,185},{192,249},{194,251},{130,187},{66,123},{... | collective-permute-start | bytes 737288 | tf_op jit(solution)/shard_map/ppermute | solution.py:100
  23.8 5.6 %collective-permute-start.5 = (f32[2,8,8,128]{3,2,1,0:T(8,128)S(1)}, f32[2,8,8,128]{3,2,1,0:T(8,128)S(1)}, u32[]{:S(2)}, u32[]{:S(2)}) collective-permute-start(f32[2,8,8,128]{3,2,1,0:T(8,128)S(1)} %get-tuple-element.73), channel_id=1, source_target_pairs={{0,6},{64,128},{128,64},{192,194},{194,192},{130,66},{66,130},{2,4... | collective-permute-start | bytes 196616 | tf_op jit(solution)/shard_map/ppermute | solution.py:100
  26.7 4.3 %collective-permute-start.4 = (f32[2,8,8,128]{3,2,1,0:T(8,128)S(1)}, f32[2,8,8,128]{3,2,1,0:T(8,128)S(1)}, u32[]{:S(2)}, u32[]{:S(2)}) collective-permute-start(f32[2,8,8,128]{3,2,1,0:T(8,128)S(1)} %get-tuple-element.73), channel_id=1, source_target_pairs={{0,64},{64,0},{128,192},{192,128},{194,130},{130,194},{66,2},{2,66... | collective-permute-start | bytes 196616 | tf_op jit(solution)/shard_map/ppermute | solution.py:100
  31.0 3.5 %collective-permute-start.6 = (f32[30,8,128]{2,1,0:T(8,128)S(1)}, f32[30,8,128]{2,1,0:T(8,128)S(1)}, u32[]{:S(2)}, u32[]{:S(2)}) collective-permute-start(f32[30,8,128]{2,1,0:T(8,128)S(1)} %get-tuple-element.76), channel_id=1, source_target_pairs={{0,8},{64,72},{128,136},{192,200},{194,202},{130,138},{66,74},{2,1... | collective-permute-start | bytes 368648 | tf_op jit(solution)/shard_map/ppermute | solution.py:100
  31.9 5.1 %collective-permute-start.7 = (f32[30,8,128]{2,1,0:T(8,128)S(1)}, f32[30,8,128]{2,1,0:T(8,128)S(1)}, u32[]{:S(2)}, u32[]{:S(2)}) collective-permute-start(f32[30,8,128]{2,1,0:T(8,128)S(1)} %get-tuple-element.77), channel_id=1, source_target_pairs={{0,57},{64,121},{128,185},{192,249},{194,251},{130,187},{66,123},{... | collective-permute-start | bytes 368648 | tf_op jit(solution)/shard_map/ppermute | solution.py:100
  39.7 6.2 %collective-permute-start.8 = (f32[4,8,8,128]{3,2,1,0:T(8,128)S(1)}, f32[4,8,8,128]{3,2,1,0:T(8,128)S(1)}, u32[]{:S(2)}, u32[]{:S(2)}) collective-permute-start(f32[4,8,8,128]{3,2,1,0:T(8,128)S(1)} %get-tuple-element.81), channel_id=1, source_target_pairs={{0,64},{64,0},{128,192},{192,128},{194,130},{130,194},{66,2},{2,66... | collective-permute-start | bytes 393224 | tf_op jit(solution)/shard_map/ppermute | solution.py:100
  39.8 7.4 %collective-permute-start.9 = (f32[4,8,8,128]{3,2,1,0:T(8,128)S(1)}, f32[4,8,8,128]{3,2,1,0:T(8,128)S(1)}, u32[]{:S(2)}, u32[]{:S(2)}) collective-permute-start(f32[4,8,8,128]{3,2,1,0:T(8,128)S(1)} %get-tuple-element.82), channel_id=1, source_target_pairs={{0,6},{64,128},{128,64},{192,194},{194,192},{130,66},{66,130},{2,4... | collective-permute-start | bytes 393224 | tf_op jit(solution)/shard_map/ppermute | solution.py:100
  47.4 6.2 %collective-permute-start.11 = (f32[66,8,128]{2,1,0:T(8,128)S(1)}, f32[66,8,128]{2,1,0:T(8,128)S(1)}, u32[]{:S(2)}, u32[]{:S(2)}) collective-permute-start(f32[66,8,128]{2,1,0:T(8,128)S(1)} %get-tuple-element.88), channel_id=1, source_target_pairs={{0,57},{64,121},{128,185},{192,249},{194,251},{130,187},{66,123},{... | collective-permute-start | bytes 811016 | tf_op jit(solution)/shard_map/ppermute | solution.py:100
  55.7 5.9 %collective-permute-start.12 = (f32[4,8,8,128]{3,2,1,0:T(8,128)S(1)}, f32[4,8,8,128]{3,2,1,0:T(8,128)S(1)}, u32[]{:S(2)}, u32[]{:S(2)}) collective-permute-start(f32[4,8,8,128]{3,2,1,0:T(8,128)S(1)} %get-tuple-element.91), channel_id=1, source_target_pairs={{0,64},{64,0},{128,192},{192,128},{194,130},{130,194},{66,2},{2,66... | collective-permute-start | bytes 393224 | tf_op jit(solution)/shard_map/ppermute | solution.py:100
  56.4 6.6 %collective-permute-start.13 = (f32[4,8,8,128]{3,2,1,0:T(8,128)S(1)}, f32[4,8,8,128]{3,2,1,0:T(8,128)S(1)}, u32[]{:S(2)}, u32[]{:S(2)}) collective-permute-start(f32[4,8,8,128]{3,2,1,0:T(8,128)S(1)} %get-tuple-element.92), channel_id=1, source_target_pairs={{0,6},{64,128},{128,64},{192,194},{194,192},{130,66},{66,130},{2,4... | collective-permute-start | bytes 393224 | tf_op jit(solution)/shard_map/ppermute | solution.py:100
  63.1 7.3 %collective-permute-start.15 = (f32[74,8,128]{2,1,0:T(8,128)S(1)}, f32[74,8,128]{2,1,0:T(8,128)S(1)}, u32[]{:S(2)}, u32[]{:S(2)}) collective-permute-start(f32[74,8,128]{2,1,0:T(8,128)S(1)} %get-tuple-element.98), channel_id=1, source_target_pairs={{0,57},{64,121},{128,185},{192,249},{194,251},{130,187},{66,123},{... | collective-permute-start | bytes 909320 | tf_op jit(solution)/shard_map/ppermute | solution.py:100
  74.2 4.7 %collective-permute-start.16 = (f32[3,8,8,128]{3,2,1,0:T(8,128)S(1)}, f32[3,8,8,128]{3,2,1,0:T(8,128)S(1)}, u32[]{:S(2)}, u32[]{:S(2)}) collective-permute-start(f32[3,8,8,128]{3,2,1,0:T(8,128)S(1)} %get-tuple-element.100), channel_id=1, source_target_pairs={{0,64},{64,0},{128,192},{192,128},{194,130},{130,194},{66,2},{2,66... | collective-permute-start | bytes 294920 | tf_op jit(solution)/shard_map/ppermute | solution.py:100
  74.4 5.9 %collective-permute-start.17 = (f32[3,8,8,128]{3,2,1,0:T(8,128)S(1)}, f32[3,8,8,128]{3,2,1,0:T(8,128)S(1)}, u32[]{:S(2)}, u32[]{:S(2)}) collective-permute-start(f32[3,8,8,128]{3,2,1,0:T(8,128)S(1)} %get-tuple-element.101), channel_id=1, source_target_pairs={{0,6},{64,128},{128,64},{192,194},{194,192},{130,66},{66,130},{2,4... | collective-permute-start | bytes 294920 | tf_op jit(solution)/shard_map/ppermute | solution.py:100
  80.4 6.7 %collective-permute-start.19 = (f32[52,8,128]{2,1,0:T(8,128)S(1)}, f32[52,8,128]{2,1,0:T(8,128)S(1)}, u32[]{:S(2)}, u32[]{:S(2)}) collective-permute-start(f32[52,8,128]{2,1,0:T(8,128)S(1)} %get-tuple-element.106), channel_id=1, source_target_pairs={{0,57},{64,121},{128,185},{192,249},{194,251},{130,187},{66,123},{... | collective-permute-start | bytes 638984 | tf_op jit(solution)/shard_map/ppermute | solution.py:100
  89.8 5.1 %collective-permute-start.20 = (f32[4,8,8,128]{3,2,1,0:T(8,128)S(1)}, f32[4,8,8,128]{3,2,1,0:T(8,128)S(1)}, u32[]{:S(2)}, u32[]{:S(2)}) collective-permute-start(f32[4,8,8,128]{3,2,1,0:T(8,128)S(1)} %get-tuple-element.109), channel_id=1, source_target_pairs={{0,64},{64,0},{128,192},{192,128},{194,130},{130,194},{66,2},{2,66... | collective-permute-start | bytes 393224 | tf_op jit(solution)/shard_map/ppermute | solution.py:100
  90.7 6.2 %collective-permute-start.21 = (f32[4,8,8,128]{3,2,1,0:T(8,128)S(1)}, f32[4,8,8,128]{3,2,1,0:T(8,128)S(1)}, u32[]{:S(2)}, u32[]{:S(2)}) collective-permute-start(f32[4,8,8,128]{3,2,1,0:T(8,128)S(1)} %get-tuple-element.110), channel_id=1, source_target_pairs={{0,6},{64,128},{128,64},{192,194},{194,192},{130,66},{66,130},{2,4... | collective-permute-start | bytes 393224 | tf_op jit(solution)/shard_map/ppermute | solution.py:100
  97.0 7.4 %collective-permute-start.23 = (f32[66,8,128]{2,1,0:T(8,128)S(1)}, f32[66,8,128]{2,1,0:T(8,128)S(1)}, u32[]{:S(2)}, u32[]{:S(2)}) collective-permute-start(f32[66,8,128]{2,1,0:T(8,128)S(1)} %get-tuple-element.116), channel_id=1, source_target_pairs={{0,57},{64,121},{128,185},{192,249},{194,251},{130,187},{66,123},{... | collective-permute-start | bytes 811016 | tf_op jit(solution)/shard_map/ppermute | solution.py:100
  106.6 4.0 %collective-permute-start.24 = (f32[1,8,8,128]{3,2,1,0:T(8,128)S(1)}, f32[1,8,8,128]{3,2,1,0:T(8,128)S(1)}, u32[]{:S(2)}, u32[]{:S(2)}) collective-permute-start(f32[1,8,8,128]{3,2,1,0:T(8,128)S(1)} %get-tuple-element.119), channel_id=1, source_target_pairs={{0,64},{64,0},{128,192},{192,128},{194,130},{130,194},{66,2},{2,66... | collective-permute-start | bytes 98312 | tf_op jit(solution)/shard_map/ppermute | solution.py:100
  106.8 5.1 %collective-permute-start.25 = (f32[1,8,8,128]{3,2,1,0:T(8,128)S(1)}, f32[1,8,8,128]{3,2,1,0:T(8,128)S(1)}, u32[]{:S(2)}, u32[]{:S(2)}) collective-permute-start(f32[1,8,8,128]{3,2,1,0:T(8,128)S(1)} %get-tuple-element.120), channel_id=1, source_target_pairs={{0,6},{64,128},{128,64},{192,194},{194,192},{130,66},{66,130},{2,4... | collective-permute-start | bytes 98312 | tf_op jit(solution)/shard_map/ppermute | solution.py:100
  112.0 4.9 %collective-permute-start.27 = (f32[14,8,128]{2,1,0:T(8,128)S(1)}, f32[14,8,128]{2,1,0:T(8,128)S(1)}, u32[]{:S(2)}, u32[]{:S(2)}) collective-permute-start(f32[14,8,128]{2,1,0:T(8,128)S(1)} %get-tuple-element.124), channel_id=1, source_target_pairs={{0,57},{64,121},{128,185},{192,249},{194,251},{130,187},{66,123},{... | collective-permute-start | bytes 172040 | tf_op jit(solution)/shard_map/ppermute | solution.py:100
  118.9 10.2 %collective-permute-start.29 = (f32[2,16,8,128]{3,2,1,0:T(8,128)S(1)}, f32[2,16,8,128]{3,2,1,0:T(8,128)S(1)}, u32[]{:S(2)}, u32[]{:S(2)}) collective-permute-start(f32[2,16,8,128]{3,2,1,0:T(8,128)S(1)} %get-tuple-element.129), channel_id=1, source_target_pairs={{0,0},{64,64},{128,1},{192,65},{194,2},{130,66},{66,3},{2,67},{4,4... | collective-permute-start | bytes 393224 | tf_op jit(solution)/shard_map/ppermute | solution.py:507
  123.5 7.5 %collective-permute-start.30 = (f32[2,16,8,128]{3,2,1,0:T(8,128)S(1)}, f32[2,16,8,128]{3,2,1,0:T(8,128)S(1)}, u32[]{:S(2)}, u32[]{:S(2)}) collective-permute-start(f32[2,16,8,128]{3,2,1,0:T(8,128)S(1)} %get-tuple-element.130), channel_id=1, source_target_pairs={{0,64},{64,0},{128,65},{192,1},{194,66},{130,2},{66,67},{2,3},{4,6... | collective-permute-start | bytes 393224 | tf_op jit(solution)/shard_map/ppermute | solution.py:507
  (10 other events, 22.3 us)

commit v2 on v1

v2 whole, which is shorter than its diff:
```python
import functools
import itertools

import jax
import jax.numpy as jnp
import numpy as np
from jax import lax
from jax.experimental import pallas as pl
from jax.experimental.pallas import tpu as pltpu
from jax.sharding import PartitionSpec as P


BRICK = 8
EXT = 3 * BRICK
LANES = 128
AXES = ("level", "gx", "gy")
COEF = (0.5, 0.25)
INV = tuple(1.0 / (1.0 + 6.0 * c) for c in COEF)
MIX = tuple(c / (1.0 + 6.0 * c) for c in COEF)
STEPS = 4
VMEM = pl.BlockSpec(memory_space=pltpu.VMEM)
HBM = pl.BlockSpec(memory_space=pltpu.HBM)


def quad_table(step_count):
    table_rows = []
    for n in range(step_count):
        first_node = min(max(n - 1, 0), step_count - 3)
        weights_row = []
        for j in range(4):
            coeffs = [1.0]
            for i in range(4):
                if i != j:
                    shifted = [0.0] + coeffs
                    scaled_terms = [-float(first_node + i) * c for c in coeffs] + [0.0]
                    coeffs = [
                        (shifted[k] + scaled_terms[k]) / float(j - i) for k in range(len(shifted))
                    ]
            integral = 0.0
            for k in range(len(coeffs)):
                integral = integral + coeffs[k] * ((n + 1.0) ** (k + 1) - float(n) ** (k + 1)) / (
                    k + 1.0
                )
            weights_row.append(float(np.float32(integral)))
        table_rows.append(weights_row)
    return table_rows


TABLE = quad_table(STEPS)


def linear(level, gx, gy):
    return (level * 8 + gx) * 8 + gy


WALK = (
    *((0, 0), (0, 1), (0, 2), (0, 3)),
    *((1, 3), (1, 2), (1, 1), (1, 0)),
    *((2, 0), (2, 1), (2, 2), (2, 3)),
    *((3, 3), (3, 2), (3, 1), (3, 0)),
)


def device_at(bx, by):
    (x, y), z = WALK[by], bx // 2
    core = (bx + (z % 4 != 3)) % 2
    return linear(y, (z // 2) * 2 + core, x * 2 + z % 2)


def odd_x():
    z = (lax.axis_index("gx") // 2) * 2 + lax.axis_index("gy") % 2
    return (lax.axis_index("gx") + jnp.where(z % 4 != 3, 1, 0)) % 2


def assigned(gy):
    def cost(pieces):
        return sum(abs(level - WALK[2 * gy + q][1]) for level, (p, q) in enumerate(pieces))

    return min(itertools.permutations(itertools.product(range(2), repeat=2)), key=cost)


def pairs_along(dim, odd):
    pairs = []
    for bx in range(16):
        for by in range(16):
            at = [bx, by]
            at[dim] = (at[dim] ^ 1) if not odd else (((at[dim] + 1) ^ 1) - 1) % 16
            pairs.append((device_at(bx, by), device_at(*at)))
    return pairs


def spread_pairs(beside):
    pairs = []
    for level in range(4):
        for gx in range(8):
            for gy in range(8):
                p, q = assigned(gy)[level]
                by = 2 * gy + q
                if beside:
                    by = (((by + 1) ^ 1) - 1) % 16
                pairs.append((linear(level, gx, gy), device_at(2 * gx + p, by)))
    return pairs


def gather_pairs(turn):
    pairs = []
    for bx in range(16):
        for by in range(16):
            level = 2 * (bx % 2) + (turn ^ (by % 2))
            pairs.append((device_at(bx, by), linear(level, bx // 2, by // 2)))
    return pairs


def sent(array, dim, odd):
    return lax.ppermute(array, AXES, pairs_along(dim, odd))


def call(kernel, name, out_shapes, args, scratch=(), space=VMEM, out_space=VMEM, limit=40):
    return pl.pallas_call(
        kernel,
        name=name,
        out_shape=[jax.ShapeDtypeStruct(s, jnp.float32) for s in out_shapes],
        in_specs=[space] * len(args),
        out_specs=[out_space] * len(out_shapes),
        scratch_shapes=[s if not isinstance(s, tuple) else pltpu.VMEM(s, jnp.float32) for s in scratch],
        compiler_params=pltpu.CompilerParams(vmem_limit_bytes=limit << 20),
    )(*args)


def planes(halo):
    return range(BRICK - halo, 2 * BRICK + halo)


OWN = slice(BRICK, 2 * BRICK)


def rows(x, halo):
    away = max(BRICK - x, x - (2 * BRICK - 1), 0)
    return slice(0, EXT) if away < halo else OWN


def around(prev, cur, nxt, at):
    count = cur.shape[0]
    second = pltpu.roll(cur, 1, 0) + pltpu.roll(cur, count - 1, 0)
    third = pltpu.roll(cur[at], 1, 1) + pltpu.roll(cur[at], LANES - 1, 1)
    return (prev[at] + nxt[at]) + (second[at] + third)


FIRST, SLIM = slice(0, BRICK), slice(0, 2 * BRICK)


def slim(ref, s, x):
    cells = ref[s, x]
    halo = jnp.where(row_index() < 4, cells[2 * BRICK :], cells[:BRICK])
    return jnp.concatenate([cells[OWN], halo], axis=0)


def row_index():
    return lax.broadcasted_iota(jnp.int32, (BRICK, LANES), 0)


def reacted(u, v, feed, both):
    uptake = u * v * v
    return 0.5 * (feed * (1.0 - u) - uptake), 0.5 * (uptake - both * v)


def whole(ref, s, x):
    return ref[s, x]


def advance(dst, field, rates, right, halo, source=None):
    thin = halo == 4
    load, own, full = (slim, FIRST, SLIM) if thin else (whole, OWN, slice(0, EXT))

    def part(x, halo):
        return own if rows(x, halo) == OWN else full

    for x in planes(halo - 1):
        at = part(x, halo - 1)
        u, v = load(field, 0, x)[at], load(field, 1, x)[at]
        du, dv = reacted(u, v, load(rates, 0, x)[at], load(rates, 1, x)[at])
        u, v = u + du, v + dv
        if source is not None:
            u, v = u + load(source, 0, x)[at], v + load(source, 1, x)[at]
        right[0, x, at] = INV[0] * u
        right[1, x, at] = INV[1] * v
    for k in range(1, 5):

        def get(s, x):
            return load(field, s, x) if k == 1 else dst[s, x, full]

        span = planes(halo - k)
        prev = [get(s, span[0] - 1) for s in range(2)]
        cur = [get(s, span[0]) for s in range(2)]
        for x in span:
            at = part(x, halo - k)
            for s in range(2):
                nxt = get(s, x + 1)
                new = right[s, x, at] + MIX[s] * around(prev[s], cur[s], nxt, at)
                dst[s, x, OWN if k == halo else at] = new
                prev[s], cur[s] = cur[s], nxt


def sources(outs, nodes, first, rates, mixed):
    for out, step, halo in outs:
        thin = halo == 3
        load, own, full = (slim, FIRST, SLIM) if thin else (whole, OWN, slice(0, EXT))
        linear_w = [TABLE[step][j] - (1.0 if first + j == step + 1 else 0.0) for j in range(4)]
        react_w = [TABLE[step][j] - (1.0 if first + j == step else 0.0) for j in range(4)]
        total = sum(react_w)
        for x in planes(halo + 1):
            at = own if rows(x, halo + 1) == OWN else full
            us = [load(node, 0, x)[at] for node in nodes]
            vs = [load(node, 1, x)[at] for node in nodes]
            mix_u = sum(w * u for w, u in zip(linear_w, us))
            mix_v = sum(w * v for w, v in zip(linear_w, vs))
            mixed[0, x, at], mixed[1, x, at] = mix_u, mix_v
            if x in planes(halo):
                after, now = step + 1 - first, step - first
                sum_u = mix_u + (us[after] - us[now])
                sum_v = mix_v + (vs[after] - vs[now])
                uptake = sum(w * (u * v * v) for w, u, v in zip(react_w, us, vs))
                out[0, x, at] = 0.5 * (load(rates, 0, x)[at] * (total - sum_u) - uptake)
                out[1, x, at] = 0.5 * (uptake - load(rates, 1, x)[at] * sum_v)
        span = planes(halo)
        for s in range(2):
            prev, cur = mixed[s, span[0] - 1, full], mixed[s, span[0], full]
            for x in span:
                at = own if rows(x, halo) == OWN else full
                nxt = mixed[s, x + 1, full]
                new = out[s, x, at] + COEF[s] * (around(prev, cur, nxt, at) - 6.0 * cur[at])
                if thin:
                    out[s, x, OWN] = new[FIRST]
                    if at == full:
                        out[s, x, :BRICK] = out[s, x, 2 * BRICK :] = new[BRICK:]
                else:
                    out[s, x, at] = new
                prev, cur = cur, nxt


FULL = (1, 8, 7, None, None)
NEAR = (1, 4, 3, 4, 0)
RING_Y = (5, 8, 7, 0, 4)
RING_S = (4, 7, 7, 1, 3)


def tiles_y(kinds):
    return sum(2 if kind is FULL else 1 for kind in kinds)


def tiles_x(kind):
    return kind[1] - kind[0] + 1 + kind[2]


def four(first):
    index = row_index()
    return (index >= first) & (index < first + 4)


def even_y():
    return (lax.axis_index("level") + lax.axis_index("gy") // 2) % 2 == 0


def tiles_c(kinds):
    return sum(2 * (kind[1] - kind[0] + 1) for kind in kinds)


def pack_c(out, kinds, fields):
    at = 0
    for kind, field in zip(kinds, fields):
        for s in range(2):
            for e in range(kind[0], kind[1] + 1):
                out[at] = field[s, BRICK + e - 1, OWN]
                at += 1


def pack_y(outs, kinds, fields):
    *outs, centre = outs
    pack_c(centre, kinds, fields)
    even = even_y()
    at = 0
    for kind, field in zip(kinds, fields):
        if kind is not FULL:
            masks = [
                four(jnp.where(even, kind[3], kind[4])),
                four(jnp.where(even, kind[4], kind[3])),
            ]
        for i in range(BRICK):
            u, v = field[0, BRICK + i, OWN], field[1, BRICK + i, OWN]
            if kind is FULL:
                for out in outs:
                    out[at, i], out[at + 1, i] = u, v
            else:
                v = pltpu.roll(v, 4, 0)
                for out, mask in zip(outs, masks):
                    out[at, i] = jnp.where(mask, u, v)
        at += tiles_y([kind])


def widen(kinds, near, far, *refs):
    fields, (_, wide, to_near, to_far) = refs[: len(kinds)], refs[len(kinds) :]
    even = even_y()
    at = 0
    for f, (kind, field) in enumerate(zip(kinds, fields)):
        for i in range(BRICK):
            for s in range(2):
                tile = at + (s if kind is FULL else 0)
                a, b = near[tile, i], far[tile, i]
                low, high = jnp.where(even, b, a), jnp.where(even, a, b)
                if kind is not FULL and s == 1:
                    low, high = pltpu.roll(low, 4, 0), pltpu.roll(high, 4, 0)
                if kind in (RING_Y, RING_S):
                    low = jnp.where(four(kind[3]), low, field[s, BRICK + i, :BRICK])
                    high = jnp.where(four(kind[4]), high, field[s, BRICK + i, 2 * BRICK :])
                wide[2 * f + s, i, :BRICK] = low
                wide[2 * f + s, i, OWN] = field[s, BRICK + i, OWN]
                wide[2 * f + s, i, 2 * BRICK :] = high
        at += tiles_y([kind])
    pack_x(kinds, wide, to_near, to_far, True)


def pack_x(kinds, wide, to_near, to_far, ahead):
    index = row_index()
    at = late = 0
    for f, kind in enumerate(kinds):
        first, last, corners = kind[:3]
        for s in range(2):
            field = wide.at[2 * f + s]
            for out, plane, short in ((to_near, lambda e: BRICK - e, False), (to_far, lambda e: e - 1, ahead)):
                start = late if short else at + last - first + 1
                if not short:
                    for e in range(first, last + 1):
                        out[at + e - first] = field[plane(e), OWN]
                for e in range(1, corners + 1):
                    low, other = (e, BRICK - e) if corners == 7 else (4, e)
                    out[start + e - 1] = jnp.where(
                        index >= low, field[plane(e), :BRICK], field[plane(other), 2 * BRICK :]
                    )
            at += tiles_x(kind)
            late += corners


def assemble(kinds, dsts, wide, near, far, centre=None, bases=()):
    bases = list(bases)
    at = late = ahead = 0
    for f, (kind, dst) in enumerate(zip(kinds, dsts)):
        first, last, corners = kind[:3]
        base = bases.pop(0) if kind in (RING_Y, RING_S) else None
        for s in range(2):
            for i in range(BRICK):
                dst[s, BRICK + i] = wide[2 * f + s, i]
            short = centre is not None
            for ref, own, first_at, start, plane in (
                (near, near, at, at + last - first + 1, lambda e: 2 * BRICK - 1 + e),
                (
                    far,
                    centre if short else far,
                    ahead if short else at,
                    late if short else at + last - first + 1,
                    lambda e: BRICK - e,
                ),
            ):
                for e in range(1, first):
                    dst[s, plane(e), OWN] = base[s, plane(e), OWN]
                for e in range(first, last + 1):
                    dst[s, plane(e), OWN] = own[first_at + e - first]
                for e in range(1, corners + 1):
                    other = BRICK - e if corners == 7 else e
                    both = ref[start + e - 1]
                    dst[s, plane(e), :BRICK] = both
                    dst[s, plane(other), 2 * BRICK :] = both
            at += tiles_x(kind)
            ahead += last - first + 1
            late += corners


def pick(state, feed, kill, pair, brick, state_v, feed_v, kill_v, sems):
    here = lax.axis_index("gy") * 4 + lax.axis_index("level")
    p, q = (
        sum(
            jnp.where(here == gy * 4 + level, 1, 0)
            for gy in range(8)
            for level in range(4)
            if assigned(gy)[level][axis]
        )
        for axis in range(2)
    )
    half = pl.ds(p * BRICK, BRICK)
    copies = [
        pltpu.make_async_copy(state.at[:, half], state_v, sems.at[0]),
        pltpu.make_async_copy(feed.at[half], feed_v, sems.at[1]),
        pltpu.make_async_copy(kill.at[half], kill_v, sems.at[2]),
    ]
    for copy in copies:
        copy.start()
    for copy in copies:
        copy.wait()
    for i in range(BRICK):
        for f, cells in enumerate((state_v[0, i], state_v[1, i], feed_v[i], kill_v[i])):
            pair[f, i] = cells
            brick[f, i] = jnp.where(q == 0, cells[:BRICK], cells[BRICK:])


def widen_0(pair, far, wide, to_near, to_far):
    even = even_y()
    odd = odd_x()
    for f in range(4):
        for i in range(BRICK):
            at = jnp.where(odd == 0, i, BRICK - 1 - i)
            one, two, three = pair[f, at, :BRICK], pair[f, at, BRICK:], far[f, at]
            wide[f, i, :BRICK] = jnp.where(even, three, one)
            wide[f, i, OWN] = jnp.where(even, one, two)
            wide[f, i, 2 * BRICK :] = jnp.where(even, two, three)
    pack_x((FULL, FULL), wide, to_near, to_far, False)


KINDS = {
    0: (FULL, FULL),
    1: (FULL,),
    2: (FULL, RING_S, NEAR),
    3: (FULL, RING_Y, RING_S),
    4: (FULL, RING_S),
    5: (FULL, RING_S, NEAR),
    6: (NEAR,),
}


def round_0(wide, near, far, out, out_c, start, rates, y1, y2, right):
    assemble(KINDS[0], (start, rates), wide, near, far)
    for x in range(EXT):
        rates[1, x] = rates[0, x] + rates[1, x]
    advance(y1, start, rates, right, 8)
    advance(y2, y1, rates, right, 4)
    pack_y((out, out_c), KINDS[1], (y2,))


def round_1(wide, near, far, centre, start, rates, y1, out_a, out_b, out_c, y2, y3, z1, t, y4, s, right, mixed):
    assemble(KINDS[1], (y2,), wide, near, far, centre)
    advance(y3, y2, rates, right, 8)
    sources([(s, 0, 3), (t, 1, 3)], (start, y1, y2, y3), 0, rates, mixed)
    advance(z1, start, rates, right, 4, s)
    advance(y4, y3, rates, right, 4)
    pack_y((out_a, out_b, out_c), KINDS[2], (z1, t, y4))


def round_2(wide, near, far, centre, base, rates, y1, y2, y3, out_a, out_b, out_c, z1, z3, z2, s3, s1, y4, s2, right, mixed):
    assemble(KINDS[2], (z1, s1, y4), wide, near, far, centre, (base,))
    advance(z2, z1, rates, right, 8, s1)
    sources([(s2, 2, 3), (s3, 3, 3)], (y1, y2, y3, y4), 1, rates, mixed)
    advance(z3, z2, rates, right, 4, s2)
    pack_y((out_a, out_b, out_c), KINDS[3], (z3, z2, s3))


def round_3(
    wide, near, far, centre, base_y, base_s, start, rates, y1, out_a, out_b, out_c, y4, z1, z2, s2, s3, y2, y3, s, right, mixed
):
    assemble(KINDS[3], (y3, y2, s), wide, near, far, centre, (base_y, base_s))
    advance(y4, y3, rates, right, 8, s)
    sources([(s, 0, 7), (s3, 1, 3)], (start, y1, y2, y3), 0, rates, mixed)
    advance(z1, start, rates, right, 8, s)
    advance(z2, z1, rates, right, 4, s3)
    sources([(s2, 2, 3), (s3, 3, 3)], (y1, y2, y3, y4), 1, rates, mixed)
    pack_y((out_a, out_b, out_c), KINDS[4], (z2, s2))


def round_4(
    wide, near, far, centre, base, start, rates, y1, s3, out_a, out_b, out_c, y2, y3, z1, t, y4, s2, right, mixed
):
    assemble(KINDS[4], (y2, s2), wide, near, far, centre, (base,))
    advance(y3, y2, rates, right, 8, s2)
    sources([(s2, 0, 3), (t, 1, 3)], (start, y1, y2, y3), 0, rates, mixed)
    advance(z1, start, rates, right, 4, s2)
    advance(y4, y3, rates, right, 4, s3)
    pack_y((out_a, out_b, out_c), KINDS[5], (z1, t, y4))


def round_5(wide, near, far, centre, base, rates, y1, y2, y3, out_a, out_b, out_c, z3, s3, z1, s1, y4, z2, s2, right, mixed):
    assemble(KINDS[5], (z1, s1, y4), wide, near, far, centre, (base,))
    advance(z2, z1, rates, right, 8, s1)
    sources([(s2, 2, 3), (s3, 3, 3)], (y1, y2, y3, y4), 1, rates, mixed)
    advance(z3, z2, rates, right, 4, s2)
    pack_y((out_a, out_b, out_c), KINDS[6], (z3,))


def round_6(wide, near, far, centre, rates, s3, f0, f1, f2, keep, give, y3, y4, right, last):
    assemble(KINDS[6], (y3,), wide, near, far, centre)
    advance(y4, y3, rates, right, 4, s3)
    half = odd_x()
    for i in range(BRICK):
        x = jnp.where(half == 0, i, BRICK - 1 - i)
        for s in range(2):
            for level, field in enumerate((f0, f1, f2, y4)):
                last[level, s, x] = field[s, BRICK + i, OWN]
    for j in range(2):
        keep[j] = last[2 * half + j]
        give[j] = last[2 * (1 - half) + j]


def join(keep, got, out_0, out_1):
    half, odd = odd_x(), jnp.where(even_y(), 0, 1)
    for turn, out in enumerate((out_0, out_1)):
        j = jnp.where(odd == turn, 0, 1)
        for i in range(BRICK):
            for s in range(2):
                out[s, half * BRICK + i] = keep[j, s, i]
                out[s, (1 - half) * BRICK + i] = got[j, s, i]


def put(in_0, in_1, out, sems):
    odd = lax.axis_index("level") % 2
    copies = []
    for turn, piece in enumerate((in_0, in_1)):
        q = jnp.where(odd == turn, 0, 1)
        at = pl.ds(pl.multiple_of(q * BRICK, BRICK), BRICK)
        copies.append(pltpu.make_async_copy(piece, out.at[0, :, :, at], sems.at[turn]))
    for copy in copies:
        copy.start()
    for copy in copies:
        copy.wait()


def per_device(state, feed, kill):
    field = (2, EXT, EXT, LANES)
    block = (2, 2 * BRICK, 2 * BRICK, LANES)

    def brick(n):
        return (n, BRICK, BRICK, LANES)

    def sends(n):
        return [brick(tiles_y(KINDS[n]))] * 2 + [(tiles_c(KINDS[n]), BRICK, LANES)]

    def wide_shapes(n):
        count = len(KINDS[n])
        near = 2 * sum(tiles_x(kind) for kind in KINDS[n])
        far = 2 * sum(kind[2] for kind in KINDS[n]) if n else near
        return [(2 * count, BRICK, EXT, LANES), (near, BRICK, LANES), (far, BRICK, LANES)]

    def along_x(wide, to_near, to_far):
        return wide, sent(to_near, 0, False), sent(to_far, 0, True)

    def exchange(n, to_near, to_far, centre, *fields):
        got = sent(to_near, 1, False), sent(to_far, 1, True)
        centre = sent(centre, 0, True)
        kernel = functools.partial(widen, KINDS[n])
        return (*along_x(*call(kernel, f"widen_{n}", wide_shapes(n), (*got, *fields, centre))), centre)

    part = (BRICK, 2 * BRICK, LANES)
    pair, one = call(
        pick,
        "pick",
        [(4, BRICK, 2 * BRICK, LANES), brick(4)],
        (state, feed, kill),
        [(2,) + part, part, part, pltpu.SemaphoreType.DMA((3,))],
        space=HBM,
        limit=63,
    )
    pair = lax.ppermute(pair, AXES, spread_pairs(False))
    one = lax.ppermute(one, AXES, spread_pairs(True))
    wide = along_x(*call(widen_0, "widen_0", wide_shapes(0), (pair, one)))
    out, centre, start, rates, y1, y2 = call(
        round_0, "round_0", sends(1)[1:] + [field] * 4, wide, [field]
    )
    wide = exchange(1, out, out, centre, y2)
    *out, y2, y3, z1, t, final_0 = call(
        round_1, "round_1", sends(2) + [field] * 5, (*wide, start, rates, y1), [field] * 3
    )
    wide = exchange(2, *out, z1, t, final_0)
    *out, z1, z3, z2, s3 = call(
        round_2, "round_2", sends(3) + [field] * 4, (*wide, t, rates, y1, y2, y3), [field] * 5
    )
    wide = exchange(3, *out, z3, z2, s3)
    *out, final_1, y1, y2, s2, s4 = call(
        round_3, "round_3", sends(4) + [field] * 5, (*wide, z2, s3, start, rates, z1), [field] * 5
    )
    wide = exchange(4, *out, y2, s2)
    *out, y2, y3, z1, t, final_2 = call(
        round_4, "round_4", sends(5) + [field] * 5, (*wide, s2, start, rates, y1, s4), [field] * 3
    )
    wide = exchange(5, *out, z1, t, final_2)
    *out, z3, s3 = call(
        round_5, "round_5", sends(6) + [field] * 2, (*wide, t, rates, y1, y2, y3), [field] * 7
    )
    wide = exchange(6, *out, z3)
    keep, give = call(
        round_6,
        "round_6",
        [(2,) + brick(2)] * 2,
        (*wide, rates, s3, final_0, final_1, final_2),
        [field] * 3 + [(4,) + brick(2)],
    )
    half = (2, 2 * BRICK, BRICK, LANES)
    outs = call(join, "join", [half] * 2, (keep, sent(give, 0, False)))
    outs = [lax.ppermute(o, AXES, gather_pairs(turn)) for turn, o in enumerate(outs)]
    return call(
        put, "put", [(1,) + block], outs, [pltpu.SemaphoreType.DMA((2,))], out_space=HBM
    )[0]


def solution(mesh):
    return jax.shard_map(
        per_device,
        mesh=mesh,
        in_specs=(P(None, "gx", "gy", None), P("gx", "gy", None), P("gx", "gy", None)),
        out_specs=P("level", None, "gx", "gy", None),
        check_vma=False,
    )
```

time: 134 us -> 126 us (0.940); the launches traced: 132 us -> 126 us
  waiting for transfers between devices: 66 us -> 56.8 us
  starting transfers between devices: 45.9 us -> 53 us
  local copies, waits for them, and re-layouts: 2.76 us -> 0 us
    ppermute x27 -> x33, waiting for transfers between devices: 56.2 us -> 42.5 us  [sent(): return lax.ppermute(array, AXES, pairs_along(dim, odd))]
    ppermute x27 -> x33, starting transfers between devices: 32.1 us -> 38.9 us  [sent(): return lax.ppermute(array, AXES, pairs_along(dim, odd))]
    ppermute x1, waiting for transfers between devices: 2.5 us -> 7.88 us  [per_device(): one = lax.ppermute(one, AXES, spread_pairs(True))]
    ppermute x2, starting transfers between devices: 4.84 us -> 8.01 us  [per_device(): lax.ppermute(o, AXES, gather_pairs(turn))]
    ppermute x1, starting transfers between devices: 5.03 us -> 1.93 us  [per_device(): one = lax.ppermute(one, AXES, spread_pairs(True))]
    unnamed x6 -> x0, local copies, waits for them, and re-layouts: 2.76 us -> none
  transfers between devices with their start and end apart: 31 -> 37, of which waited for: 24 -> 23; matrix products, arithmetic and copies ran while one was open for 0% -> 0% of each run, Pallas kernels for 0% -> 0%
where the time goes in v2:
time: 126 us
  waiting for transfers between devices  56.8 us (45%)
  starting transfers between devices  53 us (42%)
  Pallas kernels  16.1 us (13%)
    ppermute x33, waiting for transfers between devices, sent(): return lax.ppermute(array, AXES, pairs_along(dim, odd))  42.5 us
    ppermute x33, starting transfers between devices, sent(): return lax.ppermute(array, AXES, pairs_along(dim, odd))  38.9 us
    pallas_call x17, Pallas kernels, call(): pl.pallas_call(kernel, name=name, out_shape=[jax.ShapeDtypeStruct(s, jnp....  16.1 us
    ppermute x2, starting transfers between devices, per_device(): lax.ppermute(o, AXES, gather_pairs(turn))  8.01 us
    ppermute x1, waiting for transfers between devices, per_device(): one = lax.ppermute(one, AXES, spread_pairs(True))  7.88 us
    ppermute x2, waiting for transfers between devices, per_device(): lax.ppermute(o, AXES, gather_pairs(turn))  6.47 us
    ppermute x1, starting transfers between devices, per_device(): pair = lax.ppermute(pair, AXES, spread_pairs(False))  4.09 us
  transfers between devices with their start and end apart: 37, of which 23 were waited for; matrix products, arithmetic and copies ran while one was open for 0% of the time, Pallas kernels for 0%

profile of v2, /device:TPU:32, one launch (start us, length us, event | category | flops | bytes accessed | tf_op | source)
XLA Modules:
  0.0 126.3 jit_solution(10438404055713011622)
XLA Ops:
  1.7 4.1 %collective-permute-start = (f32[4,8,16,128]{3,2,1,0:T(8,128)}, f32[4,8,16,128]{3,2,1,0:T(8,128)S(1)}, u32[]{:S(2)}, u32[]{:S(2)}) collective-permute-start(f32[4,8,16,128]{3,2,1,0:T(8,128)} %get-tuple-element.74), channel_id=1, source_target_pairs={{0,8},{1,136},{2,202},{3,10},{4,12},{5,140},{6,206},{7,14},{8,9},{... | collective-permute-start | bytes 786440 | tf_op jit(solution)/shard_map/ppermute | solution.py:557
  7.8 7.9 %collective-permute-done.1.far = f32[4,8,8,128]{3,2,1,0:T(8,128)S(1)} collective-permute-done((f32[4,8,8,128]{3,2,1,0:T(8,128)}, f32[4,8,8,128]{3,2,1,0:T(8,128)S(1)}, u32[]{:S(2)}, u32[]{:S(2)}) %collective-permute-start.1) | collective-permute-done | bytes 131104 | tf_op jit(solution)/shard_map/ppermute | solution.py:558
  15.8 2.5 %collective-permute-start.3 = (f32[60,8,128]{2,1,0:T(8,128)S(1)}, f32[60,8,128]{2,1,0:T(8,128)S(1)}, u32[]{:S(2)}, u32[]{:S(2)}) collective-permute-start(f32[60,8,128]{2,1,0:T(8,128)S(1)} %get-tuple-element.78), channel_id=1, source_target_pairs={{8,57},{72,121},{136,185},{200,249},{202,251},{138,187},{74,123},{... | collective-permute-start | bytes 737288 | tf_op jit(solution)/shard_map/ppermute | solution.py:115
  18.4 3.9 %collective-permute-done.3.far = f32[60,8,128]{2,1,0:T(8,128)S(1)} collective-permute-done((f32[60,8,128]{2,1,0:T(8,128)S(1)}, f32[60,8,128]{2,1,0:T(8,128)S(1)}, u32[]{:S(2)}, u32[]{:S(2)}) %collective-permute-start.3) | collective-permute-done | bytes 245792 | tf_op jit(solution)/shard_map/ppermute | solution.py:115
  23.6 2.1 %collective-permute-start.6 = (f32[16,8,128]{2,1,0:T(8,128)S(1)}, f32[16,8,128]{2,1,0:T(8,128)S(1)}, u32[]{:S(2)}, u32[]{:S(2)}) collective-permute-start(f32[16,8,128]{2,1,0:T(8,128)S(1)} %get-tuple-element.81), channel_id=1, source_target_pairs={{8,57},{72,121},{136,185},{200,249},{202,251},{138,187},{74,123},{... | collective-permute-start | bytes 196616 | tf_op jit(solution)/shard_map/ppermute | solution.py:115
  25.7 3.4 %collective-permute-start.5 = (f32[2,8,8,128]{3,2,1,0:T(8,128)S(1)}, f32[2,8,8,128]{3,2,1,0:T(8,128)S(1)}, u32[]{:S(2)}, u32[]{:S(2)}) collective-permute-start(f32[2,8,8,128]{3,2,1,0:T(8,128)S(1)} %get-tuple-element.79), channel_id=1, source_target_pairs={{8,14},{72,136},{136,72},{200,202},{202,200},{138,74},{74,138},{10... | collective-permute-start | bytes 196616 | tf_op jit(solution)/shard_map/ppermute | solution.py:115
  29.1 2.2 %collective-permute-done.5.far = f32[2,8,8,128]{3,2,1,0:T(8,128)S(1)} collective-permute-done((f32[2,8,8,128]{3,2,1,0:T(8,128)S(1)}, f32[2,8,8,128]{3,2,1,0:T(8,128)S(1)}, u32[]{:S(2)}, u32[]{:S(2)}) %collective-permute-start.5) | collective-permute-done | bytes 65568 | tf_op jit(solution)/shard_map/ppermute | solution.py:115
  34.0 3.2 %collective-permute-done.8.far = f32[14,8,128]{2,1,0:T(8,128)S(1)} collective-permute-done((f32[14,8,128]{2,1,0:T(8,128)S(1)}, f32[14,8,128]{2,1,0:T(8,128)S(1)}, u32[]{:S(2)}, u32[]{:S(2)}) %collective-permute-start.8) | collective-permute-done | bytes 57376 | tf_op jit(solution)/shard_map/ppermute | solution.py:115
  37.2 2.2 %round_1.1 = (f32[4,8,8,128]{3,2,1,0:T(8,128)S(1)}, f32[4,8,8,128]{3,2,1,0:T(8,128)S(1)}, f32[32,8,128]{2,1,0:T(8,128)S(1)}, f32[2,24,24,128]{3,2,1,0:T(8,128)S(...) custom-call(f32[2,8,24,128]{3,2,1,0:T(8,128)S(1)} %get-tuple-element, ...), custom_call_target="tpu_custom_call" | custom-call | tf_op jit(solution)/shard_map/round_1/pallas_call | solution.py:119
  41.3 4.0 %collective-permute-done.9.near = f32[4,8,8,128]{3,2,1,0:T(8,128)S(1)} collective-permute-done((f32[4,8,8,128]{3,2,1,0:T(8,128)S(1)}, f32[4,8,8,128]{3,2,1,0:T(8,128)S(1)}, u32[]{:S(2)}, u32[]{:S(2)}) %collective-permute-start.9) | collective-permute-done | bytes 131104 | tf_op jit(solution)/shard_map/ppermute | solution.py:115
  46.8 2.1 %collective-permute-start.13 = (f32[34,8,128]{2,1,0:T(8,128)S(1)}, f32[34,8,128]{2,1,0:T(8,128)S(1)}, u32[]{:S(2)}, u32[]{:S(2)}) collective-permute-start(f32[34,8,128]{2,1,0:T(8,128)S(1)} %get-tuple-element.96), channel_id=1, source_target_pairs={{8,57},{72,121},{136,185},{200,249},{202,251},{138,187},{74,123},{... | collective-permute-start | bytes 417800 | tf_op jit(solution)/shard_map/ppermute | solution.py:115
  48.8 2.7 %collective-permute-done.13.far = f32[34,8,128]{2,1,0:T(8,128)S(1)} collective-permute-done((f32[34,8,128]{2,1,0:T(8,128)S(1)}, f32[34,8,128]{2,1,0:T(8,128)S(1)}, u32[]{:S(2)}, u32[]{:S(2)}) %collective-permute-start.13) | collective-permute-done | bytes 139296 | tf_op jit(solution)/shard_map/ppermute | solution.py:115
  61.1 2.4 %collective-permute-start.18 = (f32[42,8,128]{2,1,0:T(8,128)S(1)}, f32[42,8,128]{2,1,0:T(8,128)S(1)}, u32[]{:S(2)}, u32[]{:S(2)}) collective-permute-start(f32[42,8,128]{2,1,0:T(8,128)S(1)} %get-tuple-element.107), channel_id=1, source_target_pairs={{8,57},{72,121},{136,185},{200,249},{202,251},{138,187},{74,123},{... | collective-permute-start | bytes 516104 | tf_op jit(solution)/shard_map/ppermute | solution.py:115
  63.5 3.1 %collective-permute-done.18.far = f32[42,8,128]{2,1,0:T(8,128)S(1)} collective-permute-done((f32[42,8,128]{2,1,0:T(8,128)S(1)}, f32[42,8,128]{2,1,0:T(8,128)S(1)}, u32[]{:S(2)}, u32[]{:S(2)}) %collective-permute-start.18) | collective-permute-done | bytes 172064 | tf_op jit(solution)/shard_map/ppermute | solution.py:115
  66.6 3.4 %round_3.1 = (f32[3,8,8,128]{3,2,1,0:T(8,128)S(1)}, f32[3,8,8,128]{3,2,1,0:T(8,128)S(1)}, f32[24,8,128]{2,1,0:T(8,128)S(1)}, f32[2,24,24,128]{3,2,1,0:T(8,128)S(...) custom-call(f32[6,8,24,128]{3,2,1,0:T(8,128)S(1)} %get-tuple-element, ...), custom_call_target="tpu_custom_call" | custom-call | tf_op jit(solution)/shard_map/round_3/pallas_call | solution.py:119
  76.9 2.5 %collective-permute-start.23 = (f32[28,8,128]{2,1,0:T(8,128)S(1)}, f32[28,8,128]{2,1,0:T(8,128)S(1)}, u32[]{:S(2)}, u32[]{:S(2)}) collective-permute-start(f32[28,8,128]{2,1,0:T(8,128)S(1)} %get-tuple-element.116), channel_id=1, source_target_pairs={{8,57},{72,121},{136,185},{200,249},{202,251},{138,187},{74,123},{... | collective-permute-start | bytes 344072 | tf_op jit(solution)/shard_map/ppermute | solution.py:115
  79.4 2.5 %collective-permute-done.23.far = f32[28,8,128]{2,1,0:T(8,128)S(1)} collective-permute-done((f32[28,8,128]{2,1,0:T(8,128)S(1)}, f32[28,8,128]{2,1,0:T(8,128)S(1)}, u32[]{:S(2)}, u32[]{:S(2)}) %collective-permute-start.23) | collective-permute-done | bytes 114720 | tf_op jit(solution)/shard_map/ppermute | solution.py:115
  81.9 2.2 %round_4.1 = (f32[4,8,8,128]{3,2,1,0:T(8,128)S(1)}, f32[4,8,8,128]{3,2,1,0:T(8,128)S(1)}, f32[32,8,128]{2,1,0:T(8,128)S(1)}, f32[2,24,24,128]{3,2,1,0:T(8,128)S(...) custom-call(f32[4,8,24,128]{3,2,1,0:T(8,128)S(1)} %get-tuple-element, ...), custom_call_target="tpu_custom_call" | custom-call | tf_op jit(solution)/shard_map/round_4/pallas_call | solution.py:119
  87.7 2.6 %collective-permute-done.24.near = f32[4,8,8,128]{3,2,1,0:T(8,128)S(1)} collective-permute-done((f32[4,8,8,128]{3,2,1,0:T(8,128)S(1)}, f32[4,8,8,128]{3,2,1,0:T(8,128)S(1)}, u32[]{:S(2)}, u32[]{:S(2)}) %collective-permute-start.24) | collective-permute-done | bytes 131104 | tf_op jit(solution)/shard_map/ppermute | solution.py:115
  91.8 2.2 %collective-permute-start.28 = (f32[34,8,128]{2,1,0:T(8,128)S(1)}, f32[34,8,128]{2,1,0:T(8,128)S(1)}, u32[]{:S(2)}, u32[]{:S(2)}) collective-permute-start(f32[34,8,128]{2,1,0:T(8,128)S(1)} %get-tuple-element.127), channel_id=1, source_target_pairs={{8,57},{72,121},{136,185},{200,249},{202,251},{138,187},{74,123},{... | collective-permute-start | bytes 417800 | tf_op jit(solution)/shard_map/ppermute | solution.py:115
  94.0 2.7 %collective-permute-done.28.far = f32[34,8,128]{2,1,0:T(8,128)S(1)} collective-permute-done((f32[34,8,128]{2,1,0:T(8,128)S(1)}, f32[34,8,128]{2,1,0:T(8,128)S(1)}, u32[]{:S(2)}, u32[]{:S(2)}) %collective-permute-start.28) | collective-permute-done | bytes 139296 | tf_op jit(solution)/shard_map/ppermute | solution.py:115
  105.0 2.2 %collective-permute-start.33 = (f32[6,8,128]{2,1,0:T(8,128)S(1)}, f32[6,8,128]{2,1,0:T(8,128)S(1)}, u32[]{:S(2)}, u32[]{:S(2)}) collective-permute-start(f32[6,8,128]{2,1,0:T(8,128)S(1)} %get-tuple-element.136), channel_id=1, source_target_pairs={{8,57},{72,121},{136,185},{200,249},{202,251},{138,187},{74,123},{... | collective-permute-start | bytes 73736 | tf_op jit(solution)/shard_map/ppermute | solution.py:115
  110.9 6.1 %collective-permute-start.35 = (f32[2,16,8,128]{3,2,1,0:T(8,128)S(1)}, f32[2,16,8,128]{3,2,1,0:T(8,128)S(1)}, u32[]{:S(2)}, u32[]{:S(2)}) collective-permute-start(f32[2,16,8,128]{3,2,1,0:T(8,128)S(1)} %get-tuple-element.141), channel_id=1, source_target_pairs={{8,0},{72,64},{136,1},{200,65},{202,2},{138,66},{74,3},{10,67},{12... | collective-permute-start | bytes 393224 | tf_op jit(solution)/shard_map/ppermute | solution.py:593
  120.9 4.5 %collective-permute-done.36.in_1 = f32[2,16,8,128]{3,2,1,0:T(8,128)S(1)} collective-permute-done((f32[2,16,8,128]{3,2,1,0:T(8,128)S(1)}, f32[2,16,8,128]{3,2,1,0:T(8,128)S(1)}, u32[]{:S(2)}, u32[]{:S(2)}) %collective-permute-start.36) | collective-permute-done | bytes 131104 | tf_op jit(solution)/shard_map/ppermute | solution.py:593
  (67 shorter events, 49.2 us)
Async XLA Ops:
  1.7 13.9 %collective-permute-start = (f32[4,8,16,128]{3,2,1,0:T(8,128)}, f32[4,8,16,128]{3,2,1,0:T(8,128)S(1)}, u32[]{:S(2)}, u32[]{:S(2)}) collective-permute-start(f32[4,8,16,128]{3,2,1,0:T(8,128)} %get-tuple-element.74), channel_id=1, source_target_pairs={{0,8},{1,136},{2,202},{3,10},{4,12},{5,140},{6,206},{7,14},{8,9},{... | collective-permute-start | bytes 786440 | tf_op jit(solution)/shard_map/ppermute | solution.py:557
  5.8 9.8 %collective-permute-start.1 = (f32[4,8,8,128]{3,2,1,0:T(8,128)}, f32[4,8,8,128]{3,2,1,0:T(8,128)S(1)}, u32[]{:S(2)}, u32[]{:S(2)}) collective-permute-start(f32[4,8,8,128]{3,2,1,0:T(8,128)} %get-tuple-element.75), channel_id=1, source_target_pairs={{0,14},{1,72},{2,200},{3,12},{4,10},{5,76},{6,204},{7,8},{8,15},{9... | collective-permute-start | bytes 393224 | tf_op jit(solution)/shard_map/ppermute | solution.py:558
  15.8 6.4 %collective-permute-start.3 = (f32[60,8,128]{2,1,0:T(8,128)S(1)}, f32[60,8,128]{2,1,0:T(8,128)S(1)}, u32[]{:S(2)}, u32[]{:S(2)}) collective-permute-start(f32[60,8,128]{2,1,0:T(8,128)S(1)} %get-tuple-element.78), channel_id=1, source_target_pairs={{8,57},{72,121},{136,185},{200,249},{202,251},{138,187},{74,123},{... | collective-permute-start | bytes 737288 | tf_op jit(solution)/shard_map/ppermute | solution.py:115
  23.6 5.5 %collective-permute-start.6 = (f32[16,8,128]{2,1,0:T(8,128)S(1)}, f32[16,8,128]{2,1,0:T(8,128)S(1)}, u32[]{:S(2)}, u32[]{:S(2)}) collective-permute-start(f32[16,8,128]{2,1,0:T(8,128)S(1)} %get-tuple-element.81), channel_id=1, source_target_pairs={{8,57},{72,121},{136,185},{200,249},{202,251},{138,187},{74,123},{... | collective-permute-start | bytes 196616 | tf_op jit(solution)/shard_map/ppermute | solution.py:115
  25.7 5.6 %collective-permute-start.5 = (f32[2,8,8,128]{3,2,1,0:T(8,128)S(1)}, f32[2,8,8,128]{3,2,1,0:T(8,128)S(1)}, u32[]{:S(2)}, u32[]{:S(2)}) collective-permute-start(f32[2,8,8,128]{3,2,1,0:T(8,128)S(1)} %get-tuple-element.79), channel_id=1, source_target_pairs={{8,14},{72,136},{136,72},{200,202},{202,200},{138,74},{74,138},{10... | collective-permute-start | bytes 196616 | tf_op jit(solution)/shard_map/ppermute | solution.py:115
  39.4 5.9 %collective-permute-start.9 = (f32[4,8,8,128]{3,2,1,0:T(8,128)S(1)}, f32[4,8,8,128]{3,2,1,0:T(8,128)S(1)}, u32[]{:S(2)}, u32[]{:S(2)}) collective-permute-start(f32[4,8,8,128]{3,2,1,0:T(8,128)S(1)} %get-tuple-element.88), channel_id=1, source_target_pairs={{8,72},{72,8},{136,200},{200,136},{202,138},{138,202},{74,10},{10,... | collective-permute-start | bytes 393224 | tf_op jit(solution)/shard_map/ppermute | solution.py:115
  39.5 7.1 %collective-permute-start.10 = (f32[4,8,8,128]{3,2,1,0:T(8,128)S(1)}, f32[4,8,8,128]{3,2,1,0:T(8,128)S(1)}, u32[]{:S(2)}, u32[]{:S(2)}) collective-permute-start(f32[4,8,8,128]{3,2,1,0:T(8,128)S(1)} %get-tuple-element.89), channel_id=1, source_target_pairs={{8,14},{72,136},{136,72},{200,202},{202,200},{138,74},{74,138},{10... | collective-permute-start | bytes 393224 | tf_op jit(solution)/shard_map/ppermute | solution.py:115
  40.8 5.8 %collective-permute-start.11 = (f32[32,8,128]{2,1,0:T(8,128)S(1)}, f32[32,8,128]{2,1,0:T(8,128)S(1)}, u32[]{:S(2)}, u32[]{:S(2)}) collective-permute-start(f32[32,8,128]{2,1,0:T(8,128)S(1)} %get-tuple-element.93), channel_id=1, source_target_pairs={{8,57},{72,121},{136,185},{200,249},{202,251},{138,187},{74,123},{... | collective-permute-start | bytes 393224 | tf_op jit(solution)/shard_map/ppermute | solution.py:115
  53.4 5.9 %collective-permute-start.14 = (f32[4,8,8,128]{3,2,1,0:T(8,128)S(1)}, f32[4,8,8,128]{3,2,1,0:T(8,128)S(1)}, u32[]{:S(2)}, u32[]{:S(2)}) collective-permute-start(f32[4,8,8,128]{3,2,1,0:T(8,128)S(1)} %get-tuple-element.99), channel_id=1, source_target_pairs={{8,72},{72,8},{136,200},{200,136},{202,138},{138,202},{74,10},{10,... | collective-permute-start | bytes 393224 | tf_op jit(solution)/shard_map/ppermute | solution.py:115
  53.9 7.0 %collective-permute-start.15 = (f32[4,8,8,128]{3,2,1,0:T(8,128)S(1)}, f32[4,8,8,128]{3,2,1,0:T(8,128)S(1)}, u32[]{:S(2)}, u32[]{:S(2)}) collective-permute-start(f32[4,8,8,128]{3,2,1,0:T(8,128)S(1)} %get-tuple-element.100), channel_id=1, source_target_pairs={{8,14},{72,136},{136,72},{200,202},{202,200},{138,74},{74,138},{10... | collective-permute-start | bytes 393224 | tf_op jit(solution)/shard_map/ppermute | solution.py:115
  55.5 5.4 %collective-permute-start.16 = (f32[32,8,128]{2,1,0:T(8,128)S(1)}, f32[32,8,128]{2,1,0:T(8,128)S(1)}, u32[]{:S(2)}, u32[]{:S(2)}) collective-permute-start(f32[32,8,128]{2,1,0:T(8,128)S(1)} %get-tuple-element.104), channel_id=1, source_target_pairs={{8,57},{72,121},{136,185},{200,249},{202,251},{138,187},{74,123},{... | collective-permute-start | bytes 393224 | tf_op jit(solution)/shard_map/ppermute | solution.py:115
  61.0 5.6 %collective-permute-start.17 = (f32[74,8,128]{2,1,0:T(8,128)S(1)}, f32[74,8,128]{2,1,0:T(8,128)S(1)}, u32[]{:S(2)}, u32[]{:S(2)}) collective-permute-start(f32[74,8,128]{2,1,0:T(8,128)S(1)} %get-tuple-element.106), channel_id=1, source_target_pairs={{8,0},{72,64},{136,128},{200,192},{202,194},{138,130},{74,66},{10,... | collective-permute-start | bytes 909320 | tf_op jit(solution)/shard_map/ppermute | solution.py:115
  61.1 5.4 %collective-permute-start.18 = (f32[42,8,128]{2,1,0:T(8,128)S(1)}, f32[42,8,128]{2,1,0:T(8,128)S(1)}, u32[]{:S(2)}, u32[]{:S(2)}) collective-permute-start(f32[42,8,128]{2,1,0:T(8,128)S(1)} %get-tuple-element.107), channel_id=1, source_target_pairs={{8,57},{72,121},{136,185},{200,249},{202,251},{138,187},{74,123},{... | collective-permute-start | bytes 516104 | tf_op jit(solution)/shard_map/ppermute | solution.py:115
  70.0 5.2 %collective-permute-start.19 = (f32[3,8,8,128]{3,2,1,0:T(8,128)S(1)}, f32[3,8,8,128]{3,2,1,0:T(8,128)S(1)}, u32[]{:S(2)}, u32[]{:S(2)}) collective-permute-start(f32[3,8,8,128]{3,2,1,0:T(8,128)S(1)} %get-tuple-element.109), channel_id=1, source_target_pairs={{8,72},{72,8},{136,200},{200,136},{202,138},{138,202},{74,10},{10,... | collective-permute-start | bytes 294920 | tf_op jit(solution)/shard_map/ppermute | solution.py:115
  70.4 6.2 %collective-permute-start.20 = (f32[3,8,8,128]{3,2,1,0:T(8,128)S(1)}, f32[3,8,8,128]{3,2,1,0:T(8,128)S(1)}, u32[]{:S(2)}, u32[]{:S(2)}) collective-permute-start(f32[3,8,8,128]{3,2,1,0:T(8,128)S(1)} %get-tuple-element.110), channel_id=1, source_target_pairs={{8,14},{72,136},{136,72},{200,202},{202,200},{138,74},{74,138},{10... | collective-permute-start | bytes 294920 | tf_op jit(solution)/shard_map/ppermute | solution.py:115
  76.7 5.2 %collective-permute-start.22 = (f32[52,8,128]{2,1,0:T(8,128)S(1)}, f32[52,8,128]{2,1,0:T(8,128)S(1)}, u32[]{:S(2)}, u32[]{:S(2)}) collective-permute-start(f32[52,8,128]{2,1,0:T(8,128)S(1)} %get-tuple-element.115), channel_id=1, source_target_pairs={{8,0},{72,64},{136,128},{200,192},{202,194},{138,130},{74,66},{10,... | collective-permute-start | bytes 638984 | tf_op jit(solution)/shard_map/ppermute | solution.py:115
  76.9 5.0 %collective-permute-start.23 = (f32[28,8,128]{2,1,0:T(8,128)S(1)}, f32[28,8,128]{2,1,0:T(8,128)S(1)}, u32[]{:S(2)}, u32[]{:S(2)}) collective-permute-start(f32[28,8,128]{2,1,0:T(8,128)S(1)} %get-tuple-element.116), channel_id=1, source_target_pairs={{8,57},{72,121},{136,185},{200,249},{202,251},{138,187},{74,123},{... | collective-permute-start | bytes 344072 | tf_op jit(solution)/shard_map/ppermute | solution.py:115
  84.1 6.2 %collective-permute-start.24 = (f32[4,8,8,128]{3,2,1,0:T(8,128)S(1)}, f32[4,8,8,128]{3,2,1,0:T(8,128)S(1)}, u32[]{:S(2)}, u32[]{:S(2)}) collective-permute-start(f32[4,8,8,128]{3,2,1,0:T(8,128)S(1)} %get-tuple-element.119), channel_id=1, source_target_pairs={{8,72},{72,8},{136,200},{200,136},{202,138},{138,202},{74,10},{10,... | collective-permute-start | bytes 393224 | tf_op jit(solution)/shard_map/ppermute | solution.py:115
  84.7 6.8 %collective-permute-start.25 = (f32[4,8,8,128]{3,2,1,0:T(8,128)S(1)}, f32[4,8,8,128]{3,2,1,0:T(8,128)S(1)}, u32[]{:S(2)}, u32[]{:S(2)}) collective-permute-start(f32[4,8,8,128]{3,2,1,0:T(8,128)S(1)} %get-tuple-element.120), channel_id=1, source_target_pairs={{8,14},{72,136},{136,72},{200,202},{202,200},{138,74},{74,138},{10... | collective-permute-start | bytes 393224 | tf_op jit(solution)/shard_map/ppermute | solution.py:115
  86.2 5.4 %collective-permute-start.26 = (f32[32,8,128]{2,1,0:T(8,128)S(1)}, f32[32,8,128]{2,1,0:T(8,128)S(1)}, u32[]{:S(2)}, u32[]{:S(2)}) collective-permute-start(f32[32,8,128]{2,1,0:T(8,128)S(1)} %get-tuple-element.124), channel_id=1, source_target_pairs={{8,57},{72,121},{136,185},{200,249},{202,251},{138,187},{74,123},{... | collective-permute-start | bytes 393224 | tf_op jit(solution)/shard_map/ppermute | solution.py:115
  91.6 5.1 %collective-permute-start.27 = (f32[66,8,128]{2,1,0:T(8,128)S(1)}, f32[66,8,128]{2,1,0:T(8,128)S(1)}, u32[]{:S(2)}, u32[]{:S(2)}) collective-permute-start(f32[66,8,128]{2,1,0:T(8,128)S(1)} %get-tuple-element.126), channel_id=1, source_target_pairs={{8,0},{72,64},{136,128},{200,192},{202,194},{138,130},{74,66},{10,... | collective-permute-start | bytes 811016 | tf_op jit(solution)/shard_map/ppermute | solution.py:115
  98.9 5.1 %collective-permute-start.30 = (f32[1,8,8,128]{3,2,1,0:T(8,128)S(1)}, f32[1,8,8,128]{3,2,1,0:T(8,128)S(1)}, u32[]{:S(2)}, u32[]{:S(2)}) collective-permute-start(f32[1,8,8,128]{3,2,1,0:T(8,128)S(1)} %get-tuple-element.131), channel_id=1, source_target_pairs={{8,14},{72,136},{136,72},{200,202},{202,200},{138,74},{74,138},{10... | collective-permute-start | bytes 98312 | tf_op jit(solution)/shard_map/ppermute | solution.py:115
  110.9 10.0 %collective-permute-start.35 = (f32[2,16,8,128]{3,2,1,0:T(8,128)S(1)}, f32[2,16,8,128]{3,2,1,0:T(8,128)S(1)}, u32[]{:S(2)}, u32[]{:S(2)}) collective-permute-start(f32[2,16,8,128]{3,2,1,0:T(8,128)S(1)} %get-tuple-element.141), channel_id=1, source_target_pairs={{8,0},{72,64},{136,1},{200,65},{202,2},{138,66},{74,3},{10,67},{12... | collective-permute-start | bytes 393224 | tf_op jit(solution)/shard_map/ppermute | solution.py:593
  117.0 8.4 %collective-permute-start.36 = (f32[2,16,8,128]{3,2,1,0:T(8,128)S(1)}, f32[2,16,8,128]{3,2,1,0:T(8,128)S(1)}, u32[]{:S(2)}, u32[]{:S(2)}) collective-permute-start(f32[2,16,8,128]{3,2,1,0:T(8,128)S(1)} %get-tuple-element.142), channel_id=1, source_target_pairs={{8,64},{72,0},{136,65},{200,1},{202,66},{138,2},{74,67},{10,3},{12... | collective-permute-start | bytes 393224 | tf_op jit(solution)/shard_map/ppermute | solution.py:593
  (13 other events, 51.4 us)

commit v3 on v2

--- a/solution.py
+++ b/solution.py
@@ -1,5 +1,4 @@
 import functools
-import itertools
 
 import jax
 import jax.numpy as jnp
@@ -72,13 +71,6 @@
     return (lax.axis_index("gx") + jnp.where(z % 4 != 3, 1, 0)) % 2
 
 
-def assigned(gy):
-    def cost(pieces):
-        return sum(abs(level - WALK[2 * gy + q][1]) for level, (p, q) in enumerate(pieces))
-
-    return min(itertools.permutations(itertools.product(range(2), repeat=2)), key=cost)
-
-
 def pairs_along(dim, odd):
     pairs = []
     for bx in range(16):
@@ -89,16 +81,20 @@
     return pairs
 
 
+def first_sent(level, x):
+    return level // 2, level % 2, (level // 2 + x) % 2
+
+
 def spread_pairs(beside):
     pairs = []
     for level in range(4):
         for gx in range(8):
             for gy in range(8):
-                p, q = assigned(gy)[level]
-                by = 2 * gy + q
+                p, far_p, far_q = first_sent(level, gy // 2)
+                bx, by = 2 * gx + p, 2 * gy + ((level + 1) // 2 + gy) % 2
                 if beside:
-                    by = (((by + 1) ^ 1) - 1) % 16
-                pairs.append((linear(level, gx, gy), device_at(2 * gx + p, by)))
+                    bx, by = 2 * gx + far_p, (((2 * gy + far_q + 1) ^ 1) - 1) % 16
+                pairs.append((linear(level, gx, gy), device_at(bx, by)))
     return pairs
 
 
@@ -241,7 +237,7 @@
 FULL = (1, 8, 7, None, None)
 NEAR = (1, 4, 3, 4, 0)
 RING_Y = (5, 8, 7, 0, 4)
-RING_S = (4, 7, 7, 1, 3)
+RING_S = (4, 7, 6, 1, 3)
 
 
 def tiles_y(kinds):
@@ -298,7 +294,8 @@
 
 
 def widen(kinds, near, far, *refs):
-    fields, (_, wide, to_near, to_far) = refs[: len(kinds)], refs[len(kinds) :]
+    fields, refs = refs[: len(kinds)], refs[len(kinds) :]
+    to_near, to_far, wide = (None, *refs) if len(refs) == 2 else (refs[3], None, refs[2])
     even = even_y()
     at = 0
     for f, (kind, field) in enumerate(zip(kinds, fields)):
@@ -326,13 +323,18 @@
         first, last, corners = kind[:3]
         for s in range(2):
             field = wide.at[2 * f + s]
-            for out, plane, short in ((to_near, lambda e: BRICK - e, False), (to_far, lambda e: e - 1, ahead)):
+            for out, plane, short in (
+                (to_near, lambda e: BRICK - e, False),
+                (to_far, lambda e: e - 1, ahead),
+            ):
+                if out is None:
+                    continue
                 start = late if short else at + last - first + 1
                 if not short:
                     for e in range(first, last + 1):
                         out[at + e - first] = field[plane(e), OWN]
                 for e in range(1, corners + 1):
-                    low, other = (e, BRICK - e) if corners == 7 else (4, e)
+                    low, other = (4, e) if kind is NEAR else (e + 7 - corners, corners + 1 - e)
                     out[start + e - 1] = jnp.where(
                         index >= low, field[plane(e), :BRICK], field[plane(other), 2 * BRICK :]
                     )
@@ -365,7 +367,7 @@
                 for e in range(first, last + 1):
                     dst[s, plane(e), OWN] = own[first_at + e - first]
                 for e in range(1, corners + 1):
-                    other = BRICK - e if corners == 7 else e
+                    other = e if kind is NEAR else corners + 1 - e
                     both = ref[start + e - 1]
                     dst[s, plane(e), :BRICK] = both
                     dst[s, plane(other), 2 * BRICK :] = both
@@ -375,30 +377,20 @@
 
 
 def pick(state, feed, kill, pair, brick, state_v, feed_v, kill_v, sems):
-    here = lax.axis_index("gy") * 4 + lax.axis_index("level")
-    p, q = (
-        sum(
-            jnp.where(here == gy * 4 + level, 1, 0)
-            for gy in range(8)
-            for level in range(4)
-            if assigned(gy)[level][axis]
-        )
-        for axis in range(2)
-    )
-    half = pl.ds(p * BRICK, BRICK)
+    p, far_p, far_q = first_sent(lax.axis_index("level"), lax.axis_index("gy") // 2)
     copies = [
-        pltpu.make_async_copy(state.at[:, half], state_v, sems.at[0]),
-        pltpu.make_async_copy(feed.at[half], feed_v, sems.at[1]),
-        pltpu.make_async_copy(kill.at[half], kill_v, sems.at[2]),
+        pltpu.make_async_copy(source, target, sems.at[i])
+        for i, (source, target) in enumerate(((state, state_v), (feed, feed_v), (kill, kill_v)))
     ]
     for copy in copies:
         copy.start()
     for copy in copies:
         copy.wait()
-    for i in range(BRICK):
-        for f, cells in enumerate((state_v[0, i], state_v[1, i], feed_v[i], kill_v[i])):
-            pair[f, i] = cells
-            brick[f, i] = jnp.where(q == 0, cells[:BRICK], cells[BRICK:])
+    part = pl.ds(pl.multiple_of(far_q * BRICK, BRICK), BRICK)
+    for f, field in enumerate((state_v.at[0], state_v.at[1], feed_v, kill_v)):
+        for i in range(BRICK):
+            pair[f, i] = field[p * BRICK + i]
+            brick[f, i] = field[far_p * BRICK + i, part]
 
 
 def widen_0(pair, far, wide, to_near, to_far):
@@ -542,15 +534,17 @@
         got = sent(to_near, 1, False), sent(to_far, 1, True)
         centre = sent(centre, 0, True)
         kernel = functools.partial(widen, KINDS[n])
-        return (*along_x(*call(kernel, f"widen_{n}", wide_shapes(n), (*got, *fields, centre))), centre)
-
-    part = (BRICK, 2 * BRICK, LANES)
+        wide, near, far = wide_shapes(n)
+        to_far = call(kernel, f"corner_{n}", [far], (*got, *fields), [wide])[0]
+        wide, to_near = call(kernel, f"widen_{n}", [wide, near], (*got, *fields, centre, to_far))
+        return (*along_x(wide, to_near, to_far), centre)
+
     pair, one = call(
         pick,
         "pick",
         [(4, BRICK, 2 * BRICK, LANES), brick(4)],
         (state, feed, kill),
-        [(2,) + part, part, part, pltpu.SemaphoreType.DMA((3,))],
+        [block, block[1:], block[1:], pltpu.SemaphoreType.DMA((3,))],
         space=HBM,
         limit=63,
     )

time: 126 us -> 124 us (0.984)
  waiting for transfers between devices: 56.8 us -> 49.9 us
  starting transfers between devices: 53 us -> 57.5 us
    ppermute x33, waiting for transfers between devices: 42.5 us -> 36.9 us  [sent(): return lax.ppermute(array, AXES, pairs_along(dim, odd))]
    ppermute x33, starting transfers between devices: 38.9 us -> 43.5 us  [sent(): return lax.ppermute(array, AXES, pairs_along(dim, odd))]
    ppermute x1, waiting for transfers between devices: 7.88 us -> 6.5 us  [per_device(): one = lax.ppermute(one, AXES, spread_pairs(True))]
    pallas_call x17 -> x23, Pallas kernels: 16.1 us -> 16.4 us  [call(): pl.pallas_call(kernel, name=name, out_shape=[jax.ShapeDtypeStruct(s, jnp....]
where the time goes in v3:
time: 124 us
  starting transfers between devices  57.5 us (46%)
  waiting for transfers between devices  49.9 us (40%)
  Pallas kernels  16.4 us (13%)
    ppermute x33, starting transfers between devices, sent(): return lax.ppermute(array, AXES, pairs_along(dim, odd))  43.5 us
    ppermute x33, waiting for transfers between devices, sent(): return lax.ppermute(array, AXES, pairs_along(dim, odd))  36.9 us
    pallas_call x23, Pallas kernels, call(): pl.pallas_call(kernel, name=name, out_shape=[jax.ShapeDtypeStruct(s, jnp....  16.4 us
    ppermute x2, starting transfers between devices, per_device(): lax.ppermute(o, AXES, gather_pairs(turn))  7.99 us
    ppermute x1, waiting for transfers between devices, per_device(): one = lax.ppermute(one, AXES, spread_pairs(True))  6.5 us
    ppermute x2, waiting for transfers between devices, per_device(): lax.ppermute(o, AXES, gather_pairs(turn))  6.47 us
    ppermute x1, starting transfers between devices, per_device(): pair = lax.ppermute(pair, AXES, spread_pairs(False))  3.91 us
  transfers between devices with their start and end apart: 37, of which 23 were waited for; matrix products, arithmetic and copies ran while one was open for 0% of the time, Pallas kernels for 0%

profile of v3, /device:TPU:32, one launch (start us, length us, event | category | flops | bytes accessed | tf_op | source)
XLA Modules:
  0.0 124.3 jit_solution(9240405232072505437)
XLA Ops:
  1.8 3.9 %collective-permute-start = (f32[4,8,16,128]{3,2,1,0:T(8,128)}, f32[4,8,16,128]{3,2,1,0:T(8,128)S(1)}, u32[]{:S(2)}, u32[]{:S(2)}) collective-permute-start(f32[4,8,16,128]{3,2,1,0:T(8,128)} %get-tuple-element.68), channel_id=1, source_target_pairs={{0,8},{1,200},{2,202},{3,10},{4,12},{5,204},{6,206},{7,14},{8,9},{... | collective-permute-start | bytes 786440 | tf_op jit(solution)/shard_map/ppermute | solution.py:551
  5.8 2.1 %collective-permute-start.1 = (f32[4,8,8,128]{3,2,1,0:T(8,128)}, f32[4,8,8,128]{3,2,1,0:T(8,128)S(1)}, u32[]{:S(2)}, u32[]{:S(2)}) collective-permute-start(f32[4,8,8,128]{3,2,1,0:T(8,128)} %get-tuple-element.69), channel_id=1, source_target_pairs={{0,14},{1,72},{2,74},{3,12},{4,10},{5,76},{6,78},{7,8},{8,15},{9,7... | collective-permute-start | bytes 393224 | tf_op jit(solution)/shard_map/ppermute | solution.py:552
  7.9 6.5 %collective-permute-done.1.far = f32[4,8,8,128]{3,2,1,0:T(8,128)S(1)} collective-permute-done((f32[4,8,8,128]{3,2,1,0:T(8,128)}, f32[4,8,8,128]{3,2,1,0:T(8,128)S(1)}, u32[]{:S(2)}, u32[]{:S(2)}) %collective-permute-start.1) | collective-permute-done | bytes 131104 | tf_op jit(solution)/shard_map/ppermute | solution.py:552
  14.5 3.0 %collective-permute-start.3 = (f32[60,8,128]{2,1,0:T(8,128)S(1)}, f32[60,8,128]{2,1,0:T(8,128)S(1)}, u32[]{:S(2)}, u32[]{:S(2)}) collective-permute-start(f32[60,8,128]{2,1,0:T(8,128)S(1)} %get-tuple-element.72), channel_id=1, source_target_pairs={{8,57},{72,121},{136,185},{200,249},{202,251},{138,187},{74,123},{... | collective-permute-start | bytes 737288 | tf_op jit(solution)/shard_map/ppermute | solution.py:111
  17.5 3.9 %collective-permute-done.3.far = f32[60,8,128]{2,1,0:T(8,128)S(1)} collective-permute-done((f32[60,8,128]{2,1,0:T(8,128)S(1)}, f32[60,8,128]{2,1,0:T(8,128)S(1)}, u32[]{:S(2)}, u32[]{:S(2)}) %collective-permute-start.3) | collective-permute-done | bytes 245792 | tf_op jit(solution)/shard_map/ppermute | solution.py:111
  22.7 3.1 %collective-permute-start.5 = (f32[2,8,8,128]{3,2,1,0:T(8,128)S(1)}, f32[2,8,8,128]{3,2,1,0:T(8,128)S(1)}, u32[]{:S(2)}, u32[]{:S(2)}) collective-permute-start(f32[2,8,8,128]{3,2,1,0:T(8,128)S(1)} %get-tuple-element.73), channel_id=1, source_target_pairs={{8,14},{72,136},{136,72},{200,202},{202,200},{138,74},{74,138},{10... | collective-permute-start | bytes 196616 | tf_op jit(solution)/shard_map/ppermute | solution.py:111
  30.2 2.7 %collective-permute-start.8 = (f32[14,8,128]{2,1,0:T(8,128)S(1)}, f32[14,8,128]{2,1,0:T(8,128)S(1)}, u32[]{:S(2)}, u32[]{:S(2)}) collective-permute-start(f32[14,8,128]{2,1,0:T(8,128)S(1)} %corner_1.1.refs_2_), channel_id=1, source_target_pairs={{8,57},{72,121},{136,185},{200,249},{202,251},{138,187},{74,123},{... | collective-permute-start | bytes 172040 | tf_op jit(solution)/shard_map/ppermute | solution.py:111
  34.8 2.2 %round_1.1 = (f32[4,8,8,128]{3,2,1,0:T(8,128)S(1)}, f32[4,8,8,128]{3,2,1,0:T(8,128)S(1)}, f32[32,8,128]{2,1,0:T(8,128)S(1)}, f32[2,24,24,128]{3,2,1,0:T(8,128)S(...) custom-call(f32[2,8,24,128]{3,2,1,0:T(8,128)S(1)} %get-tuple-element, ...), custom_call_target="tpu_custom_call" | custom-call | tf_op jit(solution)/shard_map/round_1/pallas_call | solution.py:115
  37.0 2.1 %collective-permute-start.9 = (f32[4,8,8,128]{3,2,1,0:T(8,128)S(1)}, f32[4,8,8,128]{3,2,1,0:T(8,128)S(1)}, u32[]{:S(2)}, u32[]{:S(2)}) collective-permute-start(f32[4,8,8,128]{3,2,1,0:T(8,128)S(1)} %get-tuple-element.81), channel_id=1, source_target_pairs={{8,72},{72,8},{136,200},{200,136},{202,138},{138,202},{74,10},{10,... | collective-permute-start | bytes 393224 | tf_op jit(solution)/shard_map/ppermute | solution.py:111
  42.3 2.9 %collective-permute-done.10.far = f32[4,8,8,128]{3,2,1,0:T(8,128)S(1)} collective-permute-done((f32[4,8,8,128]{3,2,1,0:T(8,128)S(1)}, f32[4,8,8,128]{3,2,1,0:T(8,128)S(1)}, u32[]{:S(2)}, u32[]{:S(2)}) %collective-permute-start.10) | collective-permute-done | bytes 131104 | tf_op jit(solution)/shard_map/ppermute | solution.py:111
  45.5 2.7 %collective-permute-start.13 = (f32[32,8,128]{2,1,0:T(8,128)S(1)}, f32[32,8,128]{2,1,0:T(8,128)S(1)}, u32[]{:S(2)}, u32[]{:S(2)}) collective-permute-start(f32[32,8,128]{2,1,0:T(8,128)S(1)} %corner_2.1.refs_4_), channel_id=1, source_target_pairs={{8,57},{72,121},{136,185},{200,249},{202,251},{138,187},{74,123},{... | collective-permute-start | bytes 393224 | tf_op jit(solution)/shard_map/ppermute | solution.py:111
  48.2 2.6 %collective-permute-done.13.far = f32[32,8,128]{2,1,0:T(8,128)S(1)} collective-permute-done((f32[32,8,128]{2,1,0:T(8,128)S(1)}, f32[32,8,128]{2,1,0:T(8,128)S(1)}, u32[]{:S(2)}, u32[]{:S(2)}) %collective-permute-start.13) | collective-permute-done | bytes 131104 | tf_op jit(solution)/shard_map/ppermute | solution.py:111
  59.6 2.7 %collective-permute-start.18 = (f32[40,8,128]{2,1,0:T(8,128)S(1)}, f32[40,8,128]{2,1,0:T(8,128)S(1)}, u32[]{:S(2)}, u32[]{:S(2)}) collective-permute-start(f32[40,8,128]{2,1,0:T(8,128)S(1)} %corner_3.1.refs_4_), channel_id=1, source_target_pairs={{8,57},{72,121},{136,185},{200,249},{202,251},{138,187},{74,123},{... | collective-permute-start | bytes 491528 | tf_op jit(solution)/shard_map/ppermute | solution.py:111
  62.3 3.0 %collective-permute-done.18.far = f32[40,8,128]{2,1,0:T(8,128)S(1)} collective-permute-done((f32[40,8,128]{2,1,0:T(8,128)S(1)}, f32[40,8,128]{2,1,0:T(8,128)S(1)}, u32[]{:S(2)}, u32[]{:S(2)}) %collective-permute-start.18) | collective-permute-done | bytes 163872 | tf_op jit(solution)/shard_map/ppermute | solution.py:111
  65.3 3.4 %round_3.1 = (f32[3,8,8,128]{3,2,1,0:T(8,128)S(1)}, f32[3,8,8,128]{3,2,1,0:T(8,128)S(1)}, f32[24,8,128]{2,1,0:T(8,128)S(1)}, f32[2,24,24,128]{3,2,1,0:T(8,128)S(...) custom-call(f32[6,8,24,128]{3,2,1,0:T(8,128)S(1)} %get-tuple-element, ...), custom_call_target="tpu_custom_call" | custom-call | tf_op jit(solution)/shard_map/round_3/pallas_call | solution.py:115
  75.2 2.8 %collective-permute-start.23 = (f32[26,8,128]{2,1,0:T(8,128)S(1)}, f32[26,8,128]{2,1,0:T(8,128)S(1)}, u32[]{:S(2)}, u32[]{:S(2)}) collective-permute-start(f32[26,8,128]{2,1,0:T(8,128)S(1)} %corner_4.1.refs_3_), channel_id=1, source_target_pairs={{8,57},{72,121},{136,185},{200,249},{202,251},{138,187},{74,123},{... | collective-permute-start | bytes 319496 | tf_op jit(solution)/shard_map/ppermute | solution.py:111
  78.0 2.4 %collective-permute-done.23.far = f32[26,8,128]{2,1,0:T(8,128)S(1)} collective-permute-done((f32[26,8,128]{2,1,0:T(8,128)S(1)}, f32[26,8,128]{2,1,0:T(8,128)S(1)}, u32[]{:S(2)}, u32[]{:S(2)}) %collective-permute-start.23) | collective-permute-done | bytes 106528 | tf_op jit(solution)/shard_map/ppermute | solution.py:111
  80.4 2.2 %round_4.1 = (f32[4,8,8,128]{3,2,1,0:T(8,128)S(1)}, f32[4,8,8,128]{3,2,1,0:T(8,128)S(1)}, f32[32,8,128]{2,1,0:T(8,128)S(1)}, f32[2,24,24,128]{3,2,1,0:T(8,128)S(...) custom-call(f32[4,8,24,128]{3,2,1,0:T(8,128)S(1)} %get-tuple-element, ...), custom_call_target="tpu_custom_call" | custom-call | tf_op jit(solution)/shard_map/round_4/pallas_call | solution.py:115
  86.2 2.1 %collective-permute-done.24.near = f32[4,8,8,128]{3,2,1,0:T(8,128)S(1)} collective-permute-done((f32[4,8,8,128]{3,2,1,0:T(8,128)S(1)}, f32[4,8,8,128]{3,2,1,0:T(8,128)S(1)}, u32[]{:S(2)}, u32[]{:S(2)}) %collective-permute-start.24) | collective-permute-done | bytes 131104 | tf_op jit(solution)/shard_map/ppermute | solution.py:111
  89.8 2.7 %collective-permute-start.28 = (f32[32,8,128]{2,1,0:T(8,128)S(1)}, f32[32,8,128]{2,1,0:T(8,128)S(1)}, u32[]{:S(2)}, u32[]{:S(2)}) collective-permute-start(f32[32,8,128]{2,1,0:T(8,128)S(1)} %corner_5.1.refs_4_), channel_id=1, source_target_pairs={{8,57},{72,121},{136,185},{200,249},{202,251},{138,187},{74,123},{... | collective-permute-start | bytes 393224 | tf_op jit(solution)/shard_map/ppermute | solution.py:111
  92.4 2.6 %collective-permute-done.28.far = f32[32,8,128]{2,1,0:T(8,128)S(1)} collective-permute-done((f32[32,8,128]{2,1,0:T(8,128)S(1)}, f32[32,8,128]{2,1,0:T(8,128)S(1)}, u32[]{:S(2)}, u32[]{:S(2)}) %collective-permute-start.28) | collective-permute-done | bytes 131104 | tf_op jit(solution)/shard_map/ppermute | solution.py:111
  103.0 2.5 %collective-permute-start.33 = (f32[6,8,128]{2,1,0:T(8,128)S(1)}, f32[6,8,128]{2,1,0:T(8,128)S(1)}, u32[]{:S(2)}, u32[]{:S(2)}) collective-permute-start(f32[6,8,128]{2,1,0:T(8,128)S(1)} %corner_6.1.refs_2_), channel_id=1, source_target_pairs={{8,57},{72,121},{136,185},{200,249},{202,251},{138,187},{74,123},{... | collective-permute-start | bytes 73736 | tf_op jit(solution)/shard_map/ppermute | solution.py:111
  108.9 6.1 %collective-permute-start.35 = (f32[2,16,8,128]{3,2,1,0:T(8,128)S(1)}, f32[2,16,8,128]{3,2,1,0:T(8,128)S(1)}, u32[]{:S(2)}, u32[]{:S(2)}) collective-permute-start(f32[2,16,8,128]{3,2,1,0:T(8,128)S(1)} %get-tuple-element.129), channel_id=1, source_target_pairs={{8,0},{72,64},{136,1},{200,65},{202,2},{138,66},{74,3},{10,67},{12... | collective-permute-start | bytes 393224 | tf_op jit(solution)/shard_map/ppermute | solution.py:587
  118.8 4.5 %collective-permute-done.36.in_1 = f32[2,16,8,128]{3,2,1,0:T(8,128)S(1)} collective-permute-done((f32[2,16,8,128]{3,2,1,0:T(8,128)S(1)}, f32[2,16,8,128]{3,2,1,0:T(8,128)S(1)}, u32[]{:S(2)}, u32[]{:S(2)}) %collective-permute-start.36) | collective-permute-done | bytes 131104 | tf_op jit(solution)/shard_map/ppermute | solution.py:587
  (73 shorter events, 49.2 us)
Async XLA Ops:
  1.8 12.5 %collective-permute-start = (f32[4,8,16,128]{3,2,1,0:T(8,128)}, f32[4,8,16,128]{3,2,1,0:T(8,128)S(1)}, u32[]{:S(2)}, u32[]{:S(2)}) collective-permute-start(f32[4,8,16,128]{3,2,1,0:T(8,128)} %get-tuple-element.68), channel_id=1, source_target_pairs={{0,8},{1,200},{2,202},{3,10},{4,12},{5,204},{6,206},{7,14},{8,9},{... | collective-permute-start | bytes 786440 | tf_op jit(solution)/shard_map/ppermute | solution.py:551
  5.8 8.6 %collective-permute-start.1 = (f32[4,8,8,128]{3,2,1,0:T(8,128)}, f32[4,8,8,128]{3,2,1,0:T(8,128)S(1)}, u32[]{:S(2)}, u32[]{:S(2)}) collective-permute-start(f32[4,8,8,128]{3,2,1,0:T(8,128)} %get-tuple-element.69), channel_id=1, source_target_pairs={{0,14},{1,72},{2,74},{3,12},{4,10},{5,76},{6,78},{7,8},{8,15},{9,7... | collective-permute-start | bytes 393224 | tf_op jit(solution)/shard_map/ppermute | solution.py:552
  14.5 6.9 %collective-permute-start.3 = (f32[60,8,128]{2,1,0:T(8,128)S(1)}, f32[60,8,128]{2,1,0:T(8,128)S(1)}, u32[]{:S(2)}, u32[]{:S(2)}) collective-permute-start(f32[60,8,128]{2,1,0:T(8,128)S(1)} %get-tuple-element.72), channel_id=1, source_target_pairs={{8,57},{72,121},{136,185},{200,249},{202,251},{138,187},{74,123},{... | collective-permute-start | bytes 737288 | tf_op jit(solution)/shard_map/ppermute | solution.py:111
  22.7 5.6 %collective-permute-start.5 = (f32[2,8,8,128]{3,2,1,0:T(8,128)S(1)}, f32[2,8,8,128]{3,2,1,0:T(8,128)S(1)}, u32[]{:S(2)}, u32[]{:S(2)}) collective-permute-start(f32[2,8,8,128]{3,2,1,0:T(8,128)S(1)} %get-tuple-element.73), channel_id=1, source_target_pairs={{8,14},{72,136},{136,72},{200,202},{202,200},{138,74},{74,138},{10... | collective-permute-start | bytes 196616 | tf_op jit(solution)/shard_map/ppermute | solution.py:111
  37.0 5.3 %collective-permute-start.9 = (f32[4,8,8,128]{3,2,1,0:T(8,128)S(1)}, f32[4,8,8,128]{3,2,1,0:T(8,128)S(1)}, u32[]{:S(2)}, u32[]{:S(2)}) collective-permute-start(f32[4,8,8,128]{3,2,1,0:T(8,128)S(1)} %get-tuple-element.81), channel_id=1, source_target_pairs={{8,72},{72,8},{136,200},{200,136},{202,138},{138,202},{74,10},{10,... | collective-permute-start | bytes 393224 | tf_op jit(solution)/shard_map/ppermute | solution.py:111
  39.1 6.2 %collective-permute-start.10 = (f32[4,8,8,128]{3,2,1,0:T(8,128)S(1)}, f32[4,8,8,128]{3,2,1,0:T(8,128)S(1)}, u32[]{:S(2)}, u32[]{:S(2)}) collective-permute-start(f32[4,8,8,128]{3,2,1,0:T(8,128)S(1)} %get-tuple-element.82), channel_id=1, source_target_pairs={{8,14},{72,136},{136,72},{200,202},{202,200},{138,74},{74,138},{10... | collective-permute-start | bytes 393224 | tf_op jit(solution)/shard_map/ppermute | solution.py:111
  39.2 6.1 %collective-permute-start.11 = (f32[32,8,128]{2,1,0:T(8,128)S(1)}, f32[32,8,128]{2,1,0:T(8,128)S(1)}, u32[]{:S(2)}, u32[]{:S(2)}) collective-permute-start(f32[32,8,128]{2,1,0:T(8,128)S(1)} %get-tuple-element.86), channel_id=1, source_target_pairs={{8,57},{72,121},{136,185},{200,249},{202,251},{138,187},{74,123},{... | collective-permute-start | bytes 393224 | tf_op jit(solution)/shard_map/ppermute | solution.py:111
  45.4 5.4 %collective-permute-start.12 = (f32[64,8,128]{2,1,0:T(8,128)S(1)}, f32[64,8,128]{2,1,0:T(8,128)S(1)}, u32[]{:S(2)}, u32[]{:S(2)}) collective-permute-start(f32[64,8,128]{2,1,0:T(8,128)S(1)} %get-tuple-element.88), channel_id=1, source_target_pairs={{8,0},{72,64},{136,128},{200,192},{202,194},{138,130},{74,66},{10,... | collective-permute-start | bytes 786440 | tf_op jit(solution)/shard_map/ppermute | solution.py:111
  45.5 5.3 %collective-permute-start.13 = (f32[32,8,128]{2,1,0:T(8,128)S(1)}, f32[32,8,128]{2,1,0:T(8,128)S(1)}, u32[]{:S(2)}, u32[]{:S(2)}) collective-permute-start(f32[32,8,128]{2,1,0:T(8,128)S(1)} %corner_2.1.refs_4_), channel_id=1, source_target_pairs={{8,57},{72,121},{136,185},{200,249},{202,251},{138,187},{74,123},{... | collective-permute-start | bytes 393224 | tf_op jit(solution)/shard_map/ppermute | solution.py:111
  52.7 5.3 %collective-permute-start.14 = (f32[4,8,8,128]{3,2,1,0:T(8,128)S(1)}, f32[4,8,8,128]{3,2,1,0:T(8,128)S(1)}, u32[]{:S(2)}, u32[]{:S(2)}) collective-permute-start(f32[4,8,8,128]{3,2,1,0:T(8,128)S(1)} %get-tuple-element.91), channel_id=1, source_target_pairs={{8,72},{72,8},{136,200},{200,136},{202,138},{138,202},{74,10},{10,... | collective-permute-start | bytes 393224 | tf_op jit(solution)/shard_map/ppermute | solution.py:111
  52.8 6.6 %collective-permute-start.15 = (f32[4,8,8,128]{3,2,1,0:T(8,128)S(1)}, f32[4,8,8,128]{3,2,1,0:T(8,128)S(1)}, u32[]{:S(2)}, u32[]{:S(2)}) collective-permute-start(f32[4,8,8,128]{3,2,1,0:T(8,128)S(1)} %get-tuple-element.92), channel_id=1, source_target_pairs={{8,14},{72,136},{136,72},{200,202},{202,200},{138,74},{74,138},{10... | collective-permute-start | bytes 393224 | tf_op jit(solution)/shard_map/ppermute | solution.py:111
  59.5 5.8 %collective-permute-start.17 = (f32[72,8,128]{2,1,0:T(8,128)S(1)}, f32[72,8,128]{2,1,0:T(8,128)S(1)}, u32[]{:S(2)}, u32[]{:S(2)}) collective-permute-start(f32[72,8,128]{2,1,0:T(8,128)S(1)} %get-tuple-element.98), channel_id=1, source_target_pairs={{8,0},{72,64},{136,128},{200,192},{202,194},{138,130},{74,66},{10,... | collective-permute-start | bytes 884744 | tf_op jit(solution)/shard_map/ppermute | solution.py:111
  59.6 5.7 %collective-permute-start.18 = (f32[40,8,128]{2,1,0:T(8,128)S(1)}, f32[40,8,128]{2,1,0:T(8,128)S(1)}, u32[]{:S(2)}, u32[]{:S(2)}) collective-permute-start(f32[40,8,128]{2,1,0:T(8,128)S(1)} %corner_3.1.refs_4_), channel_id=1, source_target_pairs={{8,57},{72,121},{136,185},{200,249},{202,251},{138,187},{74,123},{... | collective-permute-start | bytes 491528 | tf_op jit(solution)/shard_map/ppermute | solution.py:111
  69.1 5.8 %collective-permute-start.20 = (f32[3,8,8,128]{3,2,1,0:T(8,128)S(1)}, f32[3,8,8,128]{3,2,1,0:T(8,128)S(1)}, u32[]{:S(2)}, u32[]{:S(2)}) collective-permute-start(f32[3,8,8,128]{3,2,1,0:T(8,128)S(1)} %get-tuple-element.101), channel_id=1, source_target_pairs={{8,14},{72,136},{136,72},{200,202},{202,200},{138,74},{74,138},{10... | collective-permute-start | bytes 294920 | tf_op jit(solution)/shard_map/ppermute | solution.py:111
  75.1 5.3 %collective-permute-start.22 = (f32[50,8,128]{2,1,0:T(8,128)S(1)}, f32[50,8,128]{2,1,0:T(8,128)S(1)}, u32[]{:S(2)}, u32[]{:S(2)}) collective-permute-start(f32[50,8,128]{2,1,0:T(8,128)S(1)} %get-tuple-element.106), channel_id=1, source_target_pairs={{8,0},{72,64},{136,128},{200,192},{202,194},{138,130},{74,66},{10,... | collective-permute-start | bytes 614408 | tf_op jit(solution)/shard_map/ppermute | solution.py:111
  75.2 5.2 %collective-permute-start.23 = (f32[26,8,128]{2,1,0:T(8,128)S(1)}, f32[26,8,128]{2,1,0:T(8,128)S(1)}, u32[]{:S(2)}, u32[]{:S(2)}) collective-permute-start(f32[26,8,128]{2,1,0:T(8,128)S(1)} %corner_4.1.refs_3_), channel_id=1, source_target_pairs={{8,57},{72,121},{136,185},{200,249},{202,251},{138,187},{74,123},{... | collective-permute-start | bytes 319496 | tf_op jit(solution)/shard_map/ppermute | solution.py:111
  82.6 5.6 %collective-permute-start.24 = (f32[4,8,8,128]{3,2,1,0:T(8,128)S(1)}, f32[4,8,8,128]{3,2,1,0:T(8,128)S(1)}, u32[]{:S(2)}, u32[]{:S(2)}) collective-permute-start(f32[4,8,8,128]{3,2,1,0:T(8,128)S(1)} %get-tuple-element.109), channel_id=1, source_target_pairs={{8,72},{72,8},{136,200},{200,136},{202,138},{138,202},{74,10},{10,... | collective-permute-start | bytes 393224 | tf_op jit(solution)/shard_map/ppermute | solution.py:111
  83.0 6.6 %collective-permute-start.25 = (f32[4,8,8,128]{3,2,1,0:T(8,128)S(1)}, f32[4,8,8,128]{3,2,1,0:T(8,128)S(1)}, u32[]{:S(2)}, u32[]{:S(2)}) collective-permute-start(f32[4,8,8,128]{3,2,1,0:T(8,128)S(1)} %get-tuple-element.110), channel_id=1, source_target_pairs={{8,14},{72,136},{136,72},{200,202},{202,200},{138,74},{74,138},{10... | collective-permute-start | bytes 393224 | tf_op jit(solution)/shard_map/ppermute | solution.py:111
  84.7 4.9 %collective-permute-start.26 = (f32[32,8,128]{2,1,0:T(8,128)S(1)}, f32[32,8,128]{2,1,0:T(8,128)S(1)}, u32[]{:S(2)}, u32[]{:S(2)}) collective-permute-start(f32[32,8,128]{2,1,0:T(8,128)S(1)} %get-tuple-element.114), channel_id=1, source_target_pairs={{8,57},{72,121},{136,185},{200,249},{202,251},{138,187},{74,123},{... | collective-permute-start | bytes 393224 | tf_op jit(solution)/shard_map/ppermute | solution.py:111
  89.7 5.4 %collective-permute-start.27 = (f32[64,8,128]{2,1,0:T(8,128)S(1)}, f32[64,8,128]{2,1,0:T(8,128)S(1)}, u32[]{:S(2)}, u32[]{:S(2)}) collective-permute-start(f32[64,8,128]{2,1,0:T(8,128)S(1)} %get-tuple-element.116), channel_id=1, source_target_pairs={{8,0},{72,64},{136,128},{200,192},{202,194},{138,130},{74,66},{10,... | collective-permute-start | bytes 786440 | tf_op jit(solution)/shard_map/ppermute | solution.py:111
  89.8 5.3 %collective-permute-start.28 = (f32[32,8,128]{2,1,0:T(8,128)S(1)}, f32[32,8,128]{2,1,0:T(8,128)S(1)}, u32[]{:S(2)}, u32[]{:S(2)}) collective-permute-start(f32[32,8,128]{2,1,0:T(8,128)S(1)} %corner_5.1.refs_4_), channel_id=1, source_target_pairs={{8,57},{72,121},{136,185},{200,249},{202,251},{138,187},{74,123},{... | collective-permute-start | bytes 393224 | tf_op jit(solution)/shard_map/ppermute | solution.py:111
  97.3 5.1 %collective-permute-start.30 = (f32[1,8,8,128]{3,2,1,0:T(8,128)S(1)}, f32[1,8,8,128]{3,2,1,0:T(8,128)S(1)}, u32[]{:S(2)}, u32[]{:S(2)}) collective-permute-start(f32[1,8,8,128]{3,2,1,0:T(8,128)S(1)} %get-tuple-element.120), channel_id=1, source_target_pairs={{8,14},{72,136},{136,72},{200,202},{202,200},{138,74},{74,138},{10... | collective-permute-start | bytes 98312 | tf_op jit(solution)/shard_map/ppermute | solution.py:111
  108.9 10.0 %collective-permute-start.35 = (f32[2,16,8,128]{3,2,1,0:T(8,128)S(1)}, f32[2,16,8,128]{3,2,1,0:T(8,128)S(1)}, u32[]{:S(2)}, u32[]{:S(2)}) collective-permute-start(f32[2,16,8,128]{3,2,1,0:T(8,128)S(1)} %get-tuple-element.129), channel_id=1, source_target_pairs={{8,0},{72,64},{136,1},{200,65},{202,2},{138,66},{74,3},{10,67},{12... | collective-permute-start | bytes 393224 | tf_op jit(solution)/shard_map/ppermute | solution.py:587
  115.0 8.4 %collective-permute-start.36 = (f32[2,16,8,128]{3,2,1,0:T(8,128)S(1)}, f32[2,16,8,128]{3,2,1,0:T(8,128)S(1)}, u32[]{:S(2)}, u32[]{:S(2)}) collective-permute-start(f32[2,16,8,128]{3,2,1,0:T(8,128)S(1)} %get-tuple-element.130), channel_id=1, source_target_pairs={{8,64},{72,0},{136,65},{200,1},{202,66},{138,2},{74,67},{10,3},{12... | collective-permute-start | bytes 393224 | tf_op jit(solution)/shard_map/ppermute | solution.py:587
  (13 other events, 52.0 us)

commit v4 on v3

--- a/solution.py
+++ b/solution.py
@@ -146,7 +146,10 @@
 
 
 def slim(ref, s, x):
-    cells = ref[s, x]
+    return slimmed(ref[s, x])
+
+
+def slimmed(cells):
     halo = jnp.where(row_index() < 4, cells[2 * BRICK :], cells[:BRICK])
     return jnp.concatenate([cells[OWN], halo], axis=0)
 
@@ -192,8 +195,17 @@
             at = part(x, halo - k)
             for s in range(2):
                 nxt = get(s, x + 1)
-                new = right[s, x, at] + MIX[s] * around(prev[s], cur[s], nxt, at)
-                dst[s, x, OWN if k == halo else at] = new
+                if halo - k == 4 and at == full:
+                    second = pltpu.roll(cur[s], 1, 0) + pltpu.roll(cur[s], EXT - 1, 0)
+                    mid = slimmed(cur[s])
+                    third = pltpu.roll(mid, 1, 1) + pltpu.roll(mid, LANES - 1, 1)
+                    new = MIX[s] * (slimmed((prev[s] + nxt) + second) + third)
+                    new = slimmed(right[s, x]) + new
+                    dst[s, x, OWN] = new[FIRST]
+                    dst[s, x, :BRICK] = dst[s, x, 2 * BRICK :] = new[BRICK:]
+                else:
+                    new = right[s, x, at] + MIX[s] * around(prev[s], cur[s], nxt, at)
+                    dst[s, x, OWN if k == halo else at] = new
                 prev[s], cur[s] = cur[s], nxt
 
 

time: 124 us -> 124 us (level)
  no operation moved by 1% of the time
where the time goes in v4:
time: 124 us
  starting transfers between devices  57.5 us (46%)
  waiting for transfers between devices  49.9 us (40%)
  Pallas kernels  16.1 us (13%)
    ppermute x33, starting transfers between devices, sent(): return lax.ppermute(array, AXES, pairs_along(dim, odd))  43.5 us
    ppermute x33, waiting for transfers between devices, sent(): return lax.ppermute(array, AXES, pairs_along(dim, odd))  36.9 us
    pallas_call x23, Pallas kernels, call(): pl.pallas_call(kernel, name=name, out_shape=[jax.ShapeDtypeStruct(s, jnp....  16.1 us
    ppermute x2, starting transfers between devices, per_device(): lax.ppermute(o, AXES, gather_pairs(turn))  7.99 us
    ppermute x1, waiting for transfers between devices, per_device(): one = lax.ppermute(one, AXES, spread_pairs(True))  6.5 us
    ppermute x2, waiting for transfers between devices, per_device(): lax.ppermute(o, AXES, gather_pairs(turn))  6.47 us
    ppermute x1, starting transfers between devices, per_device(): pair = lax.ppermute(pair, AXES, spread_pairs(False))  3.91 us
  transfers between devices with their start and end apart: 37, of which 23 were waited for; matrix products, arithmetic and copies ran while one was open for 0% of the time, Pallas kernels for 0%

profile of v4, /device:TPU:32, one launch (start us, length us, event | category | flops | bytes accessed | tf_op | source)
XLA Modules:
  0.0 124.0 jit_solution(11990024590143531946)
XLA Ops:
  1.8 3.9 %collective-permute-start = (f32[4,8,16,128]{3,2,1,0:T(8,128)}, f32[4,8,16,128]{3,2,1,0:T(8,128)S(1)}, u32[]{:S(2)}, u32[]{:S(2)}) collective-permute-start(f32[4,8,16,128]{3,2,1,0:T(8,128)} %get-tuple-element.68), channel_id=1, source_target_pairs={{0,8},{1,200},{2,202},{3,10},{4,12},{5,204},{6,206},{7,14},{8,9},{... | collective-permute-start | bytes 786440 | tf_op jit(solution)/shard_map/ppermute | solution.py:563
  5.8 2.1 %collective-permute-start.1 = (f32[4,8,8,128]{3,2,1,0:T(8,128)}, f32[4,8,8,128]{3,2,1,0:T(8,128)S(1)}, u32[]{:S(2)}, u32[]{:S(2)}) collective-permute-start(f32[4,8,8,128]{3,2,1,0:T(8,128)} %get-tuple-element.69), channel_id=1, source_target_pairs={{0,14},{1,72},{2,74},{3,12},{4,10},{5,76},{6,78},{7,8},{8,15},{9,7... | collective-permute-start | bytes 393224 | tf_op jit(solution)/shard_map/ppermute | solution.py:564
  7.9 6.5 %collective-permute-done.1.far = f32[4,8,8,128]{3,2,1,0:T(8,128)S(1)} collective-permute-done((f32[4,8,8,128]{3,2,1,0:T(8,128)}, f32[4,8,8,128]{3,2,1,0:T(8,128)S(1)}, u32[]{:S(2)}, u32[]{:S(2)}) %collective-permute-start.1) | collective-permute-done | bytes 131104 | tf_op jit(solution)/shard_map/ppermute | solution.py:564
  14.5 3.0 %collective-permute-start.3 = (f32[60,8,128]{2,1,0:T(8,128)S(1)}, f32[60,8,128]{2,1,0:T(8,128)S(1)}, u32[]{:S(2)}, u32[]{:S(2)}) collective-permute-start(f32[60,8,128]{2,1,0:T(8,128)S(1)} %get-tuple-element.72), channel_id=1, source_target_pairs={{8,57},{72,121},{136,185},{200,249},{202,251},{138,187},{74,123},{... | collective-permute-start | bytes 737288 | tf_op jit(solution)/shard_map/ppermute | solution.py:111
  17.5 3.9 %collective-permute-done.3.far = f32[60,8,128]{2,1,0:T(8,128)S(1)} collective-permute-done((f32[60,8,128]{2,1,0:T(8,128)S(1)}, f32[60,8,128]{2,1,0:T(8,128)S(1)}, u32[]{:S(2)}, u32[]{:S(2)}) %collective-permute-start.3) | collective-permute-done | bytes 245792 | tf_op jit(solution)/shard_map/ppermute | solution.py:111
  22.7 3.1 %collective-permute-start.5 = (f32[2,8,8,128]{3,2,1,0:T(8,128)S(1)}, f32[2,8,8,128]{3,2,1,0:T(8,128)S(1)}, u32[]{:S(2)}, u32[]{:S(2)}) collective-permute-start(f32[2,8,8,128]{3,2,1,0:T(8,128)S(1)} %get-tuple-element.73), channel_id=1, source_target_pairs={{8,14},{72,136},{136,72},{200,202},{202,200},{138,74},{74,138},{10... | collective-permute-start | bytes 196616 | tf_op jit(solution)/shard_map/ppermute | solution.py:111
  30.2 2.7 %collective-permute-start.8 = (f32[14,8,128]{2,1,0:T(8,128)S(1)}, f32[14,8,128]{2,1,0:T(8,128)S(1)}, u32[]{:S(2)}, u32[]{:S(2)}) collective-permute-start(f32[14,8,128]{2,1,0:T(8,128)S(1)} %corner_1.1.refs_2_), channel_id=1, source_target_pairs={{8,57},{72,121},{136,185},{200,249},{202,251},{138,187},{74,123},{... | collective-permute-start | bytes 172040 | tf_op jit(solution)/shard_map/ppermute | solution.py:111
  34.8 2.2 %round_1.1 = (f32[4,8,8,128]{3,2,1,0:T(8,128)S(1)}, f32[4,8,8,128]{3,2,1,0:T(8,128)S(1)}, f32[32,8,128]{2,1,0:T(8,128)S(1)}, f32[2,24,24,128]{3,2,1,0:T(8,128)S(...) custom-call(f32[2,8,24,128]{3,2,1,0:T(8,128)S(1)} %get-tuple-element, ...), custom_call_target="tpu_custom_call" | custom-call | tf_op jit(solution)/shard_map/round_1/pallas_call | solution.py:115
  36.9 2.1 %collective-permute-start.9 = (f32[4,8,8,128]{3,2,1,0:T(8,128)S(1)}, f32[4,8,8,128]{3,2,1,0:T(8,128)S(1)}, u32[]{:S(2)}, u32[]{:S(2)}) collective-permute-start(f32[4,8,8,128]{3,2,1,0:T(8,128)S(1)} %get-tuple-element.81), channel_id=1, source_target_pairs={{8,72},{72,8},{136,200},{200,136},{202,138},{138,202},{74,10},{10,... | collective-permute-start | bytes 393224 | tf_op jit(solution)/shard_map/ppermute | solution.py:111
  42.2 2.9 %collective-permute-done.10.far = f32[4,8,8,128]{3,2,1,0:T(8,128)S(1)} collective-permute-done((f32[4,8,8,128]{3,2,1,0:T(8,128)S(1)}, f32[4,8,8,128]{3,2,1,0:T(8,128)S(1)}, u32[]{:S(2)}, u32[]{:S(2)}) %collective-permute-start.10) | collective-permute-done | bytes 131104 | tf_op jit(solution)/shard_map/ppermute | solution.py:111
  45.4 2.7 %collective-permute-start.13 = (f32[32,8,128]{2,1,0:T(8,128)S(1)}, f32[32,8,128]{2,1,0:T(8,128)S(1)}, u32[]{:S(2)}, u32[]{:S(2)}) collective-permute-start(f32[32,8,128]{2,1,0:T(8,128)S(1)} %corner_2.1.refs_4_), channel_id=1, source_target_pairs={{8,57},{72,121},{136,185},{200,249},{202,251},{138,187},{74,123},{... | collective-permute-start | bytes 393224 | tf_op jit(solution)/shard_map/ppermute | solution.py:111
  48.1 2.6 %collective-permute-done.13.far = f32[32,8,128]{2,1,0:T(8,128)S(1)} collective-permute-done((f32[32,8,128]{2,1,0:T(8,128)S(1)}, f32[32,8,128]{2,1,0:T(8,128)S(1)}, u32[]{:S(2)}, u32[]{:S(2)}) %collective-permute-start.13) | collective-permute-done | bytes 131104 | tf_op jit(solution)/shard_map/ppermute | solution.py:111
  59.4 2.7 %collective-permute-start.18 = (f32[40,8,128]{2,1,0:T(8,128)S(1)}, f32[40,8,128]{2,1,0:T(8,128)S(1)}, u32[]{:S(2)}, u32[]{:S(2)}) collective-permute-start(f32[40,8,128]{2,1,0:T(8,128)S(1)} %corner_3.1.refs_4_), channel_id=1, source_target_pairs={{8,57},{72,121},{136,185},{200,249},{202,251},{138,187},{74,123},{... | collective-permute-start | bytes 491528 | tf_op jit(solution)/shard_map/ppermute | solution.py:111
  62.2 3.0 %collective-permute-done.18.far = f32[40,8,128]{2,1,0:T(8,128)S(1)} collective-permute-done((f32[40,8,128]{2,1,0:T(8,128)S(1)}, f32[40,8,128]{2,1,0:T(8,128)S(1)}, u32[]{:S(2)}, u32[]{:S(2)}) %collective-permute-start.18) | collective-permute-done | bytes 163872 | tf_op jit(solution)/shard_map/ppermute | solution.py:111
  65.2 3.3 %round_3.1 = (f32[3,8,8,128]{3,2,1,0:T(8,128)S(1)}, f32[3,8,8,128]{3,2,1,0:T(8,128)S(1)}, f32[24,8,128]{2,1,0:T(8,128)S(1)}, f32[2,24,24,128]{3,2,1,0:T(8,128)S(...) custom-call(f32[6,8,24,128]{3,2,1,0:T(8,128)S(1)} %get-tuple-element, ...), custom_call_target="tpu_custom_call" | custom-call | tf_op jit(solution)/shard_map/round_3/pallas_call | solution.py:115
  75.0 2.8 %collective-permute-start.23 = (f32[26,8,128]{2,1,0:T(8,128)S(1)}, f32[26,8,128]{2,1,0:T(8,128)S(1)}, u32[]{:S(2)}, u32[]{:S(2)}) collective-permute-start(f32[26,8,128]{2,1,0:T(8,128)S(1)} %corner_4.1.refs_3_), channel_id=1, source_target_pairs={{8,57},{72,121},{136,185},{200,249},{202,251},{138,187},{74,123},{... | collective-permute-start | bytes 319496 | tf_op jit(solution)/shard_map/ppermute | solution.py:111
  77.8 2.4 %collective-permute-done.23.far = f32[26,8,128]{2,1,0:T(8,128)S(1)} collective-permute-done((f32[26,8,128]{2,1,0:T(8,128)S(1)}, f32[26,8,128]{2,1,0:T(8,128)S(1)}, u32[]{:S(2)}, u32[]{:S(2)}) %collective-permute-start.23) | collective-permute-done | bytes 106528 | tf_op jit(solution)/shard_map/ppermute | solution.py:111
  80.2 2.2 %round_4.1 = (f32[4,8,8,128]{3,2,1,0:T(8,128)S(1)}, f32[4,8,8,128]{3,2,1,0:T(8,128)S(1)}, f32[32,8,128]{2,1,0:T(8,128)S(1)}, f32[2,24,24,128]{3,2,1,0:T(8,128)S(...) custom-call(f32[4,8,24,128]{3,2,1,0:T(8,128)S(1)} %get-tuple-element, ...), custom_call_target="tpu_custom_call" | custom-call | tf_op jit(solution)/shard_map/round_4/pallas_call | solution.py:115
  85.9 2.1 %collective-permute-done.24.near = f32[4,8,8,128]{3,2,1,0:T(8,128)S(1)} collective-permute-done((f32[4,8,8,128]{3,2,1,0:T(8,128)S(1)}, f32[4,8,8,128]{3,2,1,0:T(8,128)S(1)}, u32[]{:S(2)}, u32[]{:S(2)}) %collective-permute-start.24) | collective-permute-done | bytes 131104 | tf_op jit(solution)/shard_map/ppermute | solution.py:111
  89.5 2.7 %collective-permute-start.28 = (f32[32,8,128]{2,1,0:T(8,128)S(1)}, f32[32,8,128]{2,1,0:T(8,128)S(1)}, u32[]{:S(2)}, u32[]{:S(2)}) collective-permute-start(f32[32,8,128]{2,1,0:T(8,128)S(1)} %corner_5.1.refs_4_), channel_id=1, source_target_pairs={{8,57},{72,121},{136,185},{200,249},{202,251},{138,187},{74,123},{... | collective-permute-start | bytes 393224 | tf_op jit(solution)/shard_map/ppermute | solution.py:111
  92.2 2.6 %collective-permute-done.28.far = f32[32,8,128]{2,1,0:T(8,128)S(1)} collective-permute-done((f32[32,8,128]{2,1,0:T(8,128)S(1)}, f32[32,8,128]{2,1,0:T(8,128)S(1)}, u32[]{:S(2)}, u32[]{:S(2)}) %collective-permute-start.28) | collective-permute-done | bytes 131104 | tf_op jit(solution)/shard_map/ppermute | solution.py:111
  102.7 2.5 %collective-permute-start.33 = (f32[6,8,128]{2,1,0:T(8,128)S(1)}, f32[6,8,128]{2,1,0:T(8,128)S(1)}, u32[]{:S(2)}, u32[]{:S(2)}) collective-permute-start(f32[6,8,128]{2,1,0:T(8,128)S(1)} %corner_6.1.refs_2_), channel_id=1, source_target_pairs={{8,57},{72,121},{136,185},{200,249},{202,251},{138,187},{74,123},{... | collective-permute-start | bytes 73736 | tf_op jit(solution)/shard_map/ppermute | solution.py:111
  108.6 6.1 %collective-permute-start.35 = (f32[2,16,8,128]{3,2,1,0:T(8,128)S(1)}, f32[2,16,8,128]{3,2,1,0:T(8,128)S(1)}, u32[]{:S(2)}, u32[]{:S(2)}) collective-permute-start(f32[2,16,8,128]{3,2,1,0:T(8,128)S(1)} %get-tuple-element.129), channel_id=1, source_target_pairs={{8,0},{72,64},{136,1},{200,65},{202,2},{138,66},{74,3},{10,67},{12... | collective-permute-start | bytes 393224 | tf_op jit(solution)/shard_map/ppermute | solution.py:599
  118.6 4.5 %collective-permute-done.36.in_1 = f32[2,16,8,128]{3,2,1,0:T(8,128)S(1)} collective-permute-done((f32[2,16,8,128]{3,2,1,0:T(8,128)S(1)}, f32[2,16,8,128]{3,2,1,0:T(8,128)S(1)}, u32[]{:S(2)}, u32[]{:S(2)}) %collective-permute-start.36) | collective-permute-done | bytes 131104 | tf_op jit(solution)/shard_map/ppermute | solution.py:599
  (73 shorter events, 49.1 us)
Async XLA Ops:
  1.8 12.5 %collective-permute-start = (f32[4,8,16,128]{3,2,1,0:T(8,128)}, f32[4,8,16,128]{3,2,1,0:T(8,128)S(1)}, u32[]{:S(2)}, u32[]{:S(2)}) collective-permute-start(f32[4,8,16,128]{3,2,1,0:T(8,128)} %get-tuple-element.68), channel_id=1, source_target_pairs={{0,8},{1,200},{2,202},{3,10},{4,12},{5,204},{6,206},{7,14},{8,9},{... | collective-permute-start | bytes 786440 | tf_op jit(solution)/shard_map/ppermute | solution.py:563
  5.8 8.6 %collective-permute-start.1 = (f32[4,8,8,128]{3,2,1,0:T(8,128)}, f32[4,8,8,128]{3,2,1,0:T(8,128)S(1)}, u32[]{:S(2)}, u32[]{:S(2)}) collective-permute-start(f32[4,8,8,128]{3,2,1,0:T(8,128)} %get-tuple-element.69), channel_id=1, source_target_pairs={{0,14},{1,72},{2,74},{3,12},{4,10},{5,76},{6,78},{7,8},{8,15},{9,7... | collective-permute-start | bytes 393224 | tf_op jit(solution)/shard_map/ppermute | solution.py:564
  14.5 6.9 %collective-permute-start.3 = (f32[60,8,128]{2,1,0:T(8,128)S(1)}, f32[60,8,128]{2,1,0:T(8,128)S(1)}, u32[]{:S(2)}, u32[]{:S(2)}) collective-permute-start(f32[60,8,128]{2,1,0:T(8,128)S(1)} %get-tuple-element.72), channel_id=1, source_target_pairs={{8,57},{72,121},{136,185},{200,249},{202,251},{138,187},{74,123},{... | collective-permute-start | bytes 737288 | tf_op jit(solution)/shard_map/ppermute | solution.py:111
  22.7 5.6 %collective-permute-start.5 = (f32[2,8,8,128]{3,2,1,0:T(8,128)S(1)}, f32[2,8,8,128]{3,2,1,0:T(8,128)S(1)}, u32[]{:S(2)}, u32[]{:S(2)}) collective-permute-start(f32[2,8,8,128]{3,2,1,0:T(8,128)S(1)} %get-tuple-element.73), channel_id=1, source_target_pairs={{8,14},{72,136},{136,72},{200,202},{202,200},{138,74},{74,138},{10... | collective-permute-start | bytes 196616 | tf_op jit(solution)/shard_map/ppermute | solution.py:111
  36.9 5.3 %collective-permute-start.9 = (f32[4,8,8,128]{3,2,1,0:T(8,128)S(1)}, f32[4,8,8,128]{3,2,1,0:T(8,128)S(1)}, u32[]{:S(2)}, u32[]{:S(2)}) collective-permute-start(f32[4,8,8,128]{3,2,1,0:T(8,128)S(1)} %get-tuple-element.81), channel_id=1, source_target_pairs={{8,72},{72,8},{136,200},{200,136},{202,138},{138,202},{74,10},{10,... | collective-permute-start | bytes 393224 | tf_op jit(solution)/shard_map/ppermute | solution.py:111
  39.0 6.2 %collective-permute-start.10 = (f32[4,8,8,128]{3,2,1,0:T(8,128)S(1)}, f32[4,8,8,128]{3,2,1,0:T(8,128)S(1)}, u32[]{:S(2)}, u32[]{:S(2)}) collective-permute-start(f32[4,8,8,128]{3,2,1,0:T(8,128)S(1)} %get-tuple-element.82), channel_id=1, source_target_pairs={{8,14},{72,136},{136,72},{200,202},{202,200},{138,74},{74,138},{10... | collective-permute-start | bytes 393224 | tf_op jit(solution)/shard_map/ppermute | solution.py:111
  39.1 6.1 %collective-permute-start.11 = (f32[32,8,128]{2,1,0:T(8,128)S(1)}, f32[32,8,128]{2,1,0:T(8,128)S(1)}, u32[]{:S(2)}, u32[]{:S(2)}) collective-permute-start(f32[32,8,128]{2,1,0:T(8,128)S(1)} %get-tuple-element.86), channel_id=1, source_target_pairs={{8,57},{72,121},{136,185},{200,249},{202,251},{138,187},{74,123},{... | collective-permute-start | bytes 393224 | tf_op jit(solution)/shard_map/ppermute | solution.py:111
  45.3 5.4 %collective-permute-start.12 = (f32[64,8,128]{2,1,0:T(8,128)S(1)}, f32[64,8,128]{2,1,0:T(8,128)S(1)}, u32[]{:S(2)}, u32[]{:S(2)}) collective-permute-start(f32[64,8,128]{2,1,0:T(8,128)S(1)} %get-tuple-element.88), channel_id=1, source_target_pairs={{8,0},{72,64},{136,128},{200,192},{202,194},{138,130},{74,66},{10,... | collective-permute-start | bytes 786440 | tf_op jit(solution)/shard_map/ppermute | solution.py:111
  45.4 5.3 %collective-permute-start.13 = (f32[32,8,128]{2,1,0:T(8,128)S(1)}, f32[32,8,128]{2,1,0:T(8,128)S(1)}, u32[]{:S(2)}, u32[]{:S(2)}) collective-permute-start(f32[32,8,128]{2,1,0:T(8,128)S(1)} %corner_2.1.refs_4_), channel_id=1, source_target_pairs={{8,57},{72,121},{136,185},{200,249},{202,251},{138,187},{74,123},{... | collective-permute-start | bytes 393224 | tf_op jit(solution)/shard_map/ppermute | solution.py:111
  52.5 5.3 %collective-permute-start.14 = (f32[4,8,8,128]{3,2,1,0:T(8,128)S(1)}, f32[4,8,8,128]{3,2,1,0:T(8,128)S(1)}, u32[]{:S(2)}, u32[]{:S(2)}) collective-permute-start(f32[4,8,8,128]{3,2,1,0:T(8,128)S(1)} %get-tuple-element.91), channel_id=1, source_target_pairs={{8,72},{72,8},{136,200},{200,136},{202,138},{138,202},{74,10},{10,... | collective-permute-start | bytes 393224 | tf_op jit(solution)/shard_map/ppermute | solution.py:111
  52.6 6.6 %collective-permute-start.15 = (f32[4,8,8,128]{3,2,1,0:T(8,128)S(1)}, f32[4,8,8,128]{3,2,1,0:T(8,128)S(1)}, u32[]{:S(2)}, u32[]{:S(2)}) collective-permute-start(f32[4,8,8,128]{3,2,1,0:T(8,128)S(1)} %get-tuple-element.92), channel_id=1, source_target_pairs={{8,14},{72,136},{136,72},{200,202},{202,200},{138,74},{74,138},{10... | collective-permute-start | bytes 393224 | tf_op jit(solution)/shard_map/ppermute | solution.py:111
  59.3 5.8 %collective-permute-start.17 = (f32[72,8,128]{2,1,0:T(8,128)S(1)}, f32[72,8,128]{2,1,0:T(8,128)S(1)}, u32[]{:S(2)}, u32[]{:S(2)}) collective-permute-start(f32[72,8,128]{2,1,0:T(8,128)S(1)} %get-tuple-element.98), channel_id=1, source_target_pairs={{8,0},{72,64},{136,128},{200,192},{202,194},{138,130},{74,66},{10,... | collective-permute-start | bytes 884744 | tf_op jit(solution)/shard_map/ppermute | solution.py:111
  59.4 5.7 %collective-permute-start.18 = (f32[40,8,128]{2,1,0:T(8,128)S(1)}, f32[40,8,128]{2,1,0:T(8,128)S(1)}, u32[]{:S(2)}, u32[]{:S(2)}) collective-permute-start(f32[40,8,128]{2,1,0:T(8,128)S(1)} %corner_3.1.refs_4_), channel_id=1, source_target_pairs={{8,57},{72,121},{136,185},{200,249},{202,251},{138,187},{74,123},{... | collective-permute-start | bytes 491528 | tf_op jit(solution)/shard_map/ppermute | solution.py:111
  68.9 5.8 %collective-permute-start.20 = (f32[3,8,8,128]{3,2,1,0:T(8,128)S(1)}, f32[3,8,8,128]{3,2,1,0:T(8,128)S(1)}, u32[]{:S(2)}, u32[]{:S(2)}) collective-permute-start(f32[3,8,8,128]{3,2,1,0:T(8,128)S(1)} %get-tuple-element.101), channel_id=1, source_target_pairs={{8,14},{72,136},{136,72},{200,202},{202,200},{138,74},{74,138},{10... | collective-permute-start | bytes 294920 | tf_op jit(solution)/shard_map/ppermute | solution.py:111
  74.9 5.3 %collective-permute-start.22 = (f32[50,8,128]{2,1,0:T(8,128)S(1)}, f32[50,8,128]{2,1,0:T(8,128)S(1)}, u32[]{:S(2)}, u32[]{:S(2)}) collective-permute-start(f32[50,8,128]{2,1,0:T(8,128)S(1)} %get-tuple-element.106), channel_id=1, source_target_pairs={{8,0},{72,64},{136,128},{200,192},{202,194},{138,130},{74,66},{10,... | collective-permute-start | bytes 614408 | tf_op jit(solution)/shard_map/ppermute | solution.py:111
  75.0 5.2 %collective-permute-start.23 = (f32[26,8,128]{2,1,0:T(8,128)S(1)}, f32[26,8,128]{2,1,0:T(8,128)S(1)}, u32[]{:S(2)}, u32[]{:S(2)}) collective-permute-start(f32[26,8,128]{2,1,0:T(8,128)S(1)} %corner_4.1.refs_3_), channel_id=1, source_target_pairs={{8,57},{72,121},{136,185},{200,249},{202,251},{138,187},{74,123},{... | collective-permute-start | bytes 319496 | tf_op jit(solution)/shard_map/ppermute | solution.py:111
  82.4 5.6 %collective-permute-start.24 = (f32[4,8,8,128]{3,2,1,0:T(8,128)S(1)}, f32[4,8,8,128]{3,2,1,0:T(8,128)S(1)}, u32[]{:S(2)}, u32[]{:S(2)}) collective-permute-start(f32[4,8,8,128]{3,2,1,0:T(8,128)S(1)} %get-tuple-element.109), channel_id=1, source_target_pairs={{8,72},{72,8},{136,200},{200,136},{202,138},{138,202},{74,10},{10,... | collective-permute-start | bytes 393224 | tf_op jit(solution)/shard_map/ppermute | solution.py:111
  82.7 6.6 %collective-permute-start.25 = (f32[4,8,8,128]{3,2,1,0:T(8,128)S(1)}, f32[4,8,8,128]{3,2,1,0:T(8,128)S(1)}, u32[]{:S(2)}, u32[]{:S(2)}) collective-permute-start(f32[4,8,8,128]{3,2,1,0:T(8,128)S(1)} %get-tuple-element.110), channel_id=1, source_target_pairs={{8,14},{72,136},{136,72},{200,202},{202,200},{138,74},{74,138},{10... | collective-permute-start | bytes 393224 | tf_op jit(solution)/shard_map/ppermute | solution.py:111
  84.4 4.9 %collective-permute-start.26 = (f32[32,8,128]{2,1,0:T(8,128)S(1)}, f32[32,8,128]{2,1,0:T(8,128)S(1)}, u32[]{:S(2)}, u32[]{:S(2)}) collective-permute-start(f32[32,8,128]{2,1,0:T(8,128)S(1)} %get-tuple-element.114), channel_id=1, source_target_pairs={{8,57},{72,121},{136,185},{200,249},{202,251},{138,187},{74,123},{... | collective-permute-start | bytes 393224 | tf_op jit(solution)/shard_map/ppermute | solution.py:111
  89.4 5.4 %collective-permute-start.27 = (f32[64,8,128]{2,1,0:T(8,128)S(1)}, f32[64,8,128]{2,1,0:T(8,128)S(1)}, u32[]{:S(2)}, u32[]{:S(2)}) collective-permute-start(f32[64,8,128]{2,1,0:T(8,128)S(1)} %get-tuple-element.116), channel_id=1, source_target_pairs={{8,0},{72,64},{136,128},{200,192},{202,194},{138,130},{74,66},{10,... | collective-permute-start | bytes 786440 | tf_op jit(solution)/shard_map/ppermute | solution.py:111
  89.5 5.3 %collective-permute-start.28 = (f32[32,8,128]{2,1,0:T(8,128)S(1)}, f32[32,8,128]{2,1,0:T(8,128)S(1)}, u32[]{:S(2)}, u32[]{:S(2)}) collective-permute-start(f32[32,8,128]{2,1,0:T(8,128)S(1)} %corner_5.1.refs_4_), channel_id=1, source_target_pairs={{8,57},{72,121},{136,185},{200,249},{202,251},{138,187},{74,123},{... | collective-permute-start | bytes 393224 | tf_op jit(solution)/shard_map/ppermute | solution.py:111
  97.0 5.1 %collective-permute-start.30 = (f32[1,8,8,128]{3,2,1,0:T(8,128)S(1)}, f32[1,8,8,128]{3,2,1,0:T(8,128)S(1)}, u32[]{:S(2)}, u32[]{:S(2)}) collective-permute-start(f32[1,8,8,128]{3,2,1,0:T(8,128)S(1)} %get-tuple-element.120), channel_id=1, source_target_pairs={{8,14},{72,136},{136,72},{200,202},{202,200},{138,74},{74,138},{10... | collective-permute-start | bytes 98312 | tf_op jit(solution)/shard_map/ppermute | solution.py:111
  108.6 10.0 %collective-permute-start.35 = (f32[2,16,8,128]{3,2,1,0:T(8,128)S(1)}, f32[2,16,8,128]{3,2,1,0:T(8,128)S(1)}, u32[]{:S(2)}, u32[]{:S(2)}) collective-permute-start(f32[2,16,8,128]{3,2,1,0:T(8,128)S(1)} %get-tuple-element.129), channel_id=1, source_target_pairs={{8,0},{72,64},{136,1},{200,65},{202,2},{138,66},{74,3},{10,67},{12... | collective-permute-start | bytes 393224 | tf_op jit(solution)/shard_map/ppermute | solution.py:599
  114.7 8.4 %collective-permute-start.36 = (f32[2,16,8,128]{3,2,1,0:T(8,128)S(1)}, f32[2,16,8,128]{3,2,1,0:T(8,128)S(1)}, u32[]{:S(2)}, u32[]{:S(2)}) collective-permute-start(f32[2,16,8,128]{3,2,1,0:T(8,128)S(1)} %get-tuple-element.130), channel_id=1, source_target_pairs={{8,64},{72,0},{136,65},{200,1},{202,66},{138,2},{74,67},{10,3},{12... | collective-permute-start | bytes 393224 | tf_op jit(solution)/shard_map/ppermute | solution.py:599
  (13 other events, 52.0 us)
